TPU v7x, 32 devices: a whole 2x2x4 slice. The times are simulated.
32 devices in a mesh: groups: 2 (over x), dp: 8 (over z, y), split: 2 (over core).
Axes of the slice: x: 2, y: 2, z: 4, core: 2. Of those that a mesh axis runs over, the one named last changes fastest.
Arguments:
- embeddings: bfloat16 [65536, 512], P(('groups', 'dp', 'split')), parts along dimension 0, may hold values from -6 to 6
- assignment: int32 [65536, 1], P(('groups', 'dp', 'split')), parts along dimension 0, may hold values from 0 to 15; in each aligned block of 2048 rows (0 to 2047, 2048 to 4095, ...) at most 192 rows name the same one
- order_key: int32 [65536], P(('groups', 'dp', 'split')), parts along dimension 0, may hold values from 0 to 32767, each once
Outputs:
- nearest: float32 [65536], P(('groups', 'dp', 'split')), parts along dimension 0
There are 2 independent parts, one for each index of `groups`. A program takes and returns all parts, laid end to end along the dimension named above; each array names one. Nothing has to cross between parts.
Inputs may be any that keep to these rules, and one draw needn't show every extreme that they name: `assignment`: in each device's 2048 rows no cluster has more than 192 rows, and some cluster has exactly 192. `order_key`: all values within a part are distinct.
All inputs are finite; a program needn't handle non-finite values.
Results may differ from a plain program's by a relative error of at most 0.0013.
Values may be sent and summed in bfloat16 or wider, within the bound.
No kernel may reach another device: no remote copies, remote signals or barrier semaphores. Data moves between devices by JAX's collectives and lax.ppermute only.
A program may use at most 64 MiB of HBM per device.

v0:
```python
import jax
import jax.numpy as jnp
from jax import lax
from jax.sharding import PartitionSpec as P

CL_OWN = 2


empty_key = 1 << 30
epsilon = 1e-06


def as_sent(value):
    return jax.tree.map(lambda a: a.astype(jnp.bfloat16) if a.dtype == jnp.float32 else a, value)


def unit_rows(embeddings):
    values = embeddings.astype(jnp.float32)
    scale = lax.rsqrt(jnp.sum(values * values, axis=1, keepdims=True) + epsilon)
    return (values * scale).astype(jnp.bfloat16)


def by_cluster(rows, keys):
    sources, count, most, width = rows.shape
    own = jnp.moveaxis(rows, 1, 0).reshape(count, sources * most, width)
    own_key = jnp.moveaxis(keys, 1, 0).reshape(count, sources * most)
    return (own, own_key)


def tile_max(best, own, own_key, cols, col_key):
    count, length, width = own.shape
    half = length // 2
    own_blocks = own.reshape(count * 2, half, width)
    key_blocks = own_key.reshape(count * 2, half)
    best_blocks = best.reshape(count * 2, half)

    def step(index):
        which = index // 2
        sims = lax.dot_general(
            own_blocks[index],
            cols[which],
            (((1,), (1,)), ((), ())),
            preferred_element_type=jnp.float32,
        )
        allowed = col_key[which][None, :] < key_blocks[index][:, None]
        return jnp.maximum(best_blocks[index], jnp.max(jnp.where(allowed, sims, -1.0), axis=1))

    return lax.map(step, jnp.arange(count * 2)).reshape(count, length)


def per_device(embeddings, assignment, order_key):
    rows_dev, width = embeddings.shape
    n_dp = lax.axis_size("dp")
    clusters = CL_OWN * n_dp
    most = 3 * rows_dev // (2 * clusters)
    cluster = assignment[:, 0]
    onehot = cluster[:, None] == jnp.arange(clusters, dtype=jnp.int32)[None, :]
    running = jnp.cumsum(onehot.astype(jnp.int32), axis=0)
    rank = jnp.sum(jnp.where(onehot, running, 0), axis=1) - 1
    slot = cluster * most + rank
    unit = unit_rows(embeddings)
    flat_rows = jnp.zeros((clusters * most, width), jnp.bfloat16).at[slot].set(unit)
    flat_keys = jnp.full((clusters * most,), empty_key, jnp.int32).at[slot].set(order_key)
    send_rows = flat_rows.reshape(n_dp, CL_OWN, most, width)
    send_keys = flat_keys.reshape(n_dp, CL_OWN, most)
    got_rows = lax.all_to_all(send_rows, "dp", split_axis=0, concat_axis=0, tiled=True)
    got_keys = lax.all_to_all(send_keys, "dp", split_axis=0, concat_axis=0, tiled=True)
    count = got_rows.shape[1]
    own, own_key = by_cluster(got_rows, got_keys)
    start_best = jnp.full(own_key.shape, -1.0, jnp.float32)
    best = tile_max(
        start_best,
        own,
        own_key,
        lax.all_gather(own, "split", axis=1, tiled=True),
        lax.all_gather(as_sent(own_key), "split", axis=1, tiled=True),
    )
    maxima = jnp.moveaxis(best.reshape(count, n_dp, most), 0, 1)
    returned = lax.all_to_all(maxima, "dp", split_axis=0, concat_axis=0, tiled=True)
    return returned.reshape(clusters * most)[slot]


def solution(mesh):
    placed = (
        P(("groups", "dp", "split"), None),
        P(("groups", "dp", "split"), None),
        P(("groups", "dp", "split")),
    )
    return jax.shard_map(
        per_device,
        mesh=mesh,
        in_specs=placed,
        out_specs=P(("groups", "dp", "split")),
        check_vma=False,
    )
```

profile of v0, /device:TPU:0, one launch (start us, length us, event | category | flops | bytes accessed | tf_op | source)
XLA Modules:
  0.0 204.6 jit_solution(2776743660190105068)
XLA Ops:
  6.5 0.7 fusion.13
  7.2 4.5 %reduce-window.6 = s32[16,16,128]{2,1,0:T(8,128)S(1)} reduce-window(s32[16,16,128]{2,1,0:T(8,128)S(1)} %fusion.13, s32[]{:T(128)} %constant.69.clone.1), window={size=1x1x128 pad=0_0x0_0x127_0}, to_apply=%region_0.0 | reduce-window | flops 4161536 | bytes 262148 | tf_op jit(solution)/shard_map/reduce-window
  12.5 0.8 fusion.12
  13.3 0.7 compare_select_fusion
  14.0 2.1 %fusion.5 = f32[2048]{0:T(1024)S(1)} fusion(bf16[2048,512]{1,0:T(8,128)(2,1)} %param.5), kind=kLoop, calls=%fused_computation.14 | loop fusion | flops 3143680 | bytes 2105344 | tf_op jit(solution)/shard_map/reduce_sum | solution.py:19
  16.1 11.8 %scatter_custom_fusion.1 = bf16[3072,512]{1,0:T(8,128)(2,1)S(1)} fusion(s32[2048]{0:T(1024)S(1)} %bitcast.51, bf16[2048,512]{1,0:T(8,128)(2,1)} %param.5, f32[2048]{0:T(1024)S(1)} %add_rsqrt_fusion, bf16[]{:T(256)} %constant.71.clone.1), kind=kCustom, calls=%fused_computation.16 | custom fusion | flops 3145728 | bytes 5251074 | tf_op jit(solution)/shard_map/scatter | solution.py:62
  27.9 77.8 %all_to_all.15 = bf16[8,2,192,512]{3,2,1,0:T(8,128)(2,1)S(1)} all-to-all(bf16[8,2,192,512]{3,2,1,0:T(8,128)(2,1)S(1)} %bitcast.45), channel_id=1, replica_groups=mesh['groups'=2,'dp'=8,'split'=2] {'dp'}, dimensions={0} | all-to-all | bytes 6291456 | tf_op jit(solution)/shard_map/all_to_all | solution.py:66
  105.7 2.0 copy.7
  107.7 8.2 %scatter_custom_fusion = s32[3072]{0:T(1024)S(1)} fusion(s32[2048]{0:T(1024)S(1)} %bitcast.52, s32[2048]{0:T(1024)} %param.7, s32[]{:T(128)} %constant.76.clone.1), kind=kCustom, calls=%fused_computation.30 | custom fusion | bytes 12800 | tf_op jit(solution)/shard_map/scatter | solution.py:63
  115.9 0.7 reshape.60
  116.6 3.6 %all-to-all-start = ((s32[8,2,192]{2,1,0:T(2,128)}), s32[8,2,192]{2,1,0:T(2,128)S(1)}, u32[]{:S(2)}, u32[]{:S(2)}) async-start(s32[8,2,192]{2,1,0:T(2,128)} %reshape.60), calls=%async_computation | async-start | bytes 32768 | tf_op jit(solution)/shard_map/all_to_all | solution.py:67
  120.2 6.6 %all-to-all-done = s32[8,2,192]{2,1,0:T(2,128)S(1)} async-done(((s32[8,2,192]{2,1,0:T(2,128)}), s32[8,2,192]{2,1,0:T(2,128)S(1)}, u32[]{:S(2)}, u32[]{:S(2)}) %all-to-all-start) | async-done | bytes 12320 | tf_op jit(solution)/shard_map/all_to_all | solution.py:67
  126.9 1.8 all_gather.6
  128.8 37.9 %while.12 = (s32[]{:T(128)}, f32[4,768]{1,0:T(4,128)S(1)}, s32[4]{0:T(128)S(1)}, s32[2,3072]{1,0:T(2,128)S(1)}, s32[4,768]{1,0:T(4,128)S(1)}, /*index=5*/bf16[4,...) while((s32[]{:T(128)}, f32[4,768]{1,0:T(4,128)S(1)}, ...), condition=%wide.region_8.9_spmd, body=%wide.region_6.8_spmd.sunk | while | flops 2422996992 | bytes 4000102 | solution.py:48
  128.8 0.6 dynamic_slice.50
  133.3 4.9 %select_reduce_fusion.2 = f32[768]{0:T(1024)S(1)} fusion(s32[3072]{0:T(1024)S(1)} %bitcast.47, s32[768]{0:T(1024)S(1)} %dynamic-slice_reduce_fusion.2, bf16[2,3072,512]{2,1,0:T(8,128)(2,1)} %get-tuple-element.183, s32[]{:T(128)S(6)} %select_n.52, bf16[4,768,512]{2,1,0:T(8,128)(2,1)} %get-tuple-element.182, s32[]{:T(128)S(6)} %select_n.53), kind=kOutput, calls=%fused_computation.3.clone.1 | convolution fusion | flops 2422996224 | bytes 3950600 | tf_op jit(solution)/shard_map/while/body/eval_jaxpr/dot_general | solution.py:39
  138.2 0.6 dynamic_slice.50
  142.7 4.9 %select_reduce_fusion.2 = f32[768]{0:T(1024)S(1)} fusion(s32[3072]{0:T(1024)S(1)} %bitcast.47, s32[768]{0:T(1024)S(1)} %dynamic-slice_reduce_fusion.2, bf16[2,3072,512]{2,1,0:T(8,128)(2,1)} %get-tuple-element.183, s32[]{:T(128)S(6)} %select_n.52, bf16[4,768,512]{2,1,0:T(8,128)(2,1)} %get-tuple-element.182, s32[]{:T(128)S(6)} %select_n.53), kind=kOutput, calls=%fused_computation.3.clone.1 | convolution fusion | flops 2422996224 | bytes 3950600 | tf_op jit(solution)/shard_map/while/body/eval_jaxpr/dot_general | solution.py:39
  152.2 4.9 %select_reduce_fusion.2 = f32[768]{0:T(1024)S(1)} fusion(s32[3072]{0:T(1024)S(1)} %bitcast.47, s32[768]{0:T(1024)S(1)} %dynamic-slice_reduce_fusion.2, bf16[2,3072,512]{2,1,0:T(8,128)(2,1)} %get-tuple-element.183, s32[]{:T(128)S(6)} %select_n.52, bf16[4,768,512]{2,1,0:T(8,128)(2,1)} %get-tuple-element.182, s32[]{:T(128)S(6)} %select_n.53), kind=kOutput, calls=%fused_computation.3.clone.1 | convolution fusion | flops 2422996224 | bytes 3950600 | tf_op jit(solution)/shard_map/while/body/eval_jaxpr/dot_general | solution.py:39
  157.2 0.6 dynamic_slice.50
  161.6 4.9 %select_reduce_fusion.2 = f32[768]{0:T(1024)S(1)} fusion(s32[3072]{0:T(1024)S(1)} %bitcast.47, s32[768]{0:T(1024)S(1)} %dynamic-slice_reduce_fusion.2, bf16[2,3072,512]{2,1,0:T(8,128)(2,1)} %get-tuple-element.183, s32[]{:T(128)S(6)} %select_n.52, bf16[4,768,512]{2,1,0:T(8,128)(2,1)} %get-tuple-element.182, s32[]{:T(128)S(6)} %select_n.53), kind=kOutput, calls=%fused_computation.3.clone.1 | convolution fusion | flops 2422996224 | bytes 3950600 | tf_op jit(solution)/shard_map/while/body/eval_jaxpr/dot_general | solution.py:39
  167.3 3.3 %all-to-all-start.2 = ((f32[8,2,192]{2,1,0:T(2,128)}), f32[8,2,192]{2,1,0:T(2,128)S(1)}, u32[]{:S(2)}, u32[]{:S(2)}) async-start(f32[8,2,192]{2,1,0:T(2,128)} %bitcast.32), calls=%async_computation.2 | async-start | bytes 32768 | tf_op jit(solution)/shard_map/all_to_all | solution.py:79
  170.7 6.5 %all-to-all-done.2 = f32[8,2,192]{2,1,0:T(2,128)S(1)} async-done(((f32[8,2,192]{2,1,0:T(2,128)}), f32[8,2,192]{2,1,0:T(2,128)S(1)}, u32[]{:S(2)}, u32[]{:S(2)}) %all-to-all-start.2) | async-done | bytes 12320 | tf_op jit(solution)/shard_map/all_to_all | solution.py:79
  177.3 20.5 %gather_fusion = f32[2048]{0:T(1024)} fusion(f32[3072]{0:T(1024)S(1)} %reshape.64, s32[2048]{0:T(1024)S(1)} %broadcast_clamp_fusion), kind=kCustom, calls=%fused_computation | custom fusion | bytes 24576 | tf_op jit(solution)/shard_map/gather | solution.py:80
  (38 shorter events, 2.7 us)
Async XLA Ops:
  6.5 122.2 %all-gather.2.cloned.1.call-start = ((), (), s32[]{:S(2)}) async-start(), calls=%async_computation.3 | async-start | bytes 9437184 | tf_op jit(solution)/shard_map/all_gather | solution.py:75
  116.6 10.2 %all-to-all-start = ((s32[8,2,192]{2,1,0:T(2,128)}), s32[8,2,192]{2,1,0:T(2,128)S(1)}, u32[]{:S(2)}, u32[]{:S(2)}) async-start(s32[8,2,192]{2,1,0:T(2,128)} %reshape.60), calls=%async_computation | async-start | bytes 32768 | tf_op jit(solution)/shard_map/all_to_all | solution.py:67
  167.3 9.9 %all-to-all-start.2 = ((f32[8,2,192]{2,1,0:T(2,128)}), f32[8,2,192]{2,1,0:T(2,128)S(1)}, u32[]{:S(2)}, u32[]{:S(2)}) async-start(f32[8,2,192]{2,1,0:T(2,128)} %bitcast.32), calls=%async_computation.2 | async-start | bytes 32768 | tf_op jit(solution)/shard_map/all_to_all | solution.py:79
Sparse Core Ops, SparseCore 0:
  107.8 15.7 all-gather.1
where the time goes:
time: 205 us
  blocking collectives  79.6 us (39%)
  local copies, waits for them, and re-layouts  35.7 us (17%)
  other arithmetic  20.9 us (10%)
  matrix products  19.5 us (10%)
  loops' own time  15.3 us (7%)
  between operations  13.5 us (7%)
  waiting for transfers between devices  13.1 us (6%)
  starting transfers between devices  6.92 us (3%)
    all_to_all x1, blocking collectives, per_device(): lax.all_to_all(send_rows, 'dp', split_axis=0, concat_axis=0, tiled=True)  77.8 us
    gather x1, local copies, waits for them, and re-layouts, per_device(): return returned.reshape(clusters * most)[slot]  20.5 us
    dot_general x4, matrix products, step(): lax.dot_general(own_blocks[index], cols[which], (((1,), (1,)), ((), ())),...  19.5 us
    another operation x1, loops' own time, tile_max(): return lax.map(step, jnp.arange(count * 2)).reshape(count, length)  15.3 us
    scatter x1, other arithmetic, per_device(): jnp.zeros((clusters * most, width), jnp.bfloat16).at[slot].set(unit)  11.8 us
    scatter x1, local copies, waits for them, and re-layouts, per_device(): jnp.full((clusters * most,), empty_key, jnp.int32).at[slot].set(order_key)  8.22 us
    all_to_all x1, waiting for transfers between devices, per_device(): lax.all_to_all(send_keys, 'dp', split_axis=0, concat_axis=0, tiled=True)  6.57 us
    all_to_all x1, waiting for transfers between devices, per_device(): lax.all_to_all(maxima, 'dp', split_axis=0, concat_axis=0, tiled=True)  6.5 us
  transfers between devices with their start and end apart: 3, of which 2 were waited for; matrix products, arithmetic and copies ran while one was open for 4% of the time, Pallas kernels for 0%

commit v1 on v0

v1 whole, which is shorter than its diff:
```python
import functools

import jax
import jax.numpy as jnp
import numpy as np
from jax import lax
from jax.experimental import pallas as pl
from jax.experimental.pallas import tpu as pltpu
from jax.sharding import PartitionSpec as P

EPSILON = 1e-06
EMPTY = float(1 << 25)
CL_OWN = 2
DEVICE = ("dp", "split")
VMEM_LIMIT = 48 * 1024 * 1024


def pack_kernel(me_ref, cluster_ref, order_ref, emb_ref, rows_ref, keys_ref, pos_ref, slot_ref, limb_ref, *, clusters, most):
    step = pl.program_id(0)
    rows_dev = emb_ref.shape[0]
    pair = CL_OWN * most

    @pl.when(step == 0)
    def _():
        cluster = cluster_ref[...]
        span = 256
        upper = (
            lax.broadcasted_iota(jnp.int32, (span, span), 0) <= lax.broadcasted_iota(jnp.int32, (span, span), 1)
        ).astype(jnp.bfloat16)
        carry = jnp.zeros((clusters, 1), jnp.float32)
        ranks = []
        for part in range(rows_dev // span):
            here = cluster[:, part * span : (part + 1) * span]
            hot = here == lax.broadcasted_iota(jnp.int32, (clusters, span), 0)
            running = jnp.dot(hot.astype(jnp.bfloat16), upper, preferred_element_type=jnp.float32) + carry
            carry = running[:, span - 1 :]
            ranks.append(jnp.sum(jnp.where(hot, running, 0.0), axis=0, keepdims=True))
        pos = jnp.concatenate(ranks, axis=1).astype(jnp.int32) - 1
        pos_ref[...] = pos
        slot_ref[...] = (cluster ^ me_ref[0]) * most + pos
        order = order_ref[...]
        which = lax.broadcasted_iota(jnp.int32, limb_ref.shape, 0)
        limbs = jnp.where(which == 0, order & 255, jnp.where(which == 1, (order >> 8) & 255, (order >> 16) & 255))
        limbs = jnp.where(which == 3, 1, jnp.where(which < 3, limbs, 0))
        limb_ref[...] = limbs.astype(jnp.float32).astype(jnp.bfloat16)

    offset = pl.num_programs(0) - 1 - step
    slot = slot_ref[...] - offset * pair
    chosen = (lax.broadcasted_iota(jnp.int32, (pair, rows_dev), 0) == slot).astype(jnp.float32).astype(jnp.bfloat16)
    packed = jnp.dot(chosen, emb_ref[...], preferred_element_type=jnp.float32)
    scale = lax.rsqrt(jnp.sum(packed * packed, axis=1, keepdims=True) + EPSILON)
    rows_ref[0] = (packed * scale).astype(jnp.bfloat16)
    for half in range(CL_OWN):
        sums = lax.dot_general(
            limb_ref[...], chosen[half * most : (half + 1) * most], (((1,), (1,)), ((), ())), preferred_element_type=jnp.float32
        )
        keys = sums[0:1] + 256.0 * sums[1:2] + 65536.0 * sums[2:3] + EMPTY * (1.0 - sums[3:4])
        keys_ref[half] = keys


def pack(me, cluster, order, embeddings, clusters, most):
    rows_dev, width = embeddings.shape
    n_dp = clusters // CL_OWN
    whole = lambda shape: pl.BlockSpec(shape, lambda i: (0,) * len(shape))
    return pl.pallas_call(
        functools.partial(pack_kernel, clusters=clusters, most=most),
        grid=(n_dp,),
        in_specs=[
            pl.BlockSpec(memory_space=pltpu.SMEM),
            whole((1, rows_dev)),
            whole((1, rows_dev)),
            whole((rows_dev, width)),
        ],
        out_specs=[
            pl.BlockSpec((1, CL_OWN * most, width), lambda i: (n_dp - 1 - i, 0, 0)),
            pl.BlockSpec((CL_OWN, 1, most), lambda i: (n_dp - 1 - i, 0, 0)),
            whole((1, rows_dev)),
        ],
        out_shape=[
            jax.ShapeDtypeStruct((n_dp, CL_OWN * most, width), jnp.bfloat16),
            jax.ShapeDtypeStruct((clusters, 1, most), jnp.float32),
            jax.ShapeDtypeStruct((1, rows_dev), jnp.int32),
        ],
        scratch_shapes=[pltpu.VMEM((1, rows_dev), jnp.int32), pltpu.VMEM((16, rows_dev), jnp.bfloat16)],
        compiler_params=pltpu.CompilerParams(vmem_limit_bytes=VMEM_LIMIT),
        name="pack",
    )(me, cluster, order, embeddings)


def nearest_kernel(pairs_ref, keys_ref, *refs, most, tile, n_dp):
    direct, swapped = refs[:n_dp], refs[n_dp : 2 * n_dp]
    out_ref, rows, sub_keys, row_best, col_best, sem = refs[2 * n_dp :]
    total = rows.shape[0]
    tiles = total // tile
    copies = []
    for k in range(n_dp):
        copies.append(pltpu.make_async_copy(direct[k].at[pl.ds(0, most)], rows.at[pl.ds(2 * k * most, most)], sem))
        copies.append(pltpu.make_async_copy(swapped[k], rows.at[pl.ds((2 * k + 1) * most, most)], sem))
    for copy in copies:
        copy.start()
    row_best[...] = jnp.full_like(row_best, -1.0)
    col_best[...] = jnp.full_like(col_best, -1.0)
    for block in range(total // 128):
        here, lane = block * 128 // tile, block * 128 % tile
        spread = jnp.broadcast_to(keys_ref[here, :, lane : lane + 128], (128, 128))
        sub_keys[block * 128 : (block + 1) * 128] = spread.T
    for copy in copies:
        copy.wait()

    def sims(i, j):
        a = rows[pl.ds(pl.multiple_of(i * tile, tile), tile)]
        b = rows[pl.ds(pl.multiple_of(j * tile, tile), tile)]
        return lax.dot_general(a, b, (((1,), (1,)), ((), ())), preferred_element_type=jnp.float32)

    def visit(i, j, both):
        sim = sims(i, j)
        at = pl.ds(pl.multiple_of(i * tile, tile), tile)
        own = sub_keys[at]
        best = row_best[at]
        others = keys_ref[j]
        for lane in range(0, tile, 128):
            part = sim[:, lane : lane + 128]
            earlier = others[:, lane : lane + 128] < own
            best = jnp.maximum(best, jnp.where(earlier, part, -1.0))
            if both:
                later = jnp.where(earlier, -1.0, part).reshape(tile // 8, 8, 128)
                col_best[j, :, lane : lane + 128] = jnp.maximum(col_best[j, :, lane : lane + 128], jnp.max(later, axis=0))
        row_best[at] = best

    @pl.loop(0, tiles)
    def _(i):
        visit(i, i, False)

    @pl.loop(0, tiles * (tiles - 1) // 2)
    def _(p):
        visit(pairs_ref[0, p], pairs_ref[1, p], True)

    for block in range(total // 128):
        here, lane = block * 128 // tile, block * 128 % tile
        by_row = jnp.max(row_best[block * 128 : (block + 1) * 128].T, axis=0, keepdims=True)
        by_col = jnp.max(col_best[here, :, lane : lane + 128], axis=0, keepdims=True)
        out_ref[here, :, lane : lane + 128] = jnp.maximum(by_row, by_col)


def nearest(keys, direct, swapped, most, tile):
    n_dp = len(direct)
    total = 2 * n_dp * most
    width = direct[0].shape[-1]
    tiles = total // tile
    pairs = np.array([(i, j) for i in range(tiles) for j in range(i + 1, tiles)], np.int32).T
    anywhere = pl.BlockSpec(memory_space=pl.ANY)
    return pl.pallas_call(
        functools.partial(nearest_kernel, most=most, tile=tile, n_dp=n_dp),
        in_specs=[pl.BlockSpec(memory_space=pltpu.SMEM), pl.BlockSpec(memory_space=pltpu.VMEM)] + [anywhere] * (2 * n_dp),
        out_specs=pl.BlockSpec(memory_space=pltpu.VMEM),
        out_shape=jax.ShapeDtypeStruct((tiles, 1, tile), jnp.float32),
        scratch_shapes=[
            pltpu.VMEM((total, width), jnp.bfloat16),
            pltpu.VMEM((total, 128), jnp.float32),
            pltpu.VMEM((total, 128), jnp.float32),
            pltpu.VMEM((tiles, 8, tile), jnp.float32),
            pltpu.SemaphoreType.DMA,
        ],
        compiler_params=pltpu.CompilerParams(vmem_limit_bytes=VMEM_LIMIT),
        name="nearest",
    )(jnp.asarray(pairs), keys.reshape(tiles, 1, tile), *direct, *swapped)


def lookup_kernel(table_ref, cluster_ref, pos_ref, out_ref):
    clusters, most = table_ref.shape
    rows_dev = pos_ref.shape[1]
    table = table_ref[...]
    high = table.astype(jnp.bfloat16)
    rest = table - high.astype(jnp.float32)
    middle = rest.astype(jnp.bfloat16)
    low = (rest - middle.astype(jnp.float32)).astype(jnp.bfloat16)
    limbs = jnp.concatenate([high, middle, low], axis=0)
    chosen = (lax.broadcasted_iota(jnp.int32, (most, rows_dev), 0) == pos_ref[...]).astype(jnp.float32).astype(jnp.bfloat16)
    found = jnp.dot(limbs, chosen, preferred_element_type=jnp.float32)
    value = found[:clusters] + found[clusters : 2 * clusters] + found[2 * clusters :]
    mine = lax.broadcasted_iota(jnp.int32, (clusters, rows_dev), 0) == cluster_ref[...]
    out_ref[...] = jnp.sum(jnp.where(mine, value, 0.0), axis=0, keepdims=True)


def lookup(table, cluster, pos):
    return pl.pallas_call(
        lookup_kernel,
        out_shape=jax.ShapeDtypeStruct(pos.shape, jnp.float32),
        compiler_params=pltpu.CompilerParams(vmem_limit_bytes=VMEM_LIMIT),
        name="lookup",
    )(table, cluster, pos)


def per_device(embeddings, assignment, order_key):
    rows_dev, width = embeddings.shape
    n_dp, n_split = lax.axis_size("dp"), lax.axis_size("split")
    clusters = CL_OWN * n_dp
    most = 3 * rows_dev // (2 * clusters)
    me = CL_OWN * lax.axis_index("dp") + lax.axis_index("split")
    by_offset = jnp.arange(clusters, dtype=jnp.int32) ^ me
    cluster = assignment.reshape(1, rows_dev)
    order = order_key.reshape(1, rows_dev)
    packed, keys, pos = pack(me.reshape(1), cluster, order, embeddings, clusters, most)
    got = {0: packed[0]}
    for k in range(n_dp - 1, 0, -1):
        got[k] = lax.ppermute(packed[k], "dp", [(i, i ^ k) for i in range(n_dp)])
    swap = [(i, i ^ 1) for i in range(n_split)]
    swapped = [lax.ppermute(got[k][most:], "split", swap) for k in range(n_dp)]
    got_keys = lax.all_to_all(keys.reshape(clusters, most)[by_offset], DEVICE, split_axis=0, concat_axis=0, tiled=True)
    best = nearest(got_keys[by_offset], [got[k] for k in range(n_dp)], swapped, most, 384)
    maxima = best.reshape(clusters, most)[by_offset]
    table = lax.all_to_all(maxima, DEVICE, split_axis=0, concat_axis=0, tiled=True)
    return lookup(table, cluster, pos).reshape(rows_dev)


def solution(mesh):
    placed = (
        P(("groups", "dp", "split"), None),
        P(("groups", "dp", "split"), None),
        P(("groups", "dp", "split")),
    )
    return jax.shard_map(
        per_device,
        mesh=mesh,
        in_specs=placed,
        out_specs=P(("groups", "dp", "split")),
        check_vma=False,
    )
```

time: 205 us -> 149 us (0.73)
  blocking collectives: 79.6 us -> 18.9 us
  starting transfers between devices: 6.92 us -> 52.8 us
  Pallas kernels: 0 us -> 31 us
  other arithmetic: 20.9 us -> 0.75 us
  matrix products: 19.5 us -> 0 us
  local copies, waits for them, and re-layouts: 35.7 us -> 18 us
  loops' own time: 15.3 us -> 0 us
  between operations: 13.5 us -> 0.17 us
  waiting for transfers between devices: 13.1 us -> 26.3 us
    all_to_all x1 -> x2, blocking collectives: 77.8 us -> 18.9 us  [the longest x1 9.86 us: per_device(): lax.all_to_all(keys.reshape(clusters, most)[by_offset], DEVICE, split_axi...]
    ppermute x0 -> x15, starting transfers between devices: none -> 52.8 us  [the longest x7 51.2 us: per_device(): got[k] = lax.ppermute(packed[k], 'dp', [(i, i ^ k) for i in range(n_dp)])]
    pallas_call x0 -> x3, Pallas kernels: none -> 31 us  [the longest x1 18.6 us: nearest(): pl.pallas_call(functools.partial(nearest_kernel, most=most, tile=tile, n_...]
    ppermute x0 -> x15, waiting for transfers between devices: none -> 26.3 us  [the longest x7 26.2 us: per_device(): got[k] = lax.ppermute(packed[k], 'dp', [(i, i ^ k) for i in range(n_dp)])]
    dot_general x4 -> x0, matrix products: 19.5 us -> none  [step(): lax.dot_general(own_blocks[index], cols[which], (((1,), (1,)), ((), ())),...]
    gather x1 -> x3, local copies, waits for them, and re-layouts: 20.5 us -> 4.46 us  [the longest x1 1.88 us: per_device(): keys.reshape(clusters, most)[by_offset]]
    another operation x1 -> x0, loops' own time: 15.3 us -> none  [tile_max(): return lax.map(step, jnp.arange(count * 2)).reshape(count, length)]
    all_to_all x2 -> x0, waiting for transfers between devices: 13.1 us -> none  [the longest x1 6.57 us: per_device(): lax.all_to_all(send_keys, 'dp', split_axis=0, concat_axis=0, tiled=True)]
  transfers between devices with their start and end apart: 3 -> 15, of which waited for: 2 -> 3; matrix products, arithmetic and copies ran while one was open for 4% -> 7% of each run, Pallas kernels for 0% -> 0%
where the time goes in v1:
time: 149 us; the launch traced here: 148 us
  starting transfers between devices  52.8 us (35%)
  Pallas kernels  31 us (21%)
  waiting for transfers between devices  26.3 us (18%)
  blocking collectives  18.9 us (13%)
  local copies, waits for them, and re-layouts  18 us (12%)
    ppermute x7, starting transfers between devices, per_device(): got[k] = lax.ppermute(packed[k], 'dp', [(i, i ^ k) for i in range(n_dp)])  51.2 us
    ppermute x7, waiting for transfers between devices, per_device(): got[k] = lax.ppermute(packed[k], 'dp', [(i, i ^ k) for i in range(n_dp)])  26.2 us
    pallas_call x1, Pallas kernels, nearest(): pl.pallas_call(functools.partial(nearest_kernel, most=most, tile=tile, n_...  18.6 us
    pallas_call x1, Pallas kernels, pack(): pl.pallas_call(functools.partial(pack_kernel, clusters=clusters, most=mos...  11.5 us
    all_to_all x1, blocking collectives, per_device(): lax.all_to_all(keys.reshape(clusters, most)[by_offset], DEVICE, split_axi...  9.86 us
    all_to_all x1, blocking collectives, per_device(): lax.all_to_all(maxima, DEVICE, split_axis=0, concat_axis=0, tiled=True)  9.07 us
    unnamed x25, local copies, waits for them, and re-layouts  8.17 us
    slice x8, local copies, waits for them, and re-layouts, per_device(): swapped = [lax.ppermute(got[k][most:], 'split', swap) for k in range(n_dp)]  3.49 us
  transfers between devices with their start and end apart: 15, of which 3 were waited for; matrix products, arithmetic and copies ran while one was open for 7% of the time, Pallas kernels for 0%

profile of v1, /device:TPU:0, one launch (start us, length us, event | category | flops | bytes accessed | tf_op | source)
XLA Modules:
  0.0 148.0 jit_solution(15751622312895988355)
XLA Ops:
  0.0 1.6 %copy-done = bf16[2048,512]{1,0:T(8,128)(2,1)S(1)} copy-done((bf16[2048,512]{1,0:T(8,128)(2,1)S(1)}, bf16[2048,512]{1,0:T(8,128)(2,1)}, u32[]{:S(2)}) %copy-start) | copy-done | bytes 2097176
  3.0 11.5 %pack.1 = (bf16[8,384,512]{2,1,0:T(8,128)(2,1)S(1)}, f32[16,1,192]{2,1,0:T(1,128)S(1)}, s32[1,2048]{1,0:T(1,128)S(1)}) custom-call(s32[1]{0:T(128)} %bitcast.me_ref, s32[1,2048]{1,0:T(1,128)S(1)} %bitcast.36, s32[1,2048]{1,0:T(1,128)S(1)} %bitcast.38, bf16[2048,512]{1,0:T(8,128)(2,1)S(1)} %copy-done), custom_call_target="tpu_custom_call" | custom-call | tf_op jit(solution)/shard_map/pack/pallas_call | solution.py:65
  15.2 6.0 %collective-permute-start.6 = (bf16[384,512]{1,0:T(8,128)(2,1)S(1)}, bf16[384,512]{1,0:T(8,128)(2,1)S(1)}, u32[]{:S(2)}, u32[]{:S(2)}) collective-permute-start(bf16[384,512]{1,0:T(8,128)(2,1)S(1)} %get-tuple-element.11), channel_id=1, source_target_pairs={{0,14},{2,12},{4,10},{6,8},{8,6},{10,4},{12,2},{14,0},{1,15},{3,13... | collective-permute-start | bytes 1179656 | tf_op jit(solution)/shard_map/ppermute | solution.py:206
  21.4 0.7 collective-permute-start.4
  22.2 2.0 %collective-permute-start.3 = (bf16[384,512]{1,0:T(8,128)(2,1)S(1)}, bf16[384,512]{1,0:T(8,128)(2,1)S(1)}, u32[]{:S(2)}, u32[]{:S(2)}) collective-permute-start(bf16[384,512]{1,0:T(8,128)(2,1)S(1)} %get-tuple-element.14), channel_id=1, source_target_pairs={{0,8},{2,10},{4,12},{6,14},{8,0},{10,2},{12,4},{14,6},{1,9},{3,11}... | collective-permute-start | bytes 1179656 | tf_op jit(solution)/shard_map/ppermute | solution.py:206
  24.1 2.4 %collective-permute-start.2 = (bf16[384,512]{1,0:T(8,128)(2,1)S(1)}, bf16[384,512]{1,0:T(8,128)(2,1)S(1)}, u32[]{:S(2)}, u32[]{:S(2)}) collective-permute-start(bf16[384,512]{1,0:T(8,128)(2,1)S(1)} %get-tuple-element.15), channel_id=1, source_target_pairs={{0,6},{2,4},{4,2},{6,0},{8,14},{10,12},{12,10},{14,8},{1,7},{3,5},... | collective-permute-start | bytes 1179656 | tf_op jit(solution)/shard_map/ppermute | solution.py:206
  26.5 4.8 %collective-permute-done.6.refs_7_ = bf16[384,512]{1,0:T(8,128)(2,1)S(1)} collective-permute-done((bf16[384,512]{1,0:T(8,128)(2,1)S(1)}, bf16[384,512]{1,0:T(8,128)(2,1)S(1)}, u32[]{:S(2)}, u32[]{:S(2)}) %collective-permute-start.6) | collective-permute-done | bytes 393248 | tf_op jit(solution)/shard_map/ppermute | solution.py:206
  31.3 38.5 %collective-permute-start.1 = (bf16[384,512]{1,0:T(8,128)(2,1)S(1)}, bf16[384,512]{1,0:T(8,128)(2,1)S(1)}, u32[]{:S(2)}, u32[]{:S(2)}) collective-permute-start(bf16[384,512]{1,0:T(8,128)(2,1)S(1)} %get-tuple-element.16), channel_id=1, source_target_pairs={{0,4},{2,6},{4,0},{6,2},{8,12},{10,14},{12,8},{14,10},{1,5},{3,7},... | collective-permute-start | bytes 1179656 | tf_op jit(solution)/shard_map/ppermute | solution.py:206
  69.9 1.4 collective-permute-start
  71.4 13.9 %collective-permute-done.4.refs_5_ = bf16[384,512]{1,0:T(8,128)(2,1)S(1)} collective-permute-done((bf16[384,512]{1,0:T(8,128)(2,1)S(1)}, bf16[384,512]{1,0:T(8,128)(2,1)S(1)}, u32[]{:S(2)}, u32[]{:S(2)}) %collective-permute-start.4) | collective-permute-done | bytes 393248 | tf_op jit(solution)/shard_map/ppermute | solution.py:206
  85.3 7.5 %collective-permute-done.3.refs_4_ = bf16[384,512]{1,0:T(8,128)(2,1)S(1)} collective-permute-done((bf16[384,512]{1,0:T(8,128)(2,1)S(1)}, bf16[384,512]{1,0:T(8,128)(2,1)S(1)}, u32[]{:S(2)}, u32[]{:S(2)}) %collective-permute-start.3) | collective-permute-done | bytes 393248 | tf_op jit(solution)/shard_map/ppermute | solution.py:206
  95.2 0.7 slice.77
  97.1 0.7 slice.75
  99.1 1.9 %gather_fusion = f32[16,192]{1,0:T(8,128)} fusion(f32[16,192]{1,0:T(8,128)} %bitcast.39, s32[1024]{0:T(1024)S(1)} %pad_clamp_fusion), kind=kCustom, calls=%fused_computation | custom fusion | bytes 24640 | tf_op jit(solution)/shard_map/gather | solution.py:209
  101.0 0.7 copy.5
  101.8 9.9 %all_to_all.23 = f32[16,1,192]{2,1,0:T(1,128)S(1)} all-to-all(f32[16,1,192]{2,1,0:T(1,128)S(1)} %copy.5), channel_id=1, replica_groups=mesh['groups'=2,'dp'=8,'split'=2] {'dp','split'}, dimensions={0} | all-to-all | bytes 24576 | tf_op jit(solution)/shard_map/all_to_all | solution.py:209
  112.2 1.9 %gather_fusion.1 = f32[16,192]{1,0:T(8,128)} fusion(f32[16,192]{1,0:T(8,128)} %bitcast.40, s32[1024]{0:T(1024)S(1)} %pad_clamp_fusion), kind=kCustom, calls=%fused_computation.1 | custom fusion | bytes 24640 | tf_op jit(solution)/shard_map/gather | solution.py:210
  114.1 0.8 reshape.46.keys_ref
  115.0 0.9 copy-done.2
  115.9 18.6 %nearest.1 = f32[8,1,384]{2,1,0:T(1,128)S(1)} custom-call(s32[2,28]{1,0:T(2,128)S(1)} %copy-done.9, f32[8,1,384]{2,1,0:T(1,128)S(1)} %reshape.46.keys_ref, bf16[384,512]{1,0:T(8,128)(2,1)S(1)} %get-tuple-element.18.refs_0_, bf16[384,512]{1,0:T(8,128)(2,1)S(1)} %collective-permute-done.refs_1_, bf16[384,512]{1,0:T(8,128)(2,1)S(1)} %collective-permute-done.1.refs_2_, ...), custom_call_target="tpu_custom_call" | custom-call | tf_op jit(solution)/shard_map/nearest/pallas_call | solution.py:152
  135.1 0.7 reduce
  136.0 0.7 gather_fusion.2
  136.7 9.1 %all_to_all.24 = f32[16,1,192]{2,1,0:T(1,128)S(1)} all-to-all(f32[16,1,192]{2,1,0:T(1,128)S(1)} %copy.6), channel_id=1, replica_groups=mesh['groups'=2,'dp'=8,'split'=2] {'dp','split'}, dimensions={0} | all-to-all | bytes 24576 | tf_op jit(solution)/shard_map/all_to_all | solution.py:212
  147.1 0.9 lookup.1
  (55 shorter events, 10.0 us)
Async XLA Ops:
  0.0 1.6 %copy-start = (bf16[2048,512]{1,0:T(8,128)(2,1)S(1)}, bf16[2048,512]{1,0:T(8,128)(2,1)}, u32[]{:S(2)}) copy-start(bf16[2048,512]{1,0:T(8,128)(2,1)} %emb_ref.1) | copy-start | bytes 6291460
  1.6 0.7 copy-start.4
  2.3 0.7 copy-start.6
  14.5 0.7 copy-start.7
  15.2 99.8 %copy-start.9 = (s32[2,28]{1,0:T(2,128)S(1)}, s32[2,28]{1,0:T(2,128)}, u32[]{:S(2)}) copy-start(s32[2,28]{1,0:T(2,128)} %constant.16.clone.pairs_ref) | copy-start | bytes 676
  15.2 16.1 %collective-permute-start.6 = (bf16[384,512]{1,0:T(8,128)(2,1)S(1)}, bf16[384,512]{1,0:T(8,128)(2,1)S(1)}, u32[]{:S(2)}, u32[]{:S(2)}) collective-permute-start(bf16[384,512]{1,0:T(8,128)(2,1)S(1)} %get-tuple-element.11), channel_id=1, source_target_pairs={{0,14},{2,12},{4,10},{6,8},{8,6},{10,4},{12,2},{14,0},{1,15},{3,13... | collective-permute-start | bytes 1179656 | tf_op jit(solution)/shard_map/ppermute | solution.py:206
  21.2 48.7 %collective-permute-start.5 = (bf16[384,512]{1,0:T(8,128)(2,1)S(1)}, bf16[384,512]{1,0:T(8,128)(2,1)S(1)}, u32[]{:S(2)}, u32[]{:S(2)}) collective-permute-start(bf16[384,512]{1,0:T(8,128)(2,1)S(1)} %get-tuple-element.12), channel_id=1, source_target_pairs={{0,12},{2,14},{4,8},{6,10},{8,4},{10,6},{12,0},{14,2},{1,13},{3,15... | collective-permute-start | bytes 1179656 | tf_op jit(solution)/shard_map/ppermute | solution.py:206
  21.4 63.9 %collective-permute-start.4 = (bf16[384,512]{1,0:T(8,128)(2,1)S(1)}, bf16[384,512]{1,0:T(8,128)(2,1)S(1)}, u32[]{:S(2)}, u32[]{:S(2)}) collective-permute-start(bf16[384,512]{1,0:T(8,128)(2,1)S(1)} %get-tuple-element.13), channel_id=1, source_target_pairs={{0,10},{2,8},{4,14},{6,12},{8,2},{10,0},{12,6},{14,4},{1,11},{3,9}... | collective-permute-start | bytes 1179656 | tf_op jit(solution)/shard_map/ppermute | solution.py:206
  22.2 70.6 %collective-permute-start.3 = (bf16[384,512]{1,0:T(8,128)(2,1)S(1)}, bf16[384,512]{1,0:T(8,128)(2,1)S(1)}, u32[]{:S(2)}, u32[]{:S(2)}) collective-permute-start(bf16[384,512]{1,0:T(8,128)(2,1)S(1)} %get-tuple-element.14), channel_id=1, source_target_pairs={{0,8},{2,10},{4,12},{6,14},{8,0},{10,2},{12,4},{14,6},{1,9},{3,11}... | collective-permute-start | bytes 1179656 | tf_op jit(solution)/shard_map/ppermute | solution.py:206
  24.1 68.6 %collective-permute-start.2 = (bf16[384,512]{1,0:T(8,128)(2,1)S(1)}, bf16[384,512]{1,0:T(8,128)(2,1)S(1)}, u32[]{:S(2)}, u32[]{:S(2)}) collective-permute-start(bf16[384,512]{1,0:T(8,128)(2,1)S(1)} %get-tuple-element.15), channel_id=1, source_target_pairs={{0,6},{2,4},{4,2},{6,0},{8,14},{10,12},{12,10},{14,8},{1,7},{3,5},... | collective-permute-start | bytes 1179656 | tf_op jit(solution)/shard_map/ppermute | solution.py:206
  31.3 64.6 %collective-permute-start.1 = (bf16[384,512]{1,0:T(8,128)(2,1)S(1)}, bf16[384,512]{1,0:T(8,128)(2,1)S(1)}, u32[]{:S(2)}, u32[]{:S(2)}) collective-permute-start(bf16[384,512]{1,0:T(8,128)(2,1)S(1)} %get-tuple-element.16), channel_id=1, source_target_pairs={{0,4},{2,6},{4,0},{6,2},{8,12},{10,14},{12,8},{14,10},{1,5},{3,7},... | collective-permute-start | bytes 1179656 | tf_op jit(solution)/shard_map/ppermute | solution.py:206
  69.9 26.8 %collective-permute-start = (bf16[384,512]{1,0:T(8,128)(2,1)S(1)}, bf16[384,512]{1,0:T(8,128)(2,1)S(1)}, u32[]{:S(2)}, u32[]{:S(2)}) collective-permute-start(bf16[384,512]{1,0:T(8,128)(2,1)S(1)} %get-tuple-element.17), channel_id=1, source_target_pairs={{0,2},{2,0},{4,6},{6,4},{8,10},{10,8},{12,14},{14,12},{1,3},{3,1},... | collective-permute-start | bytes 1179656 | tf_op jit(solution)/shard_map/ppermute | solution.py:206
  85.3 12.6 %collective-permute-start.7 = (bf16[192,512]{1,0:T(8,128)(2,1)S(1)}, bf16[192,512]{1,0:T(8,128)(2,1)S(1)}, u32[]{:S(2)}, u32[]{:S(2)}) collective-permute-start(bf16[192,512]{1,0:T(8,128)(2,1)S(1)} %slice_bitcast_fusion.8), channel_id=1, source_target_pairs={{0,1},{1,0},{2,3},{3,2},{4,5},{5,4},{6,7},{7,6},{8,9},{9,8},{10,11... | collective-permute-start | bytes 589832 | tf_op jit(solution)/shard_map/ppermute | solution.py:208
  92.8 5.1 %collective-permute-start.14 = (bf16[192,512]{1,0:T(8,128)(2,1)S(1)}, bf16[192,512]{1,0:T(8,128)(2,1)S(1)}, u32[]{:S(2)}, u32[]{:S(2)}) collective-permute-start(bf16[192,512]{1,0:T(8,128)(2,1)S(1)} %slice.81), channel_id=1, source_target_pairs={{0,1},{1,0},{2,3},{3,2},{4,5},{5,4},{6,7},{7,6},{8,9},{9,8},{10,11... | collective-permute-start | bytes 589832 | tf_op jit(solution)/shard_map/ppermute | solution.py:208
  92.8 5.6 %collective-permute-start.13 = (bf16[192,512]{1,0:T(8,128)(2,1)S(1)}, bf16[192,512]{1,0:T(8,128)(2,1)S(1)}, u32[]{:S(2)}, u32[]{:S(2)}) collective-permute-start(bf16[192,512]{1,0:T(8,128)(2,1)S(1)} %slice.80), channel_id=1, source_target_pairs={{0,1},{1,0},{2,3},{3,2},{4,5},{5,4},{6,7},{7,6},{8,9},{9,8},{10,11... | collective-permute-start | bytes 589832 | tf_op jit(solution)/shard_map/ppermute | solution.py:208
  95.9 19.0 %collective-permute-start.12 = (bf16[192,512]{1,0:T(8,128)(2,1)}, bf16[192,512]{1,0:T(8,128)(2,1)}, u32[]{:S(2)}, u32[]{:S(2)}) collective-permute-start(bf16[192,512]{1,0:T(8,128)(2,1)} %slice.79), channel_id=1, source_target_pairs={{0,1},{1,0},{2,3},{3,2},{4,5},{5,4},{6,7},{7,6},{8,9},{9,8},{10,11... | collective-permute-start | bytes 589832 | tf_op jit(solution)/shard_map/ppermute | solution.py:208
  96.6 18.3 %collective-permute-start.11 = (bf16[192,512]{1,0:T(8,128)(2,1)}, bf16[192,512]{1,0:T(8,128)(2,1)}, u32[]{:S(2)}, u32[]{:S(2)}) collective-permute-start(bf16[192,512]{1,0:T(8,128)(2,1)} %slice.78), channel_id=1, source_target_pairs={{0,1},{1,0},{2,3},{3,2},{4,5},{5,4},{6,7},{7,6},{8,9},{9,8},{10,11... | collective-permute-start | bytes 589832 | tf_op jit(solution)/shard_map/ppermute | solution.py:208
  97.8 17.1 %collective-permute-start.10 = (bf16[192,512]{1,0:T(8,128)(2,1)}, bf16[192,512]{1,0:T(8,128)(2,1)}, u32[]{:S(2)}, u32[]{:S(2)}) collective-permute-start(bf16[192,512]{1,0:T(8,128)(2,1)} %slice.77), channel_id=1, source_target_pairs={{0,1},{1,0},{2,3},{3,2},{4,5},{5,4},{6,7},{7,6},{8,9},{9,8},{10,11... | collective-permute-start | bytes 589832 | tf_op jit(solution)/shard_map/ppermute | solution.py:208
  97.9 17.1 %collective-permute-start.9 = (bf16[192,512]{1,0:T(8,128)(2,1)}, bf16[192,512]{1,0:T(8,128)(2,1)}, u32[]{:S(2)}, u32[]{:S(2)}) collective-permute-start(bf16[192,512]{1,0:T(8,128)(2,1)} %slice.76), channel_id=1, source_target_pairs={{0,1},{1,0},{2,3},{3,2},{4,5},{5,4},{6,7},{7,6},{8,9},{9,8},{10,11... | collective-permute-start | bytes 589832 | tf_op jit(solution)/shard_map/ppermute | solution.py:208
  99.0 15.9 %collective-permute-start.8 = (bf16[192,512]{1,0:T(8,128)(2,1)}, bf16[192,512]{1,0:T(8,128)(2,1)}, u32[]{:S(2)}, u32[]{:S(2)}) collective-permute-start(bf16[192,512]{1,0:T(8,128)(2,1)} %slice.75), channel_id=1, source_target_pairs={{0,1},{1,0},{2,3},{3,2},{4,5},{5,4},{6,7},{7,6},{8,9},{9,8},{10,11... | collective-permute-start | bytes 589832 | tf_op jit(solution)/shard_map/ppermute | solution.py:208
  99.1 13.1 %copy-start.10 = (s32[1024]{0:T(1024)}, s32[1024]{0:T(1024)S(1)}, u32[]{:S(2)}) copy-start(s32[1024]{0:T(1024)S(1)} %pad_clamp_fusion) | copy-start | bytes 12292
  115.0 0.9 copy-start.2
  145.8 0.7 copy-start.5
  146.4 0.7 copy-start.8
  (2 other events, 1.3 us)

commit v2 on v0

v2 whole, which is shorter than its diff:
```python
import functools

import jax
import jax.numpy as jnp
from jax import lax
from jax.experimental import pallas as pl
from jax.experimental.pallas import tpu as pltpu
from jax.sharding import PartitionSpec as P

EPSILON = 1e-06
EMPTY = float(1 << 25)
DEVICE = ("dp", "split")
LANES = 128
GROUPS = 8
ORDER = (8, 9, 6, 7, 10, 11, 4, 5, 12, 13, 2, 3, 0, 1, 14, 15)
STAGES = (2, 2, 3, 1)
KEY_ROWS = 8
VMEM_LIMIT = 24 * 1024 * 1024
FIRST_VMEM_LIMIT = 60 * 1024 * 1024

in_vmem = pl.BlockSpec(memory_space=pltpu.VMEM)
in_smem = pl.BlockSpec(memory_space=pltpu.SMEM)
in_hbm = pl.BlockSpec(memory_space=pltpu.HBM)


def params():
    return pltpu.CompilerParams(vmem_limit_bytes=VMEM_LIMIT)


NO_COST = pl.CostEstimate(flops=0, bytes_accessed=0, transcendentals=0)


def one_hot(slot, first, count):
    shape = (count, slot.shape[1])
    return (lax.broadcasted_iota(jnp.int32, shape, 0) == slot - first).astype(jnp.float32).astype(jnp.bfloat16)


def pack_blocks(slot, limbs, emb, firsts, blocks, most):
    unit = len(blocks) // len(firsts)
    for at, first in enumerate(firsts):
        chosen = one_hot(slot, first * most, unit * most)
        rows = jnp.dot(chosen, emb, preferred_element_type=jnp.float32)
        scale = lax.rsqrt(jnp.sum(rows * rows, axis=1, keepdims=True) + EPSILON)
        rows = (rows * scale).astype(jnp.bfloat16)
        keys = lax.dot_general(limbs, chosen, (((1,), (1,)), ((), ())), preferred_element_type=jnp.float32)
        lane = lax.broadcasted_iota(jnp.int32, keys.shape, 1)
        for i in range(unit):
            block = blocks[at * unit + i]
            block[:most] = rows[i * most : (i + 1) * most]
            mine = (lane >= i * most) & (lane < (i + 1) * most)
            block[most:, : unit * most] = jnp.where(mine, keys, 0.0).astype(jnp.bfloat16)


def key_limbs(order):
    which = lax.broadcasted_iota(jnp.int32, (KEY_ROWS, order.shape[1]), 0)
    limbs = jnp.where(which == 0, order & 255, jnp.where(which == 1, (order >> 8) & 255, (order >> 16) & 255))
    return jnp.where(which == 3, 1, jnp.where(which < 3, limbs, 0)).astype(jnp.float32).astype(jnp.bfloat16)


def keys_of(blocks, most):
    limbs = functools.reduce(jnp.add, [block[most:, : len(blocks) * most].astype(jnp.float32) for block in blocks])
    return limbs[0:1] + 256.0 * limbs[1:2] + 65536.0 * limbs[2:3] + EMPTY * (1.0 - limbs[3:4])


def first_pack_kernel(me_ref, cluster_hbm, order_hbm, emb_hbm, *refs, clusters, most, firsts):
    *blocks, slot_ref, limbs_ref, cluster_ref, order_ref, emb_ref, sems = refs
    rows_dev = emb_ref.shape[0]
    load_cluster = pltpu.make_async_copy(cluster_hbm, cluster_ref, sems.at[0])
    load_order = pltpu.make_async_copy(order_hbm, order_ref, sems.at[1])
    load_emb = pltpu.make_async_copy(emb_hbm, emb_ref, sems.at[2])
    load_cluster.start()
    load_order.start()
    load_emb.start()
    span = 256
    upper = (
        lax.broadcasted_iota(jnp.int32, (span, span), 0) <= lax.broadcasted_iota(jnp.int32, (span, span), 1)
    ).astype(jnp.float32).astype(jnp.bfloat16)
    load_cluster.wait()
    cluster = cluster_ref[...]
    carry = jnp.zeros((clusters, 1), jnp.float32)
    ranks = []
    for part in range(rows_dev // span):
        hot = cluster[:, part * span : (part + 1) * span] == lax.broadcasted_iota(jnp.int32, (clusters, span), 0)
        local = jnp.dot(hot.astype(jnp.float32).astype(jnp.bfloat16), upper, preferred_element_type=jnp.float32)
        running = local + carry
        carry = carry + local[:, span - 1 :]
        ranks.append(jnp.sum(jnp.where(hot, running, 0.0), axis=0, keepdims=True))
    slot = (cluster ^ me_ref[0]) * most + jnp.concatenate(ranks, axis=1).astype(jnp.int32) - 1
    slot_ref[...] = slot
    load_order.wait()
    limbs = key_limbs(order_ref[...])
    limbs_ref[...] = limbs
    load_emb.wait()
    pack_blocks(slot, limbs, emb_ref[...], firsts, blocks, most)


def first_pack(me, cluster, order, embeddings, clusters, most, firsts, unit):
    rows_dev, width = embeddings.shape
    count = len(firsts) * unit
    *blocks, slot, limbs = pl.pallas_call(
        functools.partial(first_pack_kernel, clusters=clusters, most=most, firsts=firsts),
        in_specs=[in_smem, in_hbm, in_hbm, in_hbm],
        out_specs=[in_vmem] * (count + 2),
        out_shape=[jax.ShapeDtypeStruct((most + KEY_ROWS, width), jnp.bfloat16)] * count
        + [jax.ShapeDtypeStruct((1, rows_dev), jnp.int32), jax.ShapeDtypeStruct((KEY_ROWS, rows_dev), jnp.bfloat16)],
        scratch_shapes=[
            pltpu.VMEM((1, rows_dev), jnp.int32),
            pltpu.VMEM((1, rows_dev), jnp.int32),
            pltpu.VMEM((rows_dev, width), jnp.bfloat16),
            pltpu.SemaphoreType.DMA((3,)),
        ],
        compiler_params=pltpu.CompilerParams(vmem_limit_bytes=FIRST_VMEM_LIMIT),
        cost_estimate=NO_COST,
        name="first_pack",
    )(me, cluster, order, embeddings)
    return blocks, slot, limbs


def pack_kernel(slot_ref, limbs_ref, emb_hbm, *refs, firsts, most):
    *blocks, emb_ref, sem = refs
    load_emb = pltpu.make_async_copy(emb_hbm, emb_ref, sem)
    load_emb.start()
    load_emb.wait()
    pack_blocks(slot_ref[...], limbs_ref[...], emb_ref[...], firsts, blocks, most)


def pack(slot, limbs, embeddings, most, firsts, unit):
    rows_dev, width = embeddings.shape
    count = len(firsts) * unit
    return pl.pallas_call(
        functools.partial(pack_kernel, firsts=firsts, most=most),
        in_specs=[in_vmem, in_vmem, in_hbm],
        out_specs=[in_vmem] * count,
        out_shape=[jax.ShapeDtypeStruct((most + KEY_ROWS, width), jnp.bfloat16)] * count,
        scratch_shapes=[pltpu.VMEM((rows_dev, width), jnp.bfloat16), pltpu.SemaphoreType.DMA],
        compiler_params=params(),
        cost_estimate=NO_COST,
        name=f"pack_{firsts[0]}",
    )(slot, limbs, embeddings)


def fold_rows(partial):
    return jnp.concatenate(
        [jnp.max(partial[at : at + LANES].T, axis=0, keepdims=True) for at in range(0, partial.shape[0], LANES)], axis=1
    )


def stage_kernel(*refs, old, blocks, most, unit, arrival):
    me_ref, refs = refs[0], refs[1:]
    if old:
        best_ref, refs = refs[0], refs[1:]
    sources, (out_ref, rows, keys_ref, own_keys, row_best, all_best) = refs[:blocks], refs[blocks:]
    total, before = blocks * most, old * most
    fresh = total - before
    chunk = next(c for c in (384, 256, 128) if fresh % c == 0)
    tile = next(t for t in (768, 512, 384, 256, 128) if total % t == 0)
    for i, source in enumerate(sources):
        rows[i * most : (i + 1) * most] = source[:most]
    for i in range(0, blocks, unit):
        keys_ref[:, i * most : (i + unit) * most] = keys_of(sources[i : i + unit], most)
    for at in range(0, fresh, LANES):
        own_keys[at : at + LANES] = jnp.broadcast_to(keys_ref[:, before + at : before + at + LANES], (LANES, LANES)).T
    row_best[...] = jnp.full_like(row_best, -1.0)
    if old:
        all_best[:, :before] = best_ref[...]
        all_best[:, before:] = jnp.full((1, fresh), -1.0, jnp.float32)

    for base in range(0, fresh, chunk):
        own_rows = rows[before + base : before + base + chunk]
        own = own_keys[base : base + chunk]
        best = row_best[base : base + chunk]
        for at in range(0, total, tile):
            sim = lax.dot_general(
                own_rows, rows[at : at + tile], (((1,), (1,)), ((), ())), preferred_element_type=jnp.float32
            )
            for lane in range(0, tile, LANES):
                here = slice(at + lane, at + lane + LANES)
                part = sim[:, lane : lane + LANES]
                earlier = keys_ref[:, here] < own
                best = jnp.maximum(best, jnp.where(earlier, part, -1.0))
                if at + lane < before:
                    later = jnp.max(jnp.where(earlier, -1.0, part), axis=0, keepdims=True)
                    all_best[:, here] = jnp.maximum(all_best[:, here], later)
        row_best[base : base + chunk] = best

    found = fold_rows(row_best[...])
    if old:
        found = jnp.maximum(found, all_best[:, before:])
    if not arrival:
        out_ref[:, before:] = found
        if old:
            out_ref[:, :before] = all_best[:, :before]
        return
    all_best[:, before:] = found
    shifts = {}
    for block in range(blocks):
        shift = block * most % LANES
        if shift not in shifts:
            shifts[shift] = pltpu.roll(all_best[...], total - shift, 1) if shift else all_best[...]
        start = block * most - shift
        out_ref[arrival[block] ^ me_ref[0]] = shifts[shift][:, start : start + most]


def stage(me, best, sources, arrival, old, unit):
    blocks = len(sources)
    height, width = sources[0].shape
    most = height - KEY_ROWS
    last = blocks == len(arrival)
    total, fresh = blocks * most, (blocks - old) * most
    shape = (blocks, 1, most) if last else (1, total)
    operands = [me] + ([best] if old else []) + sources
    return pl.pallas_call(
        functools.partial(stage_kernel, old=old, blocks=blocks, most=most, unit=unit, arrival=arrival if last else None),
        in_specs=[in_smem] + [in_vmem] * (len(operands) - 1),
        out_specs=in_vmem,
        out_shape=jax.ShapeDtypeStruct(shape, jnp.float32),
        scratch_shapes=[
            pltpu.VMEM((total, width), jnp.bfloat16),
            pltpu.VMEM((1, total), jnp.float32),
            pltpu.VMEM((fresh, LANES), jnp.float32),
            pltpu.VMEM((fresh, LANES), jnp.float32),
            pltpu.VMEM((1, total), jnp.float32),
        ],
        compiler_params=params(),
        cost_estimate=NO_COST,
        name=f"stage_{old}",
    )(*operands)


def lookup_kernel(me_ref, table_ref, slot_ref, out_ref):
    clusters, _, most = table_ref.shape
    rows_dev = slot_ref.shape[1]
    table = table_ref[...].reshape(clusters, most)
    high = table.astype(jnp.bfloat16)
    rest = table - high.astype(jnp.float32)
    middle = rest.astype(jnp.bfloat16)
    low = (rest - middle.astype(jnp.float32)).astype(jnp.bfloat16)
    limbs = jnp.concatenate([high, middle, low], axis=0)
    slot = slot_ref[...]
    shape = (clusters, rows_dev)
    place = lax.broadcasted_iota(jnp.int32, shape, 0)
    start = (place ^ me_ref[0]) * most
    mine = (slot >= start) & (slot < start + most)
    within = jnp.sum(jnp.where(mine, slot - start, 0), axis=0, keepdims=True)
    found = jnp.dot(limbs, one_hot(within, 0, most), preferred_element_type=jnp.float32)
    value = found[:clusters] + found[clusters : 2 * clusters] + found[2 * clusters :]
    out_ref[...] = jnp.sum(jnp.where(mine, value, 0.0), axis=0, keepdims=True)


def lookup(me, table, slot):
    return pl.pallas_call(
        lookup_kernel,
        in_specs=[in_smem, in_vmem, in_vmem],
        out_specs=in_vmem,
        out_shape=jax.ShapeDtypeStruct(slot.shape, jnp.float32),
        compiler_params=params(),
        name="lookup",
    )(me, table, slot)


def after(value, *others):
    return lax.optimization_barrier((value, *others))


def per_device(embeddings, assignment, order_key):
    rows_dev, _ = embeddings.shape
    clusters = lax.axis_size("dp") * lax.axis_size("split")
    most = 3 * rows_dev // (2 * clusters)
    unit, half = clusters // GROUPS, clusters // 2
    me = lax.axis_index("dp") * lax.axis_size("split") + lax.axis_index("split")
    scalar = me.reshape(1).astype(jnp.int32)
    cluster = assignment.reshape(1, rows_dev)
    order = order_key.reshape(1, rows_dev)

    def send(block, offset):
        return lax.ppermute(block, DEVICE, [(i, i ^ offset) for i in range(clusters)])

    groups = [range(g * unit, (g + 1) * unit) for g in range(GROUPS)]
    rows = {}

    def keep(group_numbers, blocks):
        rows.update(zip([o for g in group_numbers for o in groups[g]], blocks, strict=True))

    head, slot, limbs = first_pack(scalar, cluster, order, embeddings, clusters, most, [half], unit)
    keep([GROUPS // 2], head)
    later = [*range(GROUPS // 2 + 1, GROUPS), *range(GROUPS // 2)]
    keep(later, pack(slot, limbs, embeddings, most, [g * unit for g in later], unit))
    got = {0: rows[0]}
    for offset in [*range(half, clusters), *range(half - 1, 0, -1)]:
        got[offset] = send(rows[offset], offset)

    part = unit // 2
    arrival = [h * part + i for h in ORDER for i in range(part)]
    best, old = None, 0
    for fresh in STAGES:
        upto = old + fresh * unit
        best = stage(scalar, best, [got[o] for o in arrival[:upto]], arrival, old, unit)
        old = upto
    returned = lax.all_to_all(best, DEVICE, split_axis=0, concat_axis=0, tiled=True)
    return lookup(scalar, returned, slot).reshape(rows_dev)


def solution(mesh):
    placed = (
        P(("groups", "dp", "split"), None),
        P(("groups", "dp", "split"), None),
        P(("groups", "dp", "split")),
    )
    return jax.shard_map(
        per_device,
        mesh=mesh,
        in_specs=placed,
        out_specs=P(("groups", "dp", "split")),
        check_vma=False,
    )
```

time: 205 us -> 95.9 us (0.47)
  blocking collectives: 79.6 us -> 16.9 us
  local copies, waits for them, and re-layouts: 35.7 us -> 1.46 us
  Pallas kernels: 0 us -> 22.9 us
  other arithmetic: 20.9 us -> 0 us
  matrix products: 19.5 us -> 0 us
  waiting for transfers between devices: 13.1 us -> 31.4 us
  starting transfers between devices: 6.92 us -> 22.9 us
  loops' own time: 15.3 us -> 0 us
  between operations: 13.5 us -> 0.08 us
    all_to_all x1, blocking collectives: 77.8 us -> 16.9 us  [per_device(): lax.all_to_all(best, DEVICE, split_axis=0, concat_axis=0, tiled=True)]
    ppermute x0 -> x15, waiting for transfers between devices: none -> 31.4 us  [send(): lax.ppermute(block, DEVICE, [(i, i ^ offset) for i in range(clusters)])]
    pallas_call x0 -> x7, Pallas kernels: none -> 22.9 us  [the longest x4 9.21 us: stage(): pl.pallas_call(functools.partial(stage_kernel, old=old, blocks=blocks, mo...]
    ppermute x0 -> x15, starting transfers between devices: none -> 22.9 us  [send(): lax.ppermute(block, DEVICE, [(i, i ^ offset) for i in range(clusters)])]
    gather x1 -> x0, local copies, waits for them, and re-layouts: 20.5 us -> none  [per_device(): return returned.reshape(clusters * most)[slot]]
    dot_general x4 -> x0, matrix products: 19.5 us -> none  [step(): lax.dot_general(own_blocks[index], cols[which], (((1,), (1,)), ((), ())),...]
    another operation x1 -> x0, loops' own time: 15.3 us -> none  [tile_max(): return lax.map(step, jnp.arange(count * 2)).reshape(count, length)]
    all_to_all x2 -> x0, waiting for transfers between devices: 13.1 us -> none  [the longest x1 6.57 us: per_device(): lax.all_to_all(send_keys, 'dp', split_axis=0, concat_axis=0, tiled=True)]
  transfers between devices with their start and end apart: 3 -> 15, of which waited for: 2 -> 6; matrix products, arithmetic and copies ran while one was open for 4% -> 0% of each run, Pallas kernels for 0% -> 17%
where the time goes in v2:
time: 95.9 us; the launch traced here: 95.7 us
  waiting for transfers between devices  31.4 us (33%)
  Pallas kernels  22.9 us (24%)
  starting transfers between devices  22.9 us (24%)
  blocking collectives  16.9 us (18%)
  local copies, waits for them, and re-layouts  1.46 us (2%)
    ppermute x15, waiting for transfers between devices, send(): lax.ppermute(block, DEVICE, [(i, i ^ offset) for i in range(clusters)])  31.4 us
    ppermute x15, starting transfers between devices, send(): lax.ppermute(block, DEVICE, [(i, i ^ offset) for i in range(clusters)])  22.9 us
    all_to_all x1, blocking collectives, per_device(): lax.all_to_all(best, DEVICE, split_axis=0, concat_axis=0, tiled=True)  16.9 us
    pallas_call x4, Pallas kernels, stage(): pl.pallas_call(functools.partial(stage_kernel, old=old, blocks=blocks, mo...  9.21 us
    pallas_call x1, Pallas kernels, pack(): pl.pallas_call(functools.partial(pack_kernel, firsts=firsts, most=most),...  8.79 us
    pallas_call x1, Pallas kernels, first_pack(): pl.pallas_call(functools.partial(first_pack_kernel, clusters=clusters, mo...  3.92 us
  transfers between devices with their start and end apart: 15, of which 6 were waited for; matrix products, arithmetic and copies ran while one was open for 0% of the time, Pallas kernels for 17%

profile of v2, /device:TPU:0, one launch (start us, length us, event | category | flops | bytes accessed | tf_op | source)
XLA Modules:
  0.0 95.7 jit_solution(14316556195907478281)
XLA Ops:
  0.0 3.9 %first_pack.1 = (bf16[200,512]{1,0:T(8,128)(2,1)}, bf16[200,512]{1,0:T(8,128)(2,1)}, s32[1,2048]{1,0:T(1,128)}, bf16[8,2048]{1,0:T(8,128)(2,1)}) custom-call(s32[1]{0:T(128)} %bitcast.me_ref.refs_0_, s32[1,2048]{1,0:T(1,128)} %bitcast.4, s32[1,2048]{1,0:T(1,128)} %bitcast.5, bf16[2048,512]{1,0:T(8,128)(2,1)} %emb_hbm.3), custom_call_target="tpu_custom_call" | custom-call | tf_op jit(solution)/shard_map/first_pack/pallas_call | solution.py:100
  3.9 4.1 %collective-permute-start = (bf16[200,512]{1,0:T(8,128)(2,1)}, bf16[200,512]{1,0:T(8,128)(2,1)S(1)}, u32[]{:S(2)}, u32[]{:S(2)}) collective-permute-start(bf16[200,512]{1,0:T(8,128)(2,1)} %get-tuple-element.23), channel_id=1, source_target_pairs={{0,8},{1,9},{2,10},{3,11},{4,12},{5,13},{6,14},{7,15},{8,0},{9,1},... | collective-permute-start | bytes 614408 | tf_op jit(solution)/shard_map/ppermute | solution.py:276
  8.0 0.8 copy-done.1
  9.5 8.8 %pack_10.1 = (bf16[200,512]{1,0:T(8,128)(2,1)S(1)}, bf16[200,512]{1,0:T(8,128)(2,1)S(1)}, bf16[200,512]{1,0:T(8,128)(2,1)S(1)}, bf16[200,512]{1,0:T(8,128)(2,1)S...) custom-call(s32[1,2048]{1,0:T(1,128)S(1)} %copy-done.2, ...), custom_call_target="tpu_custom_call" | custom-call | tf_op jit(solution)/shard_map/pack_10/pallas_call | solution.py:130
  18.3 2.6 %collective-permute-start.2 = (bf16[200,512]{1,0:T(8,128)(2,1)S(1)}, bf16[200,512]{1,0:T(8,128)(2,1)S(1)}, u32[]{:S(2)}, u32[]{:S(2)}) collective-permute-start(bf16[200,512]{1,0:T(8,128)(2,1)S(1)} %get-tuple-element.27), channel_id=1, source_target_pairs={{0,6},{1,7},{2,4},{3,5},{4,2},{5,3},{6,0},{7,1},{8,14},{9,15},{10,... | collective-permute-start | bytes 614408 | tf_op jit(solution)/shard_map/ppermute | solution.py:276
  21.0 3.6 %collective-permute-start.4 = (bf16[200,512]{1,0:T(8,128)(2,1)S(1)}, bf16[200,512]{1,0:T(8,128)(2,1)S(1)}, u32[]{:S(2)}, u32[]{:S(2)}) collective-permute-start(bf16[200,512]{1,0:T(8,128)(2,1)S(1)} %get-tuple-element.29), channel_id=1, source_target_pairs={{0,10},{1,11},{2,8},{3,9},{4,14},{5,15},{6,12},{7,13},{8,2},{9,3},... | collective-permute-start | bytes 614408 | tf_op jit(solution)/shard_map/ppermute | solution.py:276
  24.6 1.1 %collective-permute-done.1.refs_2_.refs_3_ = bf16[200,512]{1,0:T(8,128)(2,1)S(1)} collective-permute-done((bf16[200,512]{1,0:T(8,128)(2,1)}, bf16[200,512]{1,0:T(8,128)(2,1)S(1)}, u32[]{:S(2)}, u32[]{:S(2)}) %collective-permute-start.1) | collective-permute-done | bytes 204832 | tf_op jit(solution)/shard_map/ppermute | solution.py:276
  25.7 1.7 %collective-permute-start.6 = (bf16[200,512]{1,0:T(8,128)(2,1)S(1)}, bf16[200,512]{1,0:T(8,128)(2,1)S(1)}, u32[]{:S(2)}, u32[]{:S(2)}) collective-permute-start(bf16[200,512]{1,0:T(8,128)(2,1)S(1)} %get-tuple-element.31), channel_id=1, source_target_pairs={{0,4},{1,5},{2,6},{3,7},{4,0},{5,1},{6,2},{7,3},{8,12},{9,13},{10,... | collective-permute-start | bytes 614408 | tf_op jit(solution)/shard_map/ppermute | solution.py:276
  27.4 10.1 %collective-permute-done.2.refs_3_.refs_4_ = bf16[200,512]{1,0:T(8,128)(2,1)S(1)} collective-permute-done((bf16[200,512]{1,0:T(8,128)(2,1)S(1)}, bf16[200,512]{1,0:T(8,128)(2,1)S(1)}, u32[]{:S(2)}, u32[]{:S(2)}) %collective-permute-start.2) | collective-permute-done | bytes 204832 | tf_op jit(solution)/shard_map/ppermute | solution.py:276
  37.6 4.3 %collective-permute-done.3.refs_4_.refs_5_ = bf16[200,512]{1,0:T(8,128)(2,1)S(1)} collective-permute-done((bf16[200,512]{1,0:T(8,128)(2,1)S(1)}, bf16[200,512]{1,0:T(8,128)(2,1)S(1)}, u32[]{:S(2)}, u32[]{:S(2)}) %collective-permute-start.3) | collective-permute-done | bytes 204832 | tf_op jit(solution)/shard_map/ppermute | solution.py:276
  41.9 1.8 %collective-permute-start.8 = (bf16[200,512]{1,0:T(8,128)(2,1)S(1)}, bf16[200,512]{1,0:T(8,128)(2,1)S(1)}, u32[]{:S(2)}, u32[]{:S(2)}) collective-permute-start(bf16[200,512]{1,0:T(8,128)(2,1)S(1)} %get-tuple-element.33), channel_id=1, source_target_pairs={{0,12},{1,13},{2,14},{3,15},{4,8},{5,9},{6,10},{7,11},{8,4},{9,5},... | collective-permute-start | bytes 614408 | tf_op jit(solution)/shard_map/ppermute | solution.py:276
  43.6 1.6 %collective-permute-start.9 = (bf16[200,512]{1,0:T(8,128)(2,1)S(1)}, bf16[200,512]{1,0:T(8,128)(2,1)S(1)}, u32[]{:S(2)}, u32[]{:S(2)}) collective-permute-start(bf16[200,512]{1,0:T(8,128)(2,1)S(1)} %get-tuple-element.34), channel_id=1, source_target_pairs={{0,13},{1,12},{2,15},{3,14},{4,9},{5,8},{6,11},{7,10},{8,5},{9,4},... | collective-permute-start | bytes 614408 | tf_op jit(solution)/shard_map/ppermute | solution.py:276
  45.3 1.5 %collective-permute-start.10 = (bf16[200,512]{1,0:T(8,128)(2,1)S(1)}, bf16[200,512]{1,0:T(8,128)(2,1)S(1)}, u32[]{:S(2)}, u32[]{:S(2)}) collective-permute-start(bf16[200,512]{1,0:T(8,128)(2,1)S(1)} %get-tuple-element.35), channel_id=1, source_target_pairs={{0,2},{1,3},{2,0},{3,1},{4,6},{5,7},{6,4},{7,5},{8,10},{9,11},{10,... | collective-permute-start | bytes 614408 | tf_op jit(solution)/shard_map/ppermute | solution.py:276
  46.8 1.7 %collective-permute-done.6.refs_8_ = bf16[200,512]{1,0:T(8,128)(2,1)S(1)} collective-permute-done((bf16[200,512]{1,0:T(8,128)(2,1)S(1)}, bf16[200,512]{1,0:T(8,128)(2,1)S(1)}, u32[]{:S(2)}, u32[]{:S(2)}) %collective-permute-start.6) | collective-permute-done | bytes 204832 | tf_op jit(solution)/shard_map/ppermute | solution.py:276
  48.5 1.2 %collective-permute-start.11 = (bf16[200,512]{1,0:T(8,128)(2,1)S(1)}, bf16[200,512]{1,0:T(8,128)(2,1)S(1)}, u32[]{:S(2)}, u32[]{:S(2)}) collective-permute-start(bf16[200,512]{1,0:T(8,128)(2,1)S(1)} %get-tuple-element.36), channel_id=1, source_target_pairs={{0,3},{1,2},{2,1},{3,0},{4,7},{5,6},{6,5},{7,4},{8,11},{9,10},{10,... | collective-permute-start | bytes 614408 | tf_op jit(solution)/shard_map/ppermute | solution.py:276
  49.7 11.9 %collective-permute-done.7.refs_9_ = bf16[200,512]{1,0:T(8,128)(2,1)S(1)} collective-permute-done((bf16[200,512]{1,0:T(8,128)(2,1)S(1)}, bf16[200,512]{1,0:T(8,128)(2,1)S(1)}, u32[]{:S(2)}, u32[]{:S(2)}) %collective-permute-start.7) | collective-permute-done | bytes 204832 | tf_op jit(solution)/shard_map/ppermute | solution.py:276
  61.7 4.5 %collective-permute-start.13 = (bf16[200,512]{1,0:T(8,128)(2,1)S(1)}, bf16[200,512]{1,0:T(8,128)(2,1)S(1)}, u32[]{:S(2)}, u32[]{:S(2)}) collective-permute-start(bf16[200,512]{1,0:T(8,128)(2,1)S(1)} %get-tuple-element.39), channel_id=1, source_target_pairs={{0,14},{1,15},{2,12},{3,13},{4,10},{5,11},{6,8},{7,9},{8,6},{9,7},... | collective-permute-start | bytes 614408 | tf_op jit(solution)/shard_map/ppermute | solution.py:276
  66.3 0.9 stage_0.1.refs_1_
  67.2 1.6 %stage_4.1.refs_1_ = f32[1,1536]{1,0:T(1,128)S(1)} custom-call(s32[1]{0:T(128)} %bitcast.me_ref.refs_0_, f32[1,768]{1,0:T(1,128)S(1)} %stage_0.1.refs_1_, bf16[200,512]{1,0:T(8,128)(2,1)S(1)} %collective-permute-done.refs_1_.refs_2_, bf16[200,512]{1,0:T(8,128)(2,1)S(1)} %collective-permute-done.1.refs_2_.refs_3_, ...), custom_call_target="tpu_custom_call" | custom-call | tf_op jit(solution)/shard_map/stage_4/pallas_call | solution.py:212
  68.8 4.9 %stage_8.1.refs_1_ = f32[1,2688]{1,0:T(1,128)S(1)} custom-call(s32[1]{0:T(128)} %bitcast.me_ref.refs_0_, f32[1,1536]{1,0:T(1,128)S(1)} %stage_4.1.refs_1_, bf16[200,512]{1,0:T(8,128)(2,1)S(1)} %collective-permute-done.refs_1_.refs_2_, bf16[200,512]{1,0:T(8,128)(2,1)S(1)} %collective-permute-done.1.refs_2_.refs_3_, ...), custom_call_target="tpu_custom_call" | custom-call | tf_op jit(solution)/shard_map/stage_8/pallas_call | solution.py:212
  73.8 2.2 %collective-permute-done.14.refs_17_ = bf16[200,512]{1,0:T(8,128)(2,1)S(1)} collective-permute-done((bf16[200,512]{1,0:T(8,128)(2,1)S(1)}, bf16[200,512]{1,0:T(8,128)(2,1)S(1)}, u32[]{:S(2)}, u32[]{:S(2)}) %collective-permute-start.14) | collective-permute-done | bytes 204832 | tf_op jit(solution)/shard_map/ppermute | solution.py:276
  76.0 1.8 %stage_14.1 = f32[16,1,192]{2,1,0:T(1,128)S(1)} custom-call(s32[1]{0:T(128)} %bitcast.me_ref.refs_0_, f32[1,2688]{1,0:T(1,128)S(1)} %stage_8.1.refs_1_, bf16[200,512]{1,0:T(8,128)(2,1)S(1)} %collective-permute-done.refs_1_.refs_2_, bf16[200,512]{1,0:T(8,128)(2,1)S(1)} %collective-permute-done.1.refs_2_.refs_3_, ...), custom_call_target="tpu_custom_call" | custom-call | tf_op jit(solution)/shard_map/stage_14/pallas_call | solution.py:212
  77.8 16.9 %all_to_all.5.table_ref = f32[16,1,192]{2,1,0:T(1,128)S(1)} all-to-all(f32[16,1,192]{2,1,0:T(1,128)S(1)} %stage_14.1), channel_id=1, replica_groups=mesh['groups'=2,'dp'=8,'split'=2] {'dp','split'}, dimensions={0} | all-to-all | bytes 24576 | tf_op jit(solution)/shard_map/all_to_all | solution.py:299
  94.6 1.0 %lookup.1 = f32[1,2048]{1,0:T(1,128)} custom-call(s32[1]{0:T(128)} %bitcast.me_ref.refs_0_, f32[16,1,192]{2,1,0:T(1,128)S(1)} %all_to_all.5.table_ref, s32[1,2048]{1,0:T(1,128)S(1)} %copy-done.3), custom_call_target="tpu_custom_call" | custom-call | tf_op jit(solution)/shard_map/lookup/pallas_call | solution.py:251
  (22 shorter events, 1.1 us)
Async XLA Ops:
  0.0 8.0 %copy-start = (bf16[2048,512]{1,0:T(8,128)(2,1)S(1)}, bf16[2048,512]{1,0:T(8,128)(2,1)}, u32[]{:S(2)}) copy-start(bf16[2048,512]{1,0:T(8,128)(2,1)} %emb_hbm.3) | copy-start | bytes 6291460
  3.9 20.7 %collective-permute-start = (bf16[200,512]{1,0:T(8,128)(2,1)}, bf16[200,512]{1,0:T(8,128)(2,1)S(1)}, u32[]{:S(2)}, u32[]{:S(2)}) collective-permute-start(bf16[200,512]{1,0:T(8,128)(2,1)} %get-tuple-element.23), channel_id=1, source_target_pairs={{0,8},{1,9},{2,10},{3,11},{4,12},{5,13},{6,14},{7,15},{8,0},{9,1},... | collective-permute-start | bytes 614408 | tf_op jit(solution)/shard_map/ppermute | solution.py:276
  8.0 17.7 %collective-permute-start.1 = (bf16[200,512]{1,0:T(8,128)(2,1)}, bf16[200,512]{1,0:T(8,128)(2,1)S(1)}, u32[]{:S(2)}, u32[]{:S(2)}) collective-permute-start(bf16[200,512]{1,0:T(8,128)(2,1)} %get-tuple-element.24), channel_id=1, source_target_pairs={{0,9},{1,8},{2,11},{3,10},{4,13},{5,12},{6,15},{7,14},{8,1},{9,0},... | collective-permute-start | bytes 614408 | tf_op jit(solution)/shard_map/ppermute | solution.py:276
  8.0 0.8 copy-start.1
  8.8 0.7 copy-start.2
  18.3 19.3 %collective-permute-start.2 = (bf16[200,512]{1,0:T(8,128)(2,1)S(1)}, bf16[200,512]{1,0:T(8,128)(2,1)S(1)}, u32[]{:S(2)}, u32[]{:S(2)}) collective-permute-start(bf16[200,512]{1,0:T(8,128)(2,1)S(1)} %get-tuple-element.27), channel_id=1, source_target_pairs={{0,6},{1,7},{2,4},{3,5},{4,2},{5,3},{6,0},{7,1},{8,14},{9,15},{10,... | collective-permute-start | bytes 614408 | tf_op jit(solution)/shard_map/ppermute | solution.py:276
  20.9 21.0 %collective-permute-start.3 = (bf16[200,512]{1,0:T(8,128)(2,1)S(1)}, bf16[200,512]{1,0:T(8,128)(2,1)S(1)}, u32[]{:S(2)}, u32[]{:S(2)}) collective-permute-start(bf16[200,512]{1,0:T(8,128)(2,1)S(1)} %get-tuple-element.28), channel_id=1, source_target_pairs={{0,7},{1,6},{2,5},{3,4},{4,3},{5,2},{6,1},{7,0},{8,15},{9,14},{10,... | collective-permute-start | bytes 614408 | tf_op jit(solution)/shard_map/ppermute | solution.py:276
  21.0 22.6 %collective-permute-start.4 = (bf16[200,512]{1,0:T(8,128)(2,1)S(1)}, bf16[200,512]{1,0:T(8,128)(2,1)S(1)}, u32[]{:S(2)}, u32[]{:S(2)}) collective-permute-start(bf16[200,512]{1,0:T(8,128)(2,1)S(1)} %get-tuple-element.29), channel_id=1, source_target_pairs={{0,10},{1,11},{2,8},{3,9},{4,14},{5,15},{6,12},{7,13},{8,2},{9,3},... | collective-permute-start | bytes 614408 | tf_op jit(solution)/shard_map/ppermute | solution.py:276
  24.6 20.7 %collective-permute-start.5 = (bf16[200,512]{1,0:T(8,128)(2,1)S(1)}, bf16[200,512]{1,0:T(8,128)(2,1)S(1)}, u32[]{:S(2)}, u32[]{:S(2)}) collective-permute-start(bf16[200,512]{1,0:T(8,128)(2,1)S(1)} %get-tuple-element.30), channel_id=1, source_target_pairs={{0,11},{1,10},{2,9},{3,8},{4,15},{5,14},{6,13},{7,12},{8,3},{9,2},... | collective-permute-start | bytes 614408 | tf_op jit(solution)/shard_map/ppermute | solution.py:276
  25.7 22.7 %collective-permute-start.6 = (bf16[200,512]{1,0:T(8,128)(2,1)S(1)}, bf16[200,512]{1,0:T(8,128)(2,1)S(1)}, u32[]{:S(2)}, u32[]{:S(2)}) collective-permute-start(bf16[200,512]{1,0:T(8,128)(2,1)S(1)} %get-tuple-element.31), channel_id=1, source_target_pairs={{0,4},{1,5},{2,6},{3,7},{4,0},{5,1},{6,2},{7,3},{8,12},{9,13},{10,... | collective-permute-start | bytes 614408 | tf_op jit(solution)/shard_map/ppermute | solution.py:276
  37.6 23.9 %collective-permute-start.7 = (bf16[200,512]{1,0:T(8,128)(2,1)S(1)}, bf16[200,512]{1,0:T(8,128)(2,1)S(1)}, u32[]{:S(2)}, u32[]{:S(2)}) collective-permute-start(bf16[200,512]{1,0:T(8,128)(2,1)S(1)} %get-tuple-element.32), channel_id=1, source_target_pairs={{0,5},{1,4},{2,7},{3,6},{4,1},{5,0},{6,3},{7,2},{8,13},{9,12},{10,... | collective-permute-start | bytes 614408 | tf_op jit(solution)/shard_map/ppermute | solution.py:276
  41.9 19.8 %collective-permute-start.8 = (bf16[200,512]{1,0:T(8,128)(2,1)S(1)}, bf16[200,512]{1,0:T(8,128)(2,1)S(1)}, u32[]{:S(2)}, u32[]{:S(2)}) collective-permute-start(bf16[200,512]{1,0:T(8,128)(2,1)S(1)} %get-tuple-element.33), channel_id=1, source_target_pairs={{0,12},{1,13},{2,14},{3,15},{4,8},{5,9},{6,10},{7,11},{8,4},{9,5},... | collective-permute-start | bytes 614408 | tf_op jit(solution)/shard_map/ppermute | solution.py:276
  43.6 22.6 %collective-permute-start.9 = (bf16[200,512]{1,0:T(8,128)(2,1)S(1)}, bf16[200,512]{1,0:T(8,128)(2,1)S(1)}, u32[]{:S(2)}, u32[]{:S(2)}) collective-permute-start(bf16[200,512]{1,0:T(8,128)(2,1)S(1)} %get-tuple-element.34), channel_id=1, source_target_pairs={{0,13},{1,12},{2,15},{3,14},{4,9},{5,8},{6,11},{7,10},{8,5},{9,4},... | collective-permute-start | bytes 614408 | tf_op jit(solution)/shard_map/ppermute | solution.py:276
  45.3 23.5 %collective-permute-start.10 = (bf16[200,512]{1,0:T(8,128)(2,1)S(1)}, bf16[200,512]{1,0:T(8,128)(2,1)S(1)}, u32[]{:S(2)}, u32[]{:S(2)}) collective-permute-start(bf16[200,512]{1,0:T(8,128)(2,1)S(1)} %get-tuple-element.35), channel_id=1, source_target_pairs={{0,2},{1,3},{2,0},{3,1},{4,6},{5,7},{6,4},{7,5},{8,10},{9,11},{10,... | collective-permute-start | bytes 614408 | tf_op jit(solution)/shard_map/ppermute | solution.py:276
  48.5 20.3 %collective-permute-start.11 = (bf16[200,512]{1,0:T(8,128)(2,1)S(1)}, bf16[200,512]{1,0:T(8,128)(2,1)S(1)}, u32[]{:S(2)}, u32[]{:S(2)}) collective-permute-start(bf16[200,512]{1,0:T(8,128)(2,1)S(1)} %get-tuple-element.36), channel_id=1, source_target_pairs={{0,3},{1,2},{2,1},{3,0},{4,7},{5,6},{6,5},{7,4},{8,11},{9,10},{10,... | collective-permute-start | bytes 614408 | tf_op jit(solution)/shard_map/ppermute | solution.py:276
  61.5 7.3 %collective-permute-start.12 = (bf16[200,512]{1,0:T(8,128)(2,1)S(1)}, bf16[200,512]{1,0:T(8,128)(2,1)S(1)}, u32[]{:S(2)}, u32[]{:S(2)}) collective-permute-start(bf16[200,512]{1,0:T(8,128)(2,1)S(1)} %get-tuple-element.38), channel_id=1, source_target_pairs={{0,1},{1,0},{2,3},{3,2},{4,5},{5,4},{6,7},{7,6},{8,9},{9,8},{10,11... | collective-permute-start | bytes 614408 | tf_op jit(solution)/shard_map/ppermute | solution.py:276
  61.7 12.1 %collective-permute-start.13 = (bf16[200,512]{1,0:T(8,128)(2,1)S(1)}, bf16[200,512]{1,0:T(8,128)(2,1)S(1)}, u32[]{:S(2)}, u32[]{:S(2)}) collective-permute-start(bf16[200,512]{1,0:T(8,128)(2,1)S(1)} %get-tuple-element.39), channel_id=1, source_target_pairs={{0,14},{1,15},{2,12},{3,13},{4,10},{5,11},{6,8},{7,9},{8,6},{9,7},... | collective-permute-start | bytes 614408 | tf_op jit(solution)/shard_map/ppermute | solution.py:276
  66.2 9.8 %collective-permute-start.14 = (bf16[200,512]{1,0:T(8,128)(2,1)S(1)}, bf16[200,512]{1,0:T(8,128)(2,1)S(1)}, u32[]{:S(2)}, u32[]{:S(2)}) collective-permute-start(bf16[200,512]{1,0:T(8,128)(2,1)S(1)} %get-tuple-element.40), channel_id=1, source_target_pairs={{0,15},{1,14},{2,13},{3,12},{4,11},{5,10},{6,9},{7,8},{8,7},{9,6},... | collective-permute-start | bytes 614408 | tf_op jit(solution)/shard_map/ppermute | solution.py:276
  73.8 20.9 %copy-start.3 = (s32[1,2048]{1,0:T(1,128)S(1)}, s32[1,2048]{1,0:T(1,128)}, u32[]{:S(2)}) copy-start(s32[1,2048]{1,0:T(1,128)} %get-tuple-element.25.slot_ref) | copy-start | bytes 24580

commit v3 on v2

v3 whole, which is shorter than its diff:
```python
import functools

import jax
import jax.numpy as jnp
from jax import lax
from jax.experimental import pallas as pl
from jax.experimental.pallas import tpu as pltpu
from jax.sharding import PartitionSpec as P

EPSILON = 1e-06
EMPTY = float(1 << 25)
DEVICE = ("dp", "split")
LANES = 128
GROUPS = 8
ORDER = (8, 9, 6, 7, 10, 11, 4, 5, 12, 13, 2, 3, 0, 1, 14, 15)
STAGES = (2, 2, 3, 1)
LIMBS = 4
KEY_ROWS = 2 * LIMBS
VMEM_LIMIT = 24 * 1024 * 1024
FIRST_VMEM_LIMIT = 60 * 1024 * 1024

in_vmem = pl.BlockSpec(memory_space=pltpu.VMEM)
in_smem = pl.BlockSpec(memory_space=pltpu.SMEM)
in_hbm = pl.BlockSpec(memory_space=pltpu.HBM)


def params():
    return pltpu.CompilerParams(vmem_limit_bytes=VMEM_LIMIT)


NO_COST = pl.CostEstimate(flops=0, bytes_accessed=0, transcendentals=0)


def one_hot(slot, first, count):
    shape = (count, slot.shape[1])
    return (lax.broadcasted_iota(jnp.int32, shape, 0) == slot - first).astype(jnp.float32).astype(jnp.bfloat16)


def slots_of(cluster, device, clusters, most):
    span = 256
    upper = (
        lax.broadcasted_iota(jnp.int32, (span, span), 0) <= lax.broadcasted_iota(jnp.int32, (span, span), 1)
    ).astype(jnp.float32).astype(jnp.bfloat16)
    carry = jnp.zeros((clusters, 1), jnp.float32)
    ranks = []
    for at in range(0, cluster.shape[1], span):
        hot = cluster[:, at : at + span] == lax.broadcasted_iota(jnp.int32, (clusters, span), 0)
        local = jnp.dot(hot.astype(jnp.float32).astype(jnp.bfloat16), upper, preferred_element_type=jnp.float32)
        ranks.append(jnp.sum(jnp.where(hot, local + carry, 0.0), axis=0, keepdims=True))
        carry = carry + local[:, span - 1 :]
    return (cluster ^ device) * most + jnp.concatenate(ranks, axis=1).astype(jnp.int32) - 1


def key_limbs(order):
    which = lax.broadcasted_iota(jnp.int32, (KEY_ROWS, order.shape[1]), 0)
    limbs = jnp.where(which == 0, order & 255, jnp.where(which == 1, (order >> 8) & 255, (order >> 16) & 255))
    limbs = jnp.where(which < 3, limbs, jnp.where(which == 3, 1, 0))
    return limbs.astype(jnp.float32).astype(jnp.bfloat16)


def pack_unit(slot, limbs, emb, first, blocks, most):
    unit = len(blocks)
    chosen = one_hot(slot, first * most, unit * most)
    rows = jnp.dot(chosen, emb, preferred_element_type=jnp.float32)
    scale = lax.rsqrt(jnp.sum(rows * rows, axis=1, keepdims=True) + EPSILON)
    rows = (rows * scale).astype(jnp.bfloat16)
    keys = lax.dot_general(limbs, chosen, (((1,), (1,)), ((), ())), preferred_element_type=jnp.float32)
    lane = lax.broadcasted_iota(jnp.int32, keys.shape, 1)
    for i, block in enumerate(blocks):
        for chunk in range(emb.shape[1] // LANES):
            block[chunk * most : (chunk + 1) * most] = rows[i * most : (i + 1) * most, chunk * LANES : (chunk + 1) * LANES]
        mine = jnp.where((lane >= i * most) & (lane < (i + 1) * most), keys, 0.0)
        at = i * most // LANES * LANES
        held = [mine[:LIMBS, c : c + LANES] for c in (at, at + LANES) if c < keys.shape[1]]
        held += [jnp.zeros((LIMBS, LANES), jnp.float32)] * (2 - len(held))
        block[emb.shape[1] // LANES * most :] = jnp.concatenate(held, axis=0).astype(jnp.bfloat16)


def unit_keys(blocks, most):
    width = len(blocks) * most
    chunks = [jnp.zeros((LIMBS, LANES), jnp.float32) for _ in range(width // LANES)]
    for i, block in enumerate(blocks):
        held = block[block.shape[0] - KEY_ROWS :].astype(jnp.float32)
        for half in range(2):
            chunk = i * most // LANES + half
            if chunk < len(chunks):
                chunks[chunk] += held[half * LIMBS : (half + 1) * LIMBS]
    sums = jnp.concatenate(chunks, axis=1)
    return sums[0:1] + 256.0 * sums[1:2] + 65536.0 * sums[2:3] + EMPTY * (1.0 - sums[3:4])


def first_pack_kernel(me_ref, cluster_hbm, order_hbm, emb_hbm, *refs, clusters, most, first):
    *blocks, slot_ref, limbs_ref, cluster_ref, order_ref, emb_ref, sems = refs
    load_cluster = pltpu.make_async_copy(cluster_hbm, cluster_ref, sems.at[0])
    load_order = pltpu.make_async_copy(order_hbm, order_ref, sems.at[1])
    load_emb = pltpu.make_async_copy(emb_hbm, emb_ref, sems.at[2])
    load_cluster.start()
    load_order.start()
    load_emb.start()
    load_cluster.wait()
    slot = slots_of(cluster_ref[...], me_ref[0], clusters, most)
    slot_ref[...] = slot
    load_order.wait()
    limbs = key_limbs(order_ref[...])
    limbs_ref[...] = limbs
    load_emb.wait()
    pack_unit(slot, limbs, emb_ref[...], first, blocks, most)


def first_pack(me, cluster, order, embeddings, clusters, most, first, unit, block):
    rows_dev, width = embeddings.shape
    *blocks, slot, limbs = pl.pallas_call(
        functools.partial(first_pack_kernel, clusters=clusters, most=most, first=first),
        in_specs=[in_smem, in_hbm, in_hbm, in_hbm],
        out_specs=[in_vmem] * (unit + 2),
        out_shape=[block] * unit
        + [jax.ShapeDtypeStruct((1, rows_dev), jnp.int32), jax.ShapeDtypeStruct((KEY_ROWS, rows_dev), jnp.bfloat16)],
        scratch_shapes=[
            pltpu.VMEM((1, rows_dev), jnp.int32),
            pltpu.VMEM((1, rows_dev), jnp.int32),
            pltpu.VMEM((rows_dev, width), jnp.bfloat16),
            pltpu.SemaphoreType.DMA((3,)),
        ],
        compiler_params=pltpu.CompilerParams(vmem_limit_bytes=FIRST_VMEM_LIMIT),
        cost_estimate=NO_COST,
        name="first_pack",
    )(me, cluster, order, embeddings)
    return blocks, slot, limbs


def pack_kernel(slot_ref, limbs_ref, emb_hbm, *refs, firsts, unit, most):
    *blocks, emb_ref, sem = refs
    load_emb = pltpu.make_async_copy(emb_hbm, emb_ref, sem)
    load_emb.start()
    load_emb.wait()
    for i, first in enumerate(firsts):
        pack_unit(slot_ref[...], limbs_ref[...], emb_ref[...], first, blocks[i * unit : (i + 1) * unit], most)


def pack(slot, limbs, embeddings, most, firsts, unit, block):
    rows_dev, width = embeddings.shape
    count = len(firsts) * unit
    return pl.pallas_call(
        functools.partial(pack_kernel, firsts=firsts, unit=unit, most=most),
        in_specs=[in_vmem, in_vmem, in_hbm],
        out_specs=[in_vmem] * count,
        out_shape=[block] * count,
        scratch_shapes=[pltpu.VMEM((rows_dev, width), jnp.bfloat16), pltpu.SemaphoreType.DMA],
        compiler_params=params(),
        cost_estimate=NO_COST,
        name="pack",
    )(slot, limbs, embeddings)


def fold_rows(partial):
    return jnp.concatenate(
        [jnp.max(partial[at : at + LANES].T, axis=0, keepdims=True) for at in range(0, partial.shape[0], LANES)], axis=1
    )


def stage_kernel(me_ref, *refs, olds, fresh, unit, most, arrival):
    refs = list(refs)
    state_ref = refs.pop(0) if olds else None
    old_rows = [refs.pop(0) for _ in olds]
    sources = [refs.pop(0) for _ in range(fresh)]
    if arrival:
        out_ref, rows, state, own_keys, row_best = refs
    else:
        state, rows, own_keys, row_best = refs
    before, count = sum(olds), fresh * most
    chunk = next(c for c in (384, 256, 128) if count % c == 0)
    for i, source in enumerate(sources):
        for piece in range(rows.shape[1] // LANES):
            lanes = slice(piece * LANES, (piece + 1) * LANES)
            rows[i * most : (i + 1) * most, lanes] = source[piece * most : (piece + 1) * most]
    if olds:
        state[:, :before] = state_ref[...]
    state[0:1, before:] = jnp.full((1, count), -1.0, jnp.float32)
    for i in range(0, fresh, unit):
        at = before + i * most
        state[1:2, at : at + unit * most] = unit_keys(sources[i : i + unit], most)
    for at in range(0, count, LANES):
        own_keys[at : at + LANES] = jnp.broadcast_to(state[1:2, before + at : before + at + LANES], (LANES, LANES)).T

    for base in range(0, count, chunk):
        own_rows = rows[base : base + chunk]
        own = own_keys[base : base + chunk]
        best = jnp.full((chunk, LANES), -1.0, jnp.float32)
        start = 0
        for others in [*old_rows, rows]:
            height = others.shape[0]
            tile = next(t for t in (1152, 768, 512, 384, 256, 128) if height % t == 0)
            for at in range(0, height, tile):
                sim = lax.dot_general(
                    own_rows, others[at : at + tile], (((1,), (1,)), ((), ())), preferred_element_type=jnp.float32
                )
                for lane in range(0, tile, LANES):
                    here = slice(start + at + lane, start + at + lane + LANES)
                    part = sim[:, lane : lane + LANES]
                    earlier = state[1:2, here] < own
                    best = jnp.maximum(best, jnp.where(earlier, part, -1.0))
                    if start < before:
                        later = jnp.max(jnp.where(earlier, -1.0, part), axis=0, keepdims=True)
                        state[0:1, here] = jnp.maximum(state[0:1, here], later)
            start += height
        row_best[base : base + chunk] = best
    state[0:1, before:] = fold_rows(row_best[...])

    if arrival:
        total = before + count
        shifts = {}
        for place, block in enumerate(arrival):
            shift = place * most % LANES
            if shift not in shifts:
                shifts[shift] = pltpu.roll(state[0:1], total - shift, 1) if shift else state[0:1]
            at = place * most - shift
            out_ref[block ^ me_ref[0]] = shifts[shift][:, at : at + most]


def stage(me, state, old_rows, sources, unit, most, width, arrival):
    olds = [rows.shape[0] for rows in old_rows]
    count = len(sources) * most
    total = sum(olds) + count
    state_shape, rows_shape = (2, total), (count, width)
    operands = [me] + ([state] if olds else []) + old_rows + sources
    work = [pltpu.VMEM((count, LANES), jnp.float32), pltpu.VMEM((count, LANES), jnp.float32)]
    if arrival:
        out_shape = jax.ShapeDtypeStruct((len(arrival), 1, most), jnp.float32)
        work = [pltpu.VMEM(rows_shape, jnp.bfloat16), pltpu.VMEM(state_shape, jnp.float32)] + work
    else:
        out_shape = [jax.ShapeDtypeStruct(state_shape, jnp.float32), jax.ShapeDtypeStruct(rows_shape, jnp.bfloat16)]
    return pl.pallas_call(
        functools.partial(
            stage_kernel, olds=olds, fresh=len(sources), unit=unit, most=most, arrival=arrival
        ),
        in_specs=[in_smem] + [in_vmem] * (len(operands) - 1),
        out_specs=in_vmem if arrival else [in_vmem, in_vmem],
        out_shape=out_shape,
        scratch_shapes=work,
        compiler_params=params(),
        cost_estimate=NO_COST,
        name=f"stage_{len(olds)}",
    )(*operands)


def lookup_kernel(me_ref, table_ref, slot_ref, out_ref):
    clusters, _, most = table_ref.shape
    rows_dev = slot_ref.shape[1]
    table = table_ref[...].reshape(clusters, most)
    high = table.astype(jnp.bfloat16)
    rest = table - high.astype(jnp.float32)
    middle = rest.astype(jnp.bfloat16)
    low = (rest - middle.astype(jnp.float32)).astype(jnp.bfloat16)
    limbs = jnp.concatenate([high, middle, low], axis=0)
    slot = slot_ref[...]
    shape = (clusters, rows_dev)
    place = lax.broadcasted_iota(jnp.int32, shape, 0)
    start = (place ^ me_ref[0]) * most
    mine = (slot >= start) & (slot < start + most)
    within = jnp.sum(jnp.where(mine, slot - start, 0), axis=0, keepdims=True)
    found = jnp.dot(limbs, one_hot(within, 0, most), preferred_element_type=jnp.float32)
    value = found[:clusters] + found[clusters : 2 * clusters] + found[2 * clusters :]
    out_ref[...] = jnp.sum(jnp.where(mine, value, 0.0), axis=0, keepdims=True)


def lookup(me, table, slot):
    return pl.pallas_call(
        lookup_kernel,
        in_specs=[in_smem, in_vmem, in_vmem],
        out_specs=in_vmem,
        out_shape=jax.ShapeDtypeStruct(slot.shape, jnp.float32),
        compiler_params=params(),
        name="lookup",
    )(me, table, slot)


def per_device(embeddings, assignment, order_key):
    rows_dev, width = embeddings.shape
    clusters = lax.axis_size("dp") * lax.axis_size("split")
    most = 3 * rows_dev // (2 * clusters)
    unit, half = clusters // GROUPS, clusters // 2
    me = lax.axis_index("dp") * lax.axis_size("split") + lax.axis_index("split")
    scalar = me.reshape(1).astype(jnp.int32)

    def send(block, offset):
        return lax.ppermute(block, DEVICE, [(i, i ^ offset) for i in range(clusters)])

    cluster = assignment.reshape(1, rows_dev)
    order = order_key.reshape(1, rows_dev)
    groups = [list(range(g * unit, (g + 1) * unit)) for g in range(GROUPS)]
    first = GROUPS // 2
    packed = [*range(first + 1, GROUPS), *range(first)]
    block = jax.ShapeDtypeStruct((width // LANES * most + KEY_ROWS, LANES), jnp.bfloat16)
    head, slot, limbs = first_pack(scalar, cluster, order, embeddings, clusters, most, half, unit, block)
    tail = pack(slot, limbs, embeddings, most, [g * unit for g in packed], unit, block)
    rows = dict(zip([o for g in [first, *packed] for o in groups[g]], [*head, *tail], strict=True))
    got = {0: rows[0]}
    for offset in [*range(half, clusters), *range(half - 1, 0, -1)]:
        got[offset] = send(rows[offset], offset)

    part = unit // 2
    arrival = [h * part + i for h in ORDER for i in range(part)]
    state, done, old_rows = None, 0, []
    for fresh in STAGES:
        sources = [got[o] for o in arrival[done * unit : (done + fresh) * unit]]
        done += fresh
        last = done == GROUPS
        state = stage(scalar, state, old_rows, sources, unit, most, width, arrival if last else None)
        if not last:
            state, fresh_rows = state
            old_rows.append(fresh_rows)
    best = state
    returned = lax.all_to_all(best, DEVICE, split_axis=0, concat_axis=0, tiled=True)
    return lookup(scalar, returned, slot).reshape(rows_dev)


def solution(mesh):
    placed = (
        P(("groups", "dp", "split"), None),
        P(("groups", "dp", "split"), None),
        P(("groups", "dp", "split")),
    )
    return jax.shard_map(
        per_device,
        mesh=mesh,
        in_specs=placed,
        out_specs=P(("groups", "dp", "split")),
        check_vma=False,
    )
```

time: 95.9 us -> 93.8 us (0.978)
  transfers between devices with their start and end apart: 15 -> 15, of which waited for: 6 -> 6; matrix products, arithmetic and copies ran while one was open for 0% -> 0% of each run, Pallas kernels for 17% -> 16%
where the time goes in v3:
time: 93.8 us; the launch traced here: 93.6 us
  waiting for transfers between devices  30.5 us (33%)
  starting transfers between devices  22.9 us (24%)
  Pallas kernels  22.1 us (24%)
  blocking collectives  16.5 us (18%)
  local copies, waits for them, and re-layouts  1.46 us (2%)
    ppermute x15, waiting for transfers between devices, send(): lax.ppermute(block, DEVICE, [(i, i ^ offset) for i in range(clusters)])  30.5 us
    ppermute x15, starting transfers between devices, send(): lax.ppermute(block, DEVICE, [(i, i ^ offset) for i in range(clusters)])  22.9 us
    all_to_all x1, blocking collectives, per_device(): lax.all_to_all(best, DEVICE, split_axis=0, concat_axis=0, tiled=True)  16.5 us
    pallas_call x1, Pallas kernels, pack(): pl.pallas_call(functools.partial(pack_kernel, firsts=firsts, unit=unit, m...  8.79 us
    pallas_call x4, Pallas kernels, stage(): pl.pallas_call(functools.partial(stage_kernel, olds=olds, fresh=len(sourc...  8.35 us
    pallas_call x1, Pallas kernels, first_pack(): pl.pallas_call(functools.partial(first_pack_kernel, clusters=clusters, mo...  3.91 us
  transfers between devices with their start and end apart: 15, of which 6 were waited for; matrix products, arithmetic and copies ran while one was open for 0% of the time, Pallas kernels for 16%

profile of v3, /device:TPU:0, one launch (start us, length us, event | category | flops | bytes accessed | tf_op | source)
XLA Modules:
  0.0 93.6 jit_solution(10438711884479586640)
XLA Ops:
  0.0 3.9 %first_pack.1 = (bf16[776,128]{1,0:T(8,128)(2,1)}, bf16[776,128]{1,0:T(8,128)(2,1)}, s32[1,2048]{1,0:T(1,128)}, bf16[8,2048]{1,0:T(8,128)(2,1)}) custom-call(s32[1]{0:T(128)} %bitcast.me_ref, s32[1,2048]{1,0:T(1,128)} %bitcast.4, s32[1,2048]{1,0:T(1,128)} %bitcast.5, bf16[2048,512]{1,0:T(8,128)(2,1)} %emb_hbm.3), custom_call_target="tpu_custom_call" | custom-call | tf_op jit(solution)/shard_map/first_pack/pallas_call | solution.py:112
  3.9 4.1 %collective-permute-start = (bf16[776,128]{1,0:T(8,128)(2,1)}, bf16[776,128]{1,0:T(8,128)(2,1)S(1)}, u32[]{:S(2)}, u32[]{:S(2)}) collective-permute-start(bf16[776,128]{1,0:T(8,128)(2,1)} %get-tuple-element.29), channel_id=1, source_target_pairs={{0,8},{1,9},{2,10},{3,11},{4,12},{5,13},{6,14},{7,15},{8,0},{9,1},... | collective-permute-start | bytes 595976 | tf_op jit(solution)/shard_map/ppermute | solution.py:286
  8.0 0.8 copy-done.1
  8.8 0.7 copy-done.2
  9.5 8.8 %pack.1 = (bf16[776,128]{1,0:T(8,128)(2,1)S(1)}, bf16[776,128]{1,0:T(8,128)(2,1)S(1)}, bf16[776,128]{1,0:T(8,128)(2,1)S(1)}, bf16[776,128]{1,0:T(8,128)(2,1)S(1)...) custom-call(s32[1,2048]{1,0:T(1,128)S(1)} %copy-done.2, ...), custom_call_target="tpu_custom_call" | custom-call | tf_op jit(solution)/shard_map/pack/pallas_call | solution.py:143
  18.3 2.6 %collective-permute-start.2 = (bf16[776,128]{1,0:T(8,128)(2,1)S(1)}, bf16[776,128]{1,0:T(8,128)(2,1)S(1)}, u32[]{:S(2)}, u32[]{:S(2)}) collective-permute-start(bf16[776,128]{1,0:T(8,128)(2,1)S(1)} %get-tuple-element.33), channel_id=1, source_target_pairs={{0,6},{1,7},{2,4},{3,5},{4,2},{5,3},{6,0},{7,1},{8,14},{9,15},{10,... | collective-permute-start | bytes 595976 | tf_op jit(solution)/shard_map/ppermute | solution.py:286
  21.0 3.6 %collective-permute-start.4 = (bf16[776,128]{1,0:T(8,128)(2,1)S(1)}, bf16[776,128]{1,0:T(8,128)(2,1)S(1)}, u32[]{:S(2)}, u32[]{:S(2)}) collective-permute-start(bf16[776,128]{1,0:T(8,128)(2,1)S(1)} %get-tuple-element.37), channel_id=1, source_target_pairs={{0,10},{1,11},{2,8},{3,9},{4,14},{5,15},{6,12},{7,13},{8,2},{9,3},... | collective-permute-start | bytes 595976 | tf_op jit(solution)/shard_map/ppermute | solution.py:286
  25.2 1.7 %collective-permute-start.6 = (bf16[776,128]{1,0:T(8,128)(2,1)S(1)}, bf16[776,128]{1,0:T(8,128)(2,1)S(1)}, u32[]{:S(2)}, u32[]{:S(2)}) collective-permute-start(bf16[776,128]{1,0:T(8,128)(2,1)S(1)} %get-tuple-element.39), channel_id=1, source_target_pairs={{0,4},{1,5},{2,6},{3,7},{4,0},{5,1},{6,2},{7,3},{8,12},{9,13},{10,... | collective-permute-start | bytes 595976 | tf_op jit(solution)/shard_map/ppermute | solution.py:286
  26.9 10.3 %collective-permute-done.2.refs_2_ = bf16[776,128]{1,0:T(8,128)(2,1)S(1)} collective-permute-done((bf16[776,128]{1,0:T(8,128)(2,1)S(1)}, bf16[776,128]{1,0:T(8,128)(2,1)S(1)}, u32[]{:S(2)}, u32[]{:S(2)}) %collective-permute-start.2) | collective-permute-done | bytes 198688 | tf_op jit(solution)/shard_map/ppermute | solution.py:286
  37.2 4.1 %collective-permute-done.3.refs_3_ = bf16[776,128]{1,0:T(8,128)(2,1)S(1)} collective-permute-done((bf16[776,128]{1,0:T(8,128)(2,1)S(1)}, bf16[776,128]{1,0:T(8,128)(2,1)S(1)}, u32[]{:S(2)}, u32[]{:S(2)}) %collective-permute-start.3) | collective-permute-done | bytes 198688 | tf_op jit(solution)/shard_map/ppermute | solution.py:286
  41.3 1.8 %collective-permute-start.8 = (bf16[776,128]{1,0:T(8,128)(2,1)S(1)}, bf16[776,128]{1,0:T(8,128)(2,1)S(1)}, u32[]{:S(2)}, u32[]{:S(2)}) collective-permute-start(bf16[776,128]{1,0:T(8,128)(2,1)S(1)} %get-tuple-element.43), channel_id=1, source_target_pairs={{0,12},{1,13},{2,14},{3,15},{4,8},{5,9},{6,10},{7,11},{8,4},{9,5},... | collective-permute-start | bytes 595976 | tf_op jit(solution)/shard_map/ppermute | solution.py:286
  43.1 1.6 %collective-permute-start.9 = (bf16[776,128]{1,0:T(8,128)(2,1)S(1)}, bf16[776,128]{1,0:T(8,128)(2,1)S(1)}, u32[]{:S(2)}, u32[]{:S(2)}) collective-permute-start(bf16[776,128]{1,0:T(8,128)(2,1)S(1)} %get-tuple-element.44), channel_id=1, source_target_pairs={{0,13},{1,12},{2,15},{3,14},{4,9},{5,8},{6,11},{7,10},{8,5},{9,4},... | collective-permute-start | bytes 595976 | tf_op jit(solution)/shard_map/ppermute | solution.py:286
  44.7 1.5 %collective-permute-start.10 = (bf16[776,128]{1,0:T(8,128)(2,1)S(1)}, bf16[776,128]{1,0:T(8,128)(2,1)S(1)}, u32[]{:S(2)}, u32[]{:S(2)}) collective-permute-start(bf16[776,128]{1,0:T(8,128)(2,1)S(1)} %get-tuple-element.45), channel_id=1, source_target_pairs={{0,2},{1,3},{2,0},{3,1},{4,6},{5,7},{6,4},{7,5},{8,10},{9,11},{10,... | collective-permute-start | bytes 595976 | tf_op jit(solution)/shard_map/ppermute | solution.py:286
  46.2 1.0 %collective-permute-done.6.refs_4_ = bf16[776,128]{1,0:T(8,128)(2,1)S(1)} collective-permute-done((bf16[776,128]{1,0:T(8,128)(2,1)S(1)}, bf16[776,128]{1,0:T(8,128)(2,1)S(1)}, u32[]{:S(2)}, u32[]{:S(2)}) %collective-permute-start.6) | collective-permute-done | bytes 198688 | tf_op jit(solution)/shard_map/ppermute | solution.py:286
  47.3 1.2 %collective-permute-start.11 = (bf16[776,128]{1,0:T(8,128)(2,1)S(1)}, bf16[776,128]{1,0:T(8,128)(2,1)S(1)}, u32[]{:S(2)}, u32[]{:S(2)}) collective-permute-start(bf16[776,128]{1,0:T(8,128)(2,1)S(1)} %get-tuple-element.46), channel_id=1, source_target_pairs={{0,3},{1,2},{2,1},{3,0},{4,7},{5,6},{6,5},{7,4},{8,11},{9,10},{10,... | collective-permute-start | bytes 595976 | tf_op jit(solution)/shard_map/ppermute | solution.py:286
  48.5 11.5 %collective-permute-done.7.refs_5_ = bf16[776,128]{1,0:T(8,128)(2,1)S(1)} collective-permute-done((bf16[776,128]{1,0:T(8,128)(2,1)S(1)}, bf16[776,128]{1,0:T(8,128)(2,1)S(1)}, u32[]{:S(2)}, u32[]{:S(2)}) %collective-permute-start.7) | collective-permute-done | bytes 198688 | tf_op jit(solution)/shard_map/ppermute | solution.py:286
  60.1 4.5 %collective-permute-start.13 = (bf16[776,128]{1,0:T(8,128)(2,1)S(1)}, bf16[776,128]{1,0:T(8,128)(2,1)S(1)}, u32[]{:S(2)}, u32[]{:S(2)}) collective-permute-start(bf16[776,128]{1,0:T(8,128)(2,1)S(1)} %get-tuple-element.51), channel_id=1, source_target_pairs={{0,14},{1,15},{2,12},{3,13},{4,10},{5,11},{6,8},{7,9},{8,6},{9,7},... | collective-permute-start | bytes 595976 | tf_op jit(solution)/shard_map/ppermute | solution.py:286
  64.7 0.9 %stage_0.1 = (f32[2,768]{1,0:T(2,128)S(1)}, bf16[768,512]{1,0:T(8,128)(2,1)S(1)}) custom-call(s32[1]{0:T(128)} %bitcast.me_ref, bf16[776,128]{1,0:T(8,128)(2,1)S(1)} %collective-permute-done.refs_0_, bf16[776,128]{1,0:T(8,128)(2,1)S(1)} %collective-permute-done.1.refs_1_, bf16[776,128]{1,0:T(8,128)(2,1)S(1)} %collective-permute-done.2.refs_2_, ...), custom_call_target="tpu_custom_call" | custom-call | tf_op jit(solution)/shard_map/stage_0/pallas_call | solution.py:232
  65.6 1.6 %stage_1.1 = (f32[2,1536]{1,0:T(2,128)S(1)}, bf16[768,512]{1,0:T(8,128)(2,1)S(1)}) custom-call(s32[1]{0:T(128)} %bitcast.me_ref, f32[2,768]{1,0:T(2,128)S(1)} %get-tuple-element.35.refs_0_, bf16[768,512]{1,0:T(8,128)(2,1)S(1)} %get-tuple-element.36.refs_1_, bf16[776,128]{1,0:T(8,128)(2,1)S(1)} %collective-permute-done.4.refs_2_, ...), custom_call_target="tpu_custom_call" | custom-call | tf_op jit(solution)/shard_map/stage_1/pallas_call | solution.py:232
  67.2 4.0 %stage_2.1 = (f32[2,2688]{1,0:T(2,128)S(1)}, bf16[1152,512]{1,0:T(8,128)(2,1)S(1)}) custom-call(s32[1]{0:T(128)} %bitcast.me_ref, f32[2,1536]{1,0:T(2,128)S(1)} %get-tuple-element.41.refs_0_, bf16[768,512]{1,0:T(8,128)(2,1)S(1)} %get-tuple-element.36.refs_1_, bf16[768,512]{1,0:T(8,128)(2,1)S(1)} %get-tuple-element.42.refs_2_, ...), custom_call_target="tpu_custom_call" | custom-call | tf_op jit(solution)/shard_map/stage_2/pallas_call | solution.py:232
  71.3 2.9 %collective-permute-done.14.refs_5_ = bf16[776,128]{1,0:T(8,128)(2,1)S(1)} collective-permute-done((bf16[776,128]{1,0:T(8,128)(2,1)S(1)}, bf16[776,128]{1,0:T(8,128)(2,1)S(1)}, u32[]{:S(2)}, u32[]{:S(2)}) %collective-permute-start.14) | collective-permute-done | bytes 198688 | tf_op jit(solution)/shard_map/ppermute | solution.py:286
  74.2 1.8 %stage_3.1 = f32[16,1,192]{2,1,0:T(1,128)S(1)} custom-call(s32[1]{0:T(128)} %bitcast.me_ref, f32[2,2688]{1,0:T(2,128)S(1)} %get-tuple-element.49.refs_0_, bf16[768,512]{1,0:T(8,128)(2,1)S(1)} %get-tuple-element.36.refs_1_, bf16[768,512]{1,0:T(8,128)(2,1)S(1)} %get-tuple-element.42.refs_2_, bf16[1152,512]{1,0:T(8,128)(2,1)S(1)} %get-tuple-element.50.refs_3_, ...), custom_call_target="tpu_custom_call" | custom-call | tf_op jit(solution)/shard_map/stage_3/pallas_call | solution.py:232
  76.0 16.5 %all_to_all.5.table_ref = f32[16,1,192]{2,1,0:T(1,128)S(1)} all-to-all(f32[16,1,192]{2,1,0:T(1,128)S(1)} %stage_3.1), channel_id=1, replica_groups=mesh['groups'=2,'dp'=8,'split'=2] {'dp','split'}, dimensions={0} | all-to-all | bytes 24576 | tf_op jit(solution)/shard_map/all_to_all | solution.py:313
  92.6 1.0 %lookup.1 = f32[1,2048]{1,0:T(1,128)} custom-call(s32[1]{0:T(128)} %bitcast.me_ref, f32[16,1,192]{2,1,0:T(1,128)S(1)} %all_to_all.5.table_ref, s32[1,2048]{1,0:T(1,128)S(1)} %copy-done.3), custom_call_target="tpu_custom_call" | custom-call | tf_op jit(solution)/shard_map/lookup/pallas_call | solution.py:267
  (22 shorter events, 1.0 us)
Async XLA Ops:
  0.0 8.0 %copy-start = (bf16[2048,512]{1,0:T(8,128)(2,1)S(1)}, bf16[2048,512]{1,0:T(8,128)(2,1)}, u32[]{:S(2)}) copy-start(bf16[2048,512]{1,0:T(8,128)(2,1)} %emb_hbm.3) | copy-start | bytes 6291460
  3.9 20.7 %collective-permute-start = (bf16[776,128]{1,0:T(8,128)(2,1)}, bf16[776,128]{1,0:T(8,128)(2,1)S(1)}, u32[]{:S(2)}, u32[]{:S(2)}) collective-permute-start(bf16[776,128]{1,0:T(8,128)(2,1)} %get-tuple-element.29), channel_id=1, source_target_pairs={{0,8},{1,9},{2,10},{3,11},{4,12},{5,13},{6,14},{7,15},{8,0},{9,1},... | collective-permute-start | bytes 595976 | tf_op jit(solution)/shard_map/ppermute | solution.py:286
  8.0 17.2 %collective-permute-start.1 = (bf16[776,128]{1,0:T(8,128)(2,1)}, bf16[776,128]{1,0:T(8,128)(2,1)S(1)}, u32[]{:S(2)}, u32[]{:S(2)}) collective-permute-start(bf16[776,128]{1,0:T(8,128)(2,1)} %get-tuple-element.30), channel_id=1, source_target_pairs={{0,9},{1,8},{2,11},{3,10},{4,13},{5,12},{6,15},{7,14},{8,1},{9,0},... | collective-permute-start | bytes 595976 | tf_op jit(solution)/shard_map/ppermute | solution.py:286
  8.0 0.8 copy-start.1
  8.8 0.7 copy-start.2
  18.3 18.9 %collective-permute-start.2 = (bf16[776,128]{1,0:T(8,128)(2,1)S(1)}, bf16[776,128]{1,0:T(8,128)(2,1)S(1)}, u32[]{:S(2)}, u32[]{:S(2)}) collective-permute-start(bf16[776,128]{1,0:T(8,128)(2,1)S(1)} %get-tuple-element.33), channel_id=1, source_target_pairs={{0,6},{1,7},{2,4},{3,5},{4,2},{5,3},{6,0},{7,1},{8,14},{9,15},{10,... | collective-permute-start | bytes 595976 | tf_op jit(solution)/shard_map/ppermute | solution.py:286
  20.9 20.5 %collective-permute-start.3 = (bf16[776,128]{1,0:T(8,128)(2,1)S(1)}, bf16[776,128]{1,0:T(8,128)(2,1)S(1)}, u32[]{:S(2)}, u32[]{:S(2)}) collective-permute-start(bf16[776,128]{1,0:T(8,128)(2,1)S(1)} %get-tuple-element.34), channel_id=1, source_target_pairs={{0,7},{1,6},{2,5},{3,4},{4,3},{5,2},{6,1},{7,0},{8,15},{9,14},{10,... | collective-permute-start | bytes 595976 | tf_op jit(solution)/shard_map/ppermute | solution.py:286
  21.0 22.1 %collective-permute-start.4 = (bf16[776,128]{1,0:T(8,128)(2,1)S(1)}, bf16[776,128]{1,0:T(8,128)(2,1)S(1)}, u32[]{:S(2)}, u32[]{:S(2)}) collective-permute-start(bf16[776,128]{1,0:T(8,128)(2,1)S(1)} %get-tuple-element.37), channel_id=1, source_target_pairs={{0,10},{1,11},{2,8},{3,9},{4,14},{5,15},{6,12},{7,13},{8,2},{9,3},... | collective-permute-start | bytes 595976 | tf_op jit(solution)/shard_map/ppermute | solution.py:286
  24.6 20.1 %collective-permute-start.5 = (bf16[776,128]{1,0:T(8,128)(2,1)S(1)}, bf16[776,128]{1,0:T(8,128)(2,1)S(1)}, u32[]{:S(2)}, u32[]{:S(2)}) collective-permute-start(bf16[776,128]{1,0:T(8,128)(2,1)S(1)} %get-tuple-element.38), channel_id=1, source_target_pairs={{0,11},{1,10},{2,9},{3,8},{4,15},{5,14},{6,13},{7,12},{8,3},{9,2},... | collective-permute-start | bytes 595976 | tf_op jit(solution)/shard_map/ppermute | solution.py:286
  25.2 22.1 %collective-permute-start.6 = (bf16[776,128]{1,0:T(8,128)(2,1)S(1)}, bf16[776,128]{1,0:T(8,128)(2,1)S(1)}, u32[]{:S(2)}, u32[]{:S(2)}) collective-permute-start(bf16[776,128]{1,0:T(8,128)(2,1)S(1)} %get-tuple-element.39), channel_id=1, source_target_pairs={{0,4},{1,5},{2,6},{3,7},{4,0},{5,1},{6,2},{7,3},{8,12},{9,13},{10,... | collective-permute-start | bytes 595976 | tf_op jit(solution)/shard_map/ppermute | solution.py:286
  37.2 22.8 %collective-permute-start.7 = (bf16[776,128]{1,0:T(8,128)(2,1)S(1)}, bf16[776,128]{1,0:T(8,128)(2,1)S(1)}, u32[]{:S(2)}, u32[]{:S(2)}) collective-permute-start(bf16[776,128]{1,0:T(8,128)(2,1)S(1)} %get-tuple-element.40), channel_id=1, source_target_pairs={{0,5},{1,4},{2,7},{3,6},{4,1},{5,0},{6,3},{7,2},{8,13},{9,12},{10,... | collective-permute-start | bytes 595976 | tf_op jit(solution)/shard_map/ppermute | solution.py:286
  41.3 18.7 %collective-permute-start.8 = (bf16[776,128]{1,0:T(8,128)(2,1)S(1)}, bf16[776,128]{1,0:T(8,128)(2,1)S(1)}, u32[]{:S(2)}, u32[]{:S(2)}) collective-permute-start(bf16[776,128]{1,0:T(8,128)(2,1)S(1)} %get-tuple-element.43), channel_id=1, source_target_pairs={{0,12},{1,13},{2,14},{3,15},{4,8},{5,9},{6,10},{7,11},{8,4},{9,5},... | collective-permute-start | bytes 595976 | tf_op jit(solution)/shard_map/ppermute | solution.py:286
  43.1 21.5 %collective-permute-start.9 = (bf16[776,128]{1,0:T(8,128)(2,1)S(1)}, bf16[776,128]{1,0:T(8,128)(2,1)S(1)}, u32[]{:S(2)}, u32[]{:S(2)}) collective-permute-start(bf16[776,128]{1,0:T(8,128)(2,1)S(1)} %get-tuple-element.44), channel_id=1, source_target_pairs={{0,13},{1,12},{2,15},{3,14},{4,9},{5,8},{6,11},{7,10},{8,5},{9,4},... | collective-permute-start | bytes 595976 | tf_op jit(solution)/shard_map/ppermute | solution.py:286
  44.7 22.5 %collective-permute-start.10 = (bf16[776,128]{1,0:T(8,128)(2,1)S(1)}, bf16[776,128]{1,0:T(8,128)(2,1)S(1)}, u32[]{:S(2)}, u32[]{:S(2)}) collective-permute-start(bf16[776,128]{1,0:T(8,128)(2,1)S(1)} %get-tuple-element.45), channel_id=1, source_target_pairs={{0,2},{1,3},{2,0},{3,1},{4,6},{5,7},{6,4},{7,5},{8,10},{9,11},{10,... | collective-permute-start | bytes 595976 | tf_op jit(solution)/shard_map/ppermute | solution.py:286
  47.3 19.9 %collective-permute-start.11 = (bf16[776,128]{1,0:T(8,128)(2,1)S(1)}, bf16[776,128]{1,0:T(8,128)(2,1)S(1)}, u32[]{:S(2)}, u32[]{:S(2)}) collective-permute-start(bf16[776,128]{1,0:T(8,128)(2,1)S(1)} %get-tuple-element.46), channel_id=1, source_target_pairs={{0,3},{1,2},{2,1},{3,0},{4,7},{5,6},{6,5},{7,4},{8,11},{9,10},{10,... | collective-permute-start | bytes 595976 | tf_op jit(solution)/shard_map/ppermute | solution.py:286
  60.0 7.3 %collective-permute-start.12 = (bf16[776,128]{1,0:T(8,128)(2,1)S(1)}, bf16[776,128]{1,0:T(8,128)(2,1)S(1)}, u32[]{:S(2)}, u32[]{:S(2)}) collective-permute-start(bf16[776,128]{1,0:T(8,128)(2,1)S(1)} %get-tuple-element.48), channel_id=1, source_target_pairs={{0,1},{1,0},{2,3},{3,2},{4,5},{5,4},{6,7},{7,6},{8,9},{9,8},{10,11... | collective-permute-start | bytes 595976 | tf_op jit(solution)/shard_map/ppermute | solution.py:286
  60.1 11.2 %collective-permute-start.13 = (bf16[776,128]{1,0:T(8,128)(2,1)S(1)}, bf16[776,128]{1,0:T(8,128)(2,1)S(1)}, u32[]{:S(2)}, u32[]{:S(2)}) collective-permute-start(bf16[776,128]{1,0:T(8,128)(2,1)S(1)} %get-tuple-element.51), channel_id=1, source_target_pairs={{0,14},{1,15},{2,12},{3,13},{4,10},{5,11},{6,8},{7,9},{8,6},{9,7},... | collective-permute-start | bytes 595976 | tf_op jit(solution)/shard_map/ppermute | solution.py:286
  64.6 9.6 %collective-permute-start.14 = (bf16[776,128]{1,0:T(8,128)(2,1)S(1)}, bf16[776,128]{1,0:T(8,128)(2,1)S(1)}, u32[]{:S(2)}, u32[]{:S(2)}) collective-permute-start(bf16[776,128]{1,0:T(8,128)(2,1)S(1)} %get-tuple-element.52), channel_id=1, source_target_pairs={{0,15},{1,14},{2,13},{3,12},{4,11},{5,10},{6,9},{7,8},{8,7},{9,6},... | collective-permute-start | bytes 595976 | tf_op jit(solution)/shard_map/ppermute | solution.py:286
  71.3 21.3 %copy-start.3 = (s32[1,2048]{1,0:T(1,128)S(1)}, s32[1,2048]{1,0:T(1,128)}, u32[]{:S(2)}) copy-start(s32[1,2048]{1,0:T(1,128)} %get-tuple-element.31.slot_ref) | copy-start | bytes 24580

commit v4 on v3

--- a/solution.py
+++ b/solution.py
@@ -13,7 +13,7 @@
 LANES = 128
 GROUPS = 8
 ORDER = (8, 9, 6, 7, 10, 11, 4, 5, 12, 13, 2, 3, 0, 1, 14, 15)
-STAGES = (2, 2, 3, 1)
+STAGES = (2, 2, 3)
 LIMBS = 4
 KEY_ROWS = 2 * LIMBS
 VMEM_LIMIT = 24 * 1024 * 1024
@@ -36,7 +36,7 @@
     return (lax.broadcasted_iota(jnp.int32, shape, 0) == slot - first).astype(jnp.float32).astype(jnp.bfloat16)
 
 
-def slots_of(cluster, device, clusters, most):
+def ranks_of(cluster, clusters):
     span = 256
     upper = (
         lax.broadcasted_iota(jnp.int32, (span, span), 0) <= lax.broadcasted_iota(jnp.int32, (span, span), 1)
@@ -48,7 +48,7 @@
         local = jnp.dot(hot.astype(jnp.float32).astype(jnp.bfloat16), upper, preferred_element_type=jnp.float32)
         ranks.append(jnp.sum(jnp.where(hot, local + carry, 0.0), axis=0, keepdims=True))
         carry = carry + local[:, span - 1 :]
-    return (cluster ^ device) * most + jnp.concatenate(ranks, axis=1).astype(jnp.int32) - 1
+    return jnp.concatenate(ranks, axis=1).astype(jnp.int32) - 1
 
 
 def key_limbs(order):
@@ -58,32 +58,33 @@
     return limbs.astype(jnp.float32).astype(jnp.bfloat16)
 
 
-def pack_unit(slot, limbs, emb, first, blocks, most):
-    unit = len(blocks)
+def pack_unit(slot, limbs, emb_ref, first, blocks, most, loaded=lambda: None):
+    unit, pieces = len(blocks), emb_ref.shape[1] // LANES
     chosen = one_hot(slot, first * most, unit * most)
-    rows = jnp.dot(chosen, emb, preferred_element_type=jnp.float32)
+    keys = lax.dot_general(limbs, chosen, (((1,), (1,)), ((), ())), preferred_element_type=jnp.float32)
+    lane = lax.broadcasted_iota(jnp.int32, keys.shape, 1)
+    loaded()
+    rows = jnp.dot(chosen, emb_ref[...], preferred_element_type=jnp.float32)
     scale = lax.rsqrt(jnp.sum(rows * rows, axis=1, keepdims=True) + EPSILON)
     rows = (rows * scale).astype(jnp.bfloat16)
-    keys = lax.dot_general(limbs, chosen, (((1,), (1,)), ((), ())), preferred_element_type=jnp.float32)
-    lane = lax.broadcasted_iota(jnp.int32, keys.shape, 1)
     for i, block in enumerate(blocks):
-        for chunk in range(emb.shape[1] // LANES):
-            block[chunk * most : (chunk + 1) * most] = rows[i * most : (i + 1) * most, chunk * LANES : (chunk + 1) * LANES]
+        for piece in range(pieces):
+            lanes = slice(piece * LANES, (piece + 1) * LANES)
+            block[piece * most : (piece + 1) * most] = rows[i * most : (i + 1) * most, lanes]
         mine = jnp.where((lane >= i * most) & (lane < (i + 1) * most), keys, 0.0)
         at = i * most // LANES * LANES
         held = [mine[:LIMBS, c : c + LANES] for c in (at, at + LANES) if c < keys.shape[1]]
         held += [jnp.zeros((LIMBS, LANES), jnp.float32)] * (2 - len(held))
-        block[emb.shape[1] // LANES * most :] = jnp.concatenate(held, axis=0).astype(jnp.bfloat16)
-
-
-def unit_keys(blocks, most):
-    width = len(blocks) * most
+        block[pieces * most :] = jnp.concatenate(held, axis=0).astype(jnp.bfloat16)
+
+
+def keys_of(blocks, places, most, first, width):
     chunks = [jnp.zeros((LIMBS, LANES), jnp.float32) for _ in range(width // LANES)]
-    for i, block in enumerate(blocks):
+    for block, place in zip(blocks, places, strict=True):
         held = block[block.shape[0] - KEY_ROWS :].astype(jnp.float32)
         for half in range(2):
-            chunk = i * most // LANES + half
-            if chunk < len(chunks):
+            chunk = place * most // LANES + half - first // LANES
+            if 0 <= chunk < len(chunks):
                 chunks[chunk] += held[half * LIMBS : (half + 1) * LIMBS]
     sums = jnp.concatenate(chunks, axis=1)
     return sums[0:1] + 256.0 * sums[1:2] + 65536.0 * sums[2:3] + EMPTY * (1.0 - sums[3:4])
@@ -98,13 +99,15 @@
     load_order.start()
     load_emb.start()
     load_cluster.wait()
-    slot = slots_of(cluster_ref[...], me_ref[0], clusters, most)
-    slot_ref[...] = slot
+    cluster = cluster_ref[...]
+    rank = ranks_of(cluster, clusters)
+    slot = (cluster ^ me_ref[0]) * most + rank
+    slot_ref[0:1] = slot
+    slot_ref[1:2] = rank
     load_order.wait()
     limbs = key_limbs(order_ref[...])
     limbs_ref[...] = limbs
-    load_emb.wait()
-    pack_unit(slot, limbs, emb_ref[...], first, blocks, most)
+    pack_unit(slot, limbs, emb_ref, first, blocks, most, load_emb.wait)
 
 
 def first_pack(me, cluster, order, embeddings, clusters, most, first, unit, block):
@@ -114,7 +117,7 @@
         in_specs=[in_smem, in_hbm, in_hbm, in_hbm],
         out_specs=[in_vmem] * (unit + 2),
         out_shape=[block] * unit
-        + [jax.ShapeDtypeStruct((1, rows_dev), jnp.int32), jax.ShapeDtypeStruct((KEY_ROWS, rows_dev), jnp.bfloat16)],
+        + [jax.ShapeDtypeStruct((2, rows_dev), jnp.int32), jax.ShapeDtypeStruct((KEY_ROWS, rows_dev), jnp.bfloat16)],
         scratch_shapes=[
             pltpu.VMEM((1, rows_dev), jnp.int32),
             pltpu.VMEM((1, rows_dev), jnp.int32),
@@ -129,27 +132,30 @@
 
 
 def pack_kernel(slot_ref, limbs_ref, emb_hbm, *refs, firsts, unit, most):
-    *blocks, emb_ref, sem = refs
+    *blocks, picks_ref, emb_ref, sem = refs
     load_emb = pltpu.make_async_copy(emb_hbm, emb_ref, sem)
     load_emb.start()
     load_emb.wait()
+    slot = slot_ref[0:1]
     for i, first in enumerate(firsts):
-        pack_unit(slot_ref[...], limbs_ref[...], emb_ref[...], first, blocks[i * unit : (i + 1) * unit], most)
+        pack_unit(slot, limbs_ref[...], emb_ref, first, blocks[i * unit : (i + 1) * unit], most)
+    picks_ref[...] = one_hot(slot_ref[1:2], 0, most)
 
 
 def pack(slot, limbs, embeddings, most, firsts, unit, block):
     rows_dev, width = embeddings.shape
     count = len(firsts) * unit
-    return pl.pallas_call(
+    *blocks, picks = pl.pallas_call(
         functools.partial(pack_kernel, firsts=firsts, unit=unit, most=most),
         in_specs=[in_vmem, in_vmem, in_hbm],
-        out_specs=[in_vmem] * count,
-        out_shape=[block] * count,
+        out_specs=[in_vmem] * (count + 1),
+        out_shape=[block] * count + [jax.ShapeDtypeStruct((most, rows_dev), jnp.bfloat16)],
         scratch_shapes=[pltpu.VMEM((rows_dev, width), jnp.bfloat16), pltpu.SemaphoreType.DMA],
         compiler_params=params(),
         cost_estimate=NO_COST,
         name="pack",
     )(slot, limbs, embeddings)
+    return blocks, picks
 
 
 def fold_rows(partial):
@@ -158,27 +164,32 @@
     )
 
 
-def stage_kernel(me_ref, *refs, olds, fresh, unit, most, arrival):
+def stage_kernel(me_ref, *refs, olds, fresh, count, most, arrival):
     refs = list(refs)
     state_ref = refs.pop(0) if olds else None
     old_rows = [refs.pop(0) for _ in olds]
-    sources = [refs.pop(0) for _ in range(fresh)]
+    sources = [refs.pop(0) for _ in range(sum(len(places) for places, _, _ in fresh))]
     if arrival:
         out_ref, rows, state, own_keys, row_best = refs
     else:
         state, rows, own_keys, row_best = refs
-    before, count = sum(olds), fresh * most
+    before = sum(olds)
     chunk = next(c for c in (384, 256, 128) if count % c == 0)
-    for i, source in enumerate(sources):
-        for piece in range(rows.shape[1] // LANES):
-            lanes = slice(piece * LANES, (piece + 1) * LANES)
-            rows[i * most : (i + 1) * most, lanes] = source[piece * most : (piece + 1) * most]
     if olds:
         state[:, :before] = state_ref[...]
     state[0:1, before:] = jnp.full((1, count), -1.0, jnp.float32)
-    for i in range(0, fresh, unit):
-        at = before + i * most
-        state[1:2, at : at + unit * most] = unit_keys(sources[i : i + unit], most)
+    if len(sources) * most < count:
+        rows[...] = jnp.zeros_like(rows)
+    start = 0
+    for places, first, height in fresh:
+        blocks, sources = sources[: len(places)], sources[len(places) :]
+        for block, place in zip(blocks, places, strict=True):
+            at = start + place * most - first
+            for piece in range(rows.shape[1] // LANES):
+                lanes = slice(piece * LANES, (piece + 1) * LANES)
+                rows[at : at + most, lanes] = block[piece * most : (piece + 1) * most]
+        state[1:2, before + start : before + start + height] = keys_of(blocks, places, most, first, height)
+        start += height
     for at in range(0, count, LANES):
         own_keys[at : at + LANES] = jnp.broadcast_to(state[1:2, before + at : before + at + LANES], (LANES, LANES)).T
 
@@ -209,17 +220,16 @@
     if arrival:
         total = before + count
         shifts = {}
-        for place, block in enumerate(arrival):
-            shift = place * most % LANES
+        for block, at in arrival:
+            shift = at % LANES
             if shift not in shifts:
                 shifts[shift] = pltpu.roll(state[0:1], total - shift, 1) if shift else state[0:1]
-            at = place * most - shift
-            out_ref[block ^ me_ref[0]] = shifts[shift][:, at : at + most]
-
-
-def stage(me, state, old_rows, sources, unit, most, width, arrival):
+            out_ref[block ^ me_ref[0]] = shifts[shift][:, at - shift : at - shift + most]
+
+
+def stage(me, state, old_rows, sources, fresh, most, width, arrival):
     olds = [rows.shape[0] for rows in old_rows]
-    count = len(sources) * most
+    count = sum(height for _, _, height in fresh)
     total = sum(olds) + count
     state_shape, rows_shape = (2, total), (count, width)
     operands = [me] + ([state] if olds else []) + old_rows + sources
@@ -231,7 +241,7 @@
         out_shape = [jax.ShapeDtypeStruct(state_shape, jnp.float32), jax.ShapeDtypeStruct(rows_shape, jnp.bfloat16)]
     return pl.pallas_call(
         functools.partial(
-            stage_kernel, olds=olds, fresh=len(sources), unit=unit, most=most, arrival=arrival
+            stage_kernel, olds=olds, fresh=fresh, count=count, most=most, arrival=arrival
         ),
         in_specs=[in_smem] + [in_vmem] * (len(operands) - 1),
         out_specs=in_vmem if arrival else [in_vmem, in_vmem],
@@ -243,35 +253,31 @@
     )(*operands)
 
 
-def lookup_kernel(me_ref, table_ref, slot_ref, out_ref):
+def lookup_kernel(me_ref, table_ref, slot_ref, picks_ref, out_ref):
     clusters, _, most = table_ref.shape
-    rows_dev = slot_ref.shape[1]
     table = table_ref[...].reshape(clusters, most)
     high = table.astype(jnp.bfloat16)
     rest = table - high.astype(jnp.float32)
     middle = rest.astype(jnp.bfloat16)
     low = (rest - middle.astype(jnp.float32)).astype(jnp.bfloat16)
     limbs = jnp.concatenate([high, middle, low], axis=0)
-    slot = slot_ref[...]
-    shape = (clusters, rows_dev)
-    place = lax.broadcasted_iota(jnp.int32, shape, 0)
-    start = (place ^ me_ref[0]) * most
+    found = jnp.dot(limbs, picks_ref[...], preferred_element_type=jnp.float32)
+    value = found[:clusters] + found[clusters : 2 * clusters] + found[2 * clusters :]
+    slot = slot_ref[0:1]
+    start = (lax.broadcasted_iota(jnp.int32, value.shape, 0) ^ me_ref[0]) * most
     mine = (slot >= start) & (slot < start + most)
-    within = jnp.sum(jnp.where(mine, slot - start, 0), axis=0, keepdims=True)
-    found = jnp.dot(limbs, one_hot(within, 0, most), preferred_element_type=jnp.float32)
-    value = found[:clusters] + found[clusters : 2 * clusters] + found[2 * clusters :]
     out_ref[...] = jnp.sum(jnp.where(mine, value, 0.0), axis=0, keepdims=True)
 
 
-def lookup(me, table, slot):
+def lookup(me, table, slot, picks):
     return pl.pallas_call(
         lookup_kernel,
-        in_specs=[in_smem, in_vmem, in_vmem],
+        in_specs=[in_smem, in_vmem, in_vmem, in_vmem],
         out_specs=in_vmem,
-        out_shape=jax.ShapeDtypeStruct(slot.shape, jnp.float32),
+        out_shape=jax.ShapeDtypeStruct((1, slot.shape[1]), jnp.float32),
         compiler_params=params(),
         name="lookup",
-    )(me, table, slot)
+    )(me, table, slot, picks)
 
 
 def per_device(embeddings, assignment, order_key):
@@ -292,26 +298,37 @@
     packed = [*range(first + 1, GROUPS), *range(first)]
     block = jax.ShapeDtypeStruct((width // LANES * most + KEY_ROWS, LANES), jnp.bfloat16)
     head, slot, limbs = first_pack(scalar, cluster, order, embeddings, clusters, most, half, unit, block)
-    tail = pack(slot, limbs, embeddings, most, [g * unit for g in packed], unit, block)
+    tail, picks = pack(slot, limbs, embeddings, most, [g * unit for g in packed], unit, block)
     rows = dict(zip([o for g in [first, *packed] for o in groups[g]], [*head, *tail], strict=True))
     got = {0: rows[0]}
     for offset in [*range(half, clusters), *range(half - 1, 0, -1)]:
         got[offset] = send(rows[offset], offset)
 
     part = unit // 2
-    arrival = [h * part + i for h in ORDER for i in range(part)]
-    state, done, old_rows = None, 0, []
-    for fresh in STAGES:
-        sources = [got[o] for o in arrival[done * unit : (done + fresh) * unit]]
-        done += fresh
-        last = done == GROUPS
-        state = stage(scalar, state, old_rows, sources, unit, most, width, arrival if last else None)
+    order_in = [h * part + i for h in ORDER for i in range(part)]
+    steps = [[(list(range(unit)), 0, unit * most)] * whole for whole in STAGES]
+    for half_unit in range(2):
+        begin, end = half_unit * part * most, (half_unit + 1) * part * most
+        begin = begin // LANES * LANES
+        places = list(range(half_unit * part, (half_unit + 1) * part))
+        steps.append([(places, begin, -(-(end - begin) // LANES) * LANES)])
+    state, taken, filled, old_rows, arrival = None, 0, 0, [], []
+    for fresh in steps:
+        sources = []
+        for places, begin, height in fresh:
+            for place in places:
+                arrival.append((order_in[taken], filled + place * most - begin))
+                sources.append(got[order_in[taken]])
+                taken += 1
+            filled += height
+        last = taken == clusters
+        state = stage(scalar, state, old_rows, sources, fresh, most, width, arrival if last else None)
         if not last:
             state, fresh_rows = state
             old_rows.append(fresh_rows)
     best = state
     returned = lax.all_to_all(best, DEVICE, split_axis=0, concat_axis=0, tiled=True)
-    return lookup(scalar, returned, slot).reshape(rows_dev)
+    return lookup(scalar, returned, slot, picks).reshape(rows_dev)
 
 
 def solution(mesh):

time: 93.8 us -> 93.1 us (level)
  waiting for transfers between devices: 30.5 us -> 29.3 us
  Pallas kernels: 22.1 us -> 23.1 us
    ppermute x15, waiting for transfers between devices: 30.5 us -> 29.3 us  [send(): lax.ppermute(block, DEVICE, [(i, i ^ offset) for i in range(clusters)])]
    pallas_call x5 -> x6, Pallas kernels: 9.36 us -> 9.9 us  [the longest x5 8.99 us: stage(): pl.pallas_call(functools.partial(stage_kernel, olds=olds, fresh=fresh, co...]
  transfers between devices with their start and end apart: 15 -> 15, of which waited for: 6 -> 5; matrix products, arithmetic and copies ran while one was open for 0% -> 0% of each run, Pallas kernels for 16% -> 18%
where the time goes in v4:
time: 93.1 us; the launch traced here: 92.9 us
  waiting for transfers between devices  29.3 us (31%)
  Pallas kernels  23.1 us (25%)
  starting transfers between devices  22.4 us (24%)
  blocking collectives  16.5 us (18%)
  local copies, waits for them, and re-layouts  1.48 us (2%)
    ppermute x15, waiting for transfers between devices, send(): lax.ppermute(block, DEVICE, [(i, i ^ offset) for i in range(clusters)])  29.3 us
    ppermute x15, starting transfers between devices, send(): lax.ppermute(block, DEVICE, [(i, i ^ offset) for i in range(clusters)])  22.4 us
    all_to_all x1, blocking collectives, per_device(): lax.all_to_all(best, DEVICE, split_axis=0, concat_axis=0, tiled=True)  16.5 us
    pallas_call x1, Pallas kernels, pack(): pl.pallas_call(functools.partial(pack_kernel, firsts=firsts, unit=unit, m...  9.43 us
    pallas_call x5, Pallas kernels, stage(): pl.pallas_call(functools.partial(stage_kernel, olds=olds, fresh=fresh, co...  8.99 us
    pallas_call x1, Pallas kernels, first_pack(): pl.pallas_call(functools.partial(first_pack_kernel, clusters=clusters, mo...  3.79 us
  transfers between devices with their start and end apart: 15, of which 5 were waited for; matrix products, arithmetic and copies ran while one was open for 0% of the time, Pallas kernels for 18%

profile of v4, /device:TPU:0, one launch (start us, length us, event | category | flops | bytes accessed | tf_op | source)
XLA Modules:
  0.0 92.9 jit_solution(11463421228068508612)
XLA Ops:
  0.0 3.8 %first_pack.1 = (bf16[776,128]{1,0:T(8,128)(2,1)}, bf16[776,128]{1,0:T(8,128)(2,1)}, s32[2,2048]{1,0:T(2,128)}, bf16[8,2048]{1,0:T(8,128)(2,1)}) custom-call(s32[1]{0:T(128)} %bitcast.me_ref, s32[1,2048]{1,0:T(1,128)} %bitcast.4, s32[1,2048]{1,0:T(1,128)} %bitcast.5, bf16[2048,512]{1,0:T(8,128)(2,1)} %emb_hbm.3), custom_call_target="tpu_custom_call" | custom-call | tf_op jit(solution)/shard_map/first_pack/pallas_call | solution.py:115
  3.8 4.1 %collective-permute-start = (bf16[776,128]{1,0:T(8,128)(2,1)}, bf16[776,128]{1,0:T(8,128)(2,1)S(1)}, u32[]{:S(2)}, u32[]{:S(2)}) collective-permute-start(bf16[776,128]{1,0:T(8,128)(2,1)} %get-tuple-element.32), channel_id=1, source_target_pairs={{0,8},{1,9},{2,10},{3,11},{4,12},{5,13},{6,14},{7,15},{8,0},{9,1},... | collective-permute-start | bytes 595976 | tf_op jit(solution)/shard_map/ppermute | solution.py:292
  8.6 0.8 copy-done.3
  9.4 9.4 %pack.1 = (bf16[776,128]{1,0:T(8,128)(2,1)S(1)}, bf16[776,128]{1,0:T(8,128)(2,1)S(1)}, bf16[776,128]{1,0:T(8,128)(2,1)S(1)}, bf16[776,128]{1,0:T(8,128)(2,1)S(1)...) custom-call(s32[2,2048]{1,0:T(2,128)S(1)} %copy-done.1, ...), custom_call_target="tpu_custom_call" | custom-call | tf_op jit(solution)/shard_map/pack/pallas_call | solution.py:148
  18.8 2.6 %collective-permute-start.2 = (bf16[776,128]{1,0:T(8,128)(2,1)S(1)}, bf16[776,128]{1,0:T(8,128)(2,1)S(1)}, u32[]{:S(2)}, u32[]{:S(2)}) collective-permute-start(bf16[776,128]{1,0:T(8,128)(2,1)S(1)} %get-tuple-element.36), channel_id=1, source_target_pairs={{0,6},{1,7},{2,4},{3,5},{4,2},{5,3},{6,0},{7,1},{8,14},{9,15},{10,... | collective-permute-start | bytes 595976 | tf_op jit(solution)/shard_map/ppermute | solution.py:292
  21.6 3.6 %collective-permute-start.4 = (bf16[776,128]{1,0:T(8,128)(2,1)S(1)}, bf16[776,128]{1,0:T(8,128)(2,1)S(1)}, u32[]{:S(2)}, u32[]{:S(2)}) collective-permute-start(bf16[776,128]{1,0:T(8,128)(2,1)S(1)} %get-tuple-element.40), channel_id=1, source_target_pairs={{0,10},{1,11},{2,8},{3,9},{4,14},{5,15},{6,12},{7,13},{8,2},{9,3},... | collective-permute-start | bytes 595976 | tf_op jit(solution)/shard_map/ppermute | solution.py:292
  25.1 1.7 %collective-permute-start.6 = (bf16[776,128]{1,0:T(8,128)(2,1)S(1)}, bf16[776,128]{1,0:T(8,128)(2,1)S(1)}, u32[]{:S(2)}, u32[]{:S(2)}) collective-permute-start(bf16[776,128]{1,0:T(8,128)(2,1)S(1)} %get-tuple-element.42), channel_id=1, source_target_pairs={{0,4},{1,5},{2,6},{3,7},{4,0},{5,1},{6,2},{7,3},{8,12},{9,13},{10,... | collective-permute-start | bytes 595976 | tf_op jit(solution)/shard_map/ppermute | solution.py:292
  26.8 10.9 %collective-permute-done.2.refs_2_ = bf16[776,128]{1,0:T(8,128)(2,1)S(1)} collective-permute-done((bf16[776,128]{1,0:T(8,128)(2,1)S(1)}, bf16[776,128]{1,0:T(8,128)(2,1)S(1)}, u32[]{:S(2)}, u32[]{:S(2)}) %collective-permute-start.2) | collective-permute-done | bytes 198688 | tf_op jit(solution)/shard_map/ppermute | solution.py:292
  37.7 4.1 %collective-permute-done.3.refs_3_ = bf16[776,128]{1,0:T(8,128)(2,1)S(1)} collective-permute-done((bf16[776,128]{1,0:T(8,128)(2,1)S(1)}, bf16[776,128]{1,0:T(8,128)(2,1)S(1)}, u32[]{:S(2)}, u32[]{:S(2)}) %collective-permute-start.3) | collective-permute-done | bytes 198688 | tf_op jit(solution)/shard_map/ppermute | solution.py:292
  41.9 1.8 %collective-permute-start.8 = (bf16[776,128]{1,0:T(8,128)(2,1)S(1)}, bf16[776,128]{1,0:T(8,128)(2,1)S(1)}, u32[]{:S(2)}, u32[]{:S(2)}) collective-permute-start(bf16[776,128]{1,0:T(8,128)(2,1)S(1)} %get-tuple-element.46), channel_id=1, source_target_pairs={{0,12},{1,13},{2,14},{3,15},{4,8},{5,9},{6,10},{7,11},{8,4},{9,5},... | collective-permute-start | bytes 595976 | tf_op jit(solution)/shard_map/ppermute | solution.py:292
  43.6 1.6 %collective-permute-start.9 = (bf16[776,128]{1,0:T(8,128)(2,1)S(1)}, bf16[776,128]{1,0:T(8,128)(2,1)S(1)}, u32[]{:S(2)}, u32[]{:S(2)}) collective-permute-start(bf16[776,128]{1,0:T(8,128)(2,1)S(1)} %get-tuple-element.47), channel_id=1, source_target_pairs={{0,13},{1,12},{2,15},{3,14},{4,9},{5,8},{6,11},{7,10},{8,5},{9,4},... | collective-permute-start | bytes 595976 | tf_op jit(solution)/shard_map/ppermute | solution.py:292
  45.3 1.0 %collective-permute-start.10 = (bf16[776,128]{1,0:T(8,128)(2,1)S(1)}, bf16[776,128]{1,0:T(8,128)(2,1)S(1)}, u32[]{:S(2)}, u32[]{:S(2)}) collective-permute-start(bf16[776,128]{1,0:T(8,128)(2,1)S(1)} %get-tuple-element.48), channel_id=1, source_target_pairs={{0,2},{1,3},{2,0},{3,1},{4,6},{5,7},{6,4},{7,5},{8,10},{9,11},{10,... | collective-permute-start | bytes 595976 | tf_op jit(solution)/shard_map/ppermute | solution.py:292
  46.3 0.9 collective-permute-done.6.refs_4_
  47.2 1.2 %collective-permute-start.11 = (bf16[776,128]{1,0:T(8,128)(2,1)S(1)}, bf16[776,128]{1,0:T(8,128)(2,1)S(1)}, u32[]{:S(2)}, u32[]{:S(2)}) collective-permute-start(bf16[776,128]{1,0:T(8,128)(2,1)S(1)} %get-tuple-element.49), channel_id=1, source_target_pairs={{0,3},{1,2},{2,1},{3,0},{4,7},{5,6},{6,5},{7,4},{8,11},{9,10},{10,... | collective-permute-start | bytes 595976 | tf_op jit(solution)/shard_map/ppermute | solution.py:292
  48.3 11.5 %collective-permute-done.7.refs_5_ = bf16[776,128]{1,0:T(8,128)(2,1)S(1)} collective-permute-done((bf16[776,128]{1,0:T(8,128)(2,1)S(1)}, bf16[776,128]{1,0:T(8,128)(2,1)S(1)}, u32[]{:S(2)}, u32[]{:S(2)}) %collective-permute-start.7) | collective-permute-done | bytes 198688 | tf_op jit(solution)/shard_map/ppermute | solution.py:292
  60.0 4.5 %collective-permute-start.13 = (bf16[776,128]{1,0:T(8,128)(2,1)S(1)}, bf16[776,128]{1,0:T(8,128)(2,1)S(1)}, u32[]{:S(2)}, u32[]{:S(2)}) collective-permute-start(bf16[776,128]{1,0:T(8,128)(2,1)S(1)} %get-tuple-element.54), channel_id=1, source_target_pairs={{0,14},{1,15},{2,12},{3,13},{4,10},{5,11},{6,8},{7,9},{8,6},{9,7},... | collective-permute-start | bytes 595976 | tf_op jit(solution)/shard_map/ppermute | solution.py:292
  64.6 0.9 %stage_0.1 = (f32[2,768]{1,0:T(2,128)S(1)}, bf16[768,512]{1,0:T(8,128)(2,1)S(1)}) custom-call(s32[1]{0:T(128)} %bitcast.me_ref, bf16[776,128]{1,0:T(8,128)(2,1)S(1)} %collective-permute-done.refs_0_, bf16[776,128]{1,0:T(8,128)(2,1)S(1)} %collective-permute-done.1.refs_1_, bf16[776,128]{1,0:T(8,128)(2,1)S(1)} %collective-permute-done.2.refs_2_, ...), custom_call_target="tpu_custom_call" | custom-call | tf_op jit(solution)/shard_map/stage_0/pallas_call | solution.py:242
  65.5 1.6 %stage_1.1 = (f32[2,1536]{1,0:T(2,128)S(1)}, bf16[768,512]{1,0:T(8,128)(2,1)S(1)}) custom-call(s32[1]{0:T(128)} %bitcast.me_ref, f32[2,768]{1,0:T(2,128)S(1)} %get-tuple-element.38.refs_0_, bf16[768,512]{1,0:T(8,128)(2,1)S(1)} %get-tuple-element.39.refs_1_, bf16[776,128]{1,0:T(8,128)(2,1)S(1)} %collective-permute-done.4.refs_2_, ...), custom_call_target="tpu_custom_call" | custom-call | tf_op jit(solution)/shard_map/stage_1/pallas_call | solution.py:242
  67.1 4.0 %stage_2.1 = (f32[2,2688]{1,0:T(2,128)S(1)}, bf16[1152,512]{1,0:T(8,128)(2,1)S(1)}) custom-call(s32[1]{0:T(128)} %bitcast.me_ref, f32[2,1536]{1,0:T(2,128)S(1)} %get-tuple-element.44.refs_0_, bf16[768,512]{1,0:T(8,128)(2,1)S(1)} %get-tuple-element.39.refs_1_, bf16[768,512]{1,0:T(8,128)(2,1)S(1)} %get-tuple-element.45.refs_2_, ...), custom_call_target="tpu_custom_call" | custom-call | tf_op jit(solution)/shard_map/stage_2/pallas_call | solution.py:242
  71.1 1.2 %stage_3.1 = (f32[2,2944]{1,0:T(2,128)S(1)}, bf16[256,512]{1,0:T(8,128)(2,1)S(1)}) custom-call(s32[1]{0:T(128)} %bitcast.me_ref, f32[2,2688]{1,0:T(2,128)S(1)} %get-tuple-element.52.refs_0_, bf16[768,512]{1,0:T(8,128)(2,1)S(1)} %get-tuple-element.39.refs_1_, bf16[768,512]{1,0:T(8,128)(2,1)S(1)} %get-tuple-element.45.refs_2_, ...), custom_call_target="tpu_custom_call" | custom-call | tf_op jit(solution)/shard_map/stage_3/pallas_call | solution.py:242
  72.3 1.8 %collective-permute-done.14.refs_5_ = bf16[776,128]{1,0:T(8,128)(2,1)S(1)} collective-permute-done((bf16[776,128]{1,0:T(8,128)(2,1)S(1)}, bf16[776,128]{1,0:T(8,128)(2,1)S(1)}, u32[]{:S(2)}, u32[]{:S(2)}) %collective-permute-start.14) | collective-permute-done | bytes 198688 | tf_op jit(solution)/shard_map/ppermute | solution.py:292
  74.1 1.3 %stage_4.1 = f32[16,1,192]{2,1,0:T(1,128)S(1)} custom-call(s32[1]{0:T(128)} %bitcast.me_ref, f32[2,2944]{1,0:T(2,128)S(1)} %get-tuple-element.55.refs_0_, bf16[768,512]{1,0:T(8,128)(2,1)S(1)} %get-tuple-element.39.refs_1_, bf16[768,512]{1,0:T(8,128)(2,1)S(1)} %get-tuple-element.45.refs_2_, bf16[1152,512]{1,0:T(8,128)(2,1)S(1)} %get-tuple-element.53.refs_3_, ...), custom_call_target="tpu_custom_call" | custom-call | tf_op jit(solution)/shard_map/stage_4/pallas_call | solution.py:242
  75.4 16.5 %all_to_all.5.table_ref = f32[16,1,192]{2,1,0:T(1,128)S(1)} all-to-all(f32[16,1,192]{2,1,0:T(1,128)S(1)} %stage_4.1), channel_id=1, replica_groups=mesh['groups'=2,'dp'=8,'split'=2] {'dp','split'}, dimensions={0} | all-to-all | bytes 24576 | tf_op jit(solution)/shard_map/all_to_all | solution.py:330
  91.9 0.9 lookup.1
  (23 shorter events, 1.1 us)
Async XLA Ops:
  0.0 7.9 %copy-start = (bf16[2048,512]{1,0:T(8,128)(2,1)S(1)}, bf16[2048,512]{1,0:T(8,128)(2,1)}, u32[]{:S(2)}) copy-start(bf16[2048,512]{1,0:T(8,128)(2,1)} %emb_hbm.3) | copy-start | bytes 6291460
  3.8 21.3 %collective-permute-start = (bf16[776,128]{1,0:T(8,128)(2,1)}, bf16[776,128]{1,0:T(8,128)(2,1)S(1)}, u32[]{:S(2)}, u32[]{:S(2)}) collective-permute-start(bf16[776,128]{1,0:T(8,128)(2,1)} %get-tuple-element.32), channel_id=1, source_target_pairs={{0,8},{1,9},{2,10},{3,11},{4,12},{5,13},{6,14},{7,15},{8,0},{9,1},... | collective-permute-start | bytes 595976 | tf_op jit(solution)/shard_map/ppermute | solution.py:292
  7.9 17.2 %collective-permute-start.1 = (bf16[776,128]{1,0:T(8,128)(2,1)}, bf16[776,128]{1,0:T(8,128)(2,1)S(1)}, u32[]{:S(2)}, u32[]{:S(2)}) collective-permute-start(bf16[776,128]{1,0:T(8,128)(2,1)} %get-tuple-element.33), channel_id=1, source_target_pairs={{0,9},{1,8},{2,11},{3,10},{4,13},{5,12},{6,15},{7,14},{8,1},{9,0},... | collective-permute-start | bytes 595976 | tf_op jit(solution)/shard_map/ppermute | solution.py:292
  7.9 0.7 copy-start.1
  8.6 0.8 copy-start.3
  18.8 18.9 %collective-permute-start.2 = (bf16[776,128]{1,0:T(8,128)(2,1)S(1)}, bf16[776,128]{1,0:T(8,128)(2,1)S(1)}, u32[]{:S(2)}, u32[]{:S(2)}) collective-permute-start(bf16[776,128]{1,0:T(8,128)(2,1)S(1)} %get-tuple-element.36), channel_id=1, source_target_pairs={{0,6},{1,7},{2,4},{3,5},{4,2},{5,3},{6,0},{7,1},{8,14},{9,15},{10,... | collective-permute-start | bytes 595976 | tf_op jit(solution)/shard_map/ppermute | solution.py:292
  21.4 20.5 %collective-permute-start.3 = (bf16[776,128]{1,0:T(8,128)(2,1)S(1)}, bf16[776,128]{1,0:T(8,128)(2,1)S(1)}, u32[]{:S(2)}, u32[]{:S(2)}) collective-permute-start(bf16[776,128]{1,0:T(8,128)(2,1)S(1)} %get-tuple-element.37), channel_id=1, source_target_pairs={{0,7},{1,6},{2,5},{3,4},{4,3},{5,2},{6,1},{7,0},{8,15},{9,14},{10,... | collective-permute-start | bytes 595976 | tf_op jit(solution)/shard_map/ppermute | solution.py:292
  21.6 22.1 %collective-permute-start.4 = (bf16[776,128]{1,0:T(8,128)(2,1)S(1)}, bf16[776,128]{1,0:T(8,128)(2,1)S(1)}, u32[]{:S(2)}, u32[]{:S(2)}) collective-permute-start(bf16[776,128]{1,0:T(8,128)(2,1)S(1)} %get-tuple-element.40), channel_id=1, source_target_pairs={{0,10},{1,11},{2,8},{3,9},{4,14},{5,15},{6,12},{7,13},{8,2},{9,3},... | collective-permute-start | bytes 595976 | tf_op jit(solution)/shard_map/ppermute | solution.py:292
  25.1 20.2 %collective-permute-start.5 = (bf16[776,128]{1,0:T(8,128)(2,1)S(1)}, bf16[776,128]{1,0:T(8,128)(2,1)S(1)}, u32[]{:S(2)}, u32[]{:S(2)}) collective-permute-start(bf16[776,128]{1,0:T(8,128)(2,1)S(1)} %get-tuple-element.41), channel_id=1, source_target_pairs={{0,11},{1,10},{2,9},{3,8},{4,15},{5,14},{6,13},{7,12},{8,3},{9,2},... | collective-permute-start | bytes 595976 | tf_op jit(solution)/shard_map/ppermute | solution.py:292
  25.1 22.0 %collective-permute-start.6 = (bf16[776,128]{1,0:T(8,128)(2,1)S(1)}, bf16[776,128]{1,0:T(8,128)(2,1)S(1)}, u32[]{:S(2)}, u32[]{:S(2)}) collective-permute-start(bf16[776,128]{1,0:T(8,128)(2,1)S(1)} %get-tuple-element.42), channel_id=1, source_target_pairs={{0,4},{1,5},{2,6},{3,7},{4,0},{5,1},{6,2},{7,3},{8,12},{9,13},{10,... | collective-permute-start | bytes 595976 | tf_op jit(solution)/shard_map/ppermute | solution.py:292
  37.7 22.1 %collective-permute-start.7 = (bf16[776,128]{1,0:T(8,128)(2,1)S(1)}, bf16[776,128]{1,0:T(8,128)(2,1)S(1)}, u32[]{:S(2)}, u32[]{:S(2)}) collective-permute-start(bf16[776,128]{1,0:T(8,128)(2,1)S(1)} %get-tuple-element.43), channel_id=1, source_target_pairs={{0,5},{1,4},{2,7},{3,6},{4,1},{5,0},{6,3},{7,2},{8,13},{9,12},{10,... | collective-permute-start | bytes 595976 | tf_op jit(solution)/shard_map/ppermute | solution.py:292
  41.9 18.1 %collective-permute-start.8 = (bf16[776,128]{1,0:T(8,128)(2,1)S(1)}, bf16[776,128]{1,0:T(8,128)(2,1)S(1)}, u32[]{:S(2)}, u32[]{:S(2)}) collective-permute-start(bf16[776,128]{1,0:T(8,128)(2,1)S(1)} %get-tuple-element.46), channel_id=1, source_target_pairs={{0,12},{1,13},{2,14},{3,15},{4,8},{5,9},{6,10},{7,11},{8,4},{9,5},... | collective-permute-start | bytes 595976 | tf_op jit(solution)/shard_map/ppermute | solution.py:292
  43.6 20.9 %collective-permute-start.9 = (bf16[776,128]{1,0:T(8,128)(2,1)S(1)}, bf16[776,128]{1,0:T(8,128)(2,1)S(1)}, u32[]{:S(2)}, u32[]{:S(2)}) collective-permute-start(bf16[776,128]{1,0:T(8,128)(2,1)S(1)} %get-tuple-element.47), channel_id=1, source_target_pairs={{0,13},{1,12},{2,15},{3,14},{4,9},{5,8},{6,11},{7,10},{8,5},{9,4},... | collective-permute-start | bytes 595976 | tf_op jit(solution)/shard_map/ppermute | solution.py:292
  45.3 21.8 %collective-permute-start.10 = (bf16[776,128]{1,0:T(8,128)(2,1)S(1)}, bf16[776,128]{1,0:T(8,128)(2,1)S(1)}, u32[]{:S(2)}, u32[]{:S(2)}) collective-permute-start(bf16[776,128]{1,0:T(8,128)(2,1)S(1)} %get-tuple-element.48), channel_id=1, source_target_pairs={{0,2},{1,3},{2,0},{3,1},{4,6},{5,7},{6,4},{7,5},{8,10},{9,11},{10,... | collective-permute-start | bytes 595976 | tf_op jit(solution)/shard_map/ppermute | solution.py:292
  47.2 19.9 %collective-permute-start.11 = (bf16[776,128]{1,0:T(8,128)(2,1)S(1)}, bf16[776,128]{1,0:T(8,128)(2,1)S(1)}, u32[]{:S(2)}, u32[]{:S(2)}) collective-permute-start(bf16[776,128]{1,0:T(8,128)(2,1)S(1)} %get-tuple-element.49), channel_id=1, source_target_pairs={{0,3},{1,2},{2,1},{3,0},{4,7},{5,6},{6,5},{7,4},{8,11},{9,10},{10,... | collective-permute-start | bytes 595976 | tf_op jit(solution)/shard_map/ppermute | solution.py:292
  59.8 7.3 %collective-permute-start.12 = (bf16[776,128]{1,0:T(8,128)(2,1)S(1)}, bf16[776,128]{1,0:T(8,128)(2,1)S(1)}, u32[]{:S(2)}, u32[]{:S(2)}) collective-permute-start(bf16[776,128]{1,0:T(8,128)(2,1)S(1)} %get-tuple-element.51), channel_id=1, source_target_pairs={{0,1},{1,0},{2,3},{3,2},{4,5},{5,4},{6,7},{7,6},{8,9},{9,8},{10,11... | collective-permute-start | bytes 595976 | tf_op jit(solution)/shard_map/ppermute | solution.py:292
  60.0 11.2 %collective-permute-start.13 = (bf16[776,128]{1,0:T(8,128)(2,1)S(1)}, bf16[776,128]{1,0:T(8,128)(2,1)S(1)}, u32[]{:S(2)}, u32[]{:S(2)}) collective-permute-start(bf16[776,128]{1,0:T(8,128)(2,1)S(1)} %get-tuple-element.54), channel_id=1, source_target_pairs={{0,14},{1,15},{2,12},{3,13},{4,10},{5,11},{6,8},{7,9},{8,6},{9,7},... | collective-permute-start | bytes 595976 | tf_op jit(solution)/shard_map/ppermute | solution.py:292
  64.5 9.6 %collective-permute-start.14 = (bf16[776,128]{1,0:T(8,128)(2,1)S(1)}, bf16[776,128]{1,0:T(8,128)(2,1)S(1)}, u32[]{:S(2)}, u32[]{:S(2)}) collective-permute-start(bf16[776,128]{1,0:T(8,128)(2,1)S(1)} %get-tuple-element.57), channel_id=1, source_target_pairs={{0,15},{1,14},{2,13},{3,12},{4,11},{5,10},{6,9},{7,8},{8,7},{9,6},... | collective-permute-start | bytes 595976 | tf_op jit(solution)/shard_map/ppermute | solution.py:292
  72.3 19.6 %copy-start.2 = (s32[2,2048]{1,0:T(2,128)S(1)}, s32[2,2048]{1,0:T(2,128)}, u32[]{:S(2)}) copy-start(s32[2,2048]{1,0:T(2,128)} %get-tuple-element.34.slot_ref) | copy-start | bytes 49156

commit v5 on v4

--- a/solution.py
+++ b/solution.py
@@ -12,7 +12,7 @@
 DEVICE = ("dp", "split")
 LANES = 128
 GROUPS = 8
-ORDER = (8, 9, 6, 7, 10, 11, 4, 5, 12, 13, 2, 3, 0, 1, 14, 15)
+ORDER = (8, 9, 6, 7, 10, 11, 4, 5, 14, 15, 0, 1, 2, 3, 12, 13)
 STAGES = (2, 2, 3)
 LIMBS = 4
 KEY_ROWS = 2 * LIMBS

time: 93.1 us -> 92.4 us (level)
  waiting for transfers between devices: 29.3 us -> 28.1 us
  starting transfers between devices: 22.4 us -> 23.4 us
    ppermute x15, waiting for transfers between devices: 29.3 us -> 28.1 us  [send(): lax.ppermute(block, DEVICE, [(i, i ^ offset) for i in range(clusters)])]
    ppermute x15, starting transfers between devices: 22.4 us -> 23.4 us  [send(): lax.ppermute(block, DEVICE, [(i, i ^ offset) for i in range(clusters)])]
  transfers between devices with their start and end apart: 15 -> 15, of which waited for: 5 -> 5; matrix products, arithmetic and copies ran while one was open for 0% -> 0% of each run, Pallas kernels for 18% -> 19%
where the time goes in v5:
time: 92.4 us; the launch traced here: 92.1 us
  waiting for transfers between devices  28.1 us (30%)
  starting transfers between devices  23.4 us (25%)
  Pallas kernels  23.1 us (25%)
  blocking collectives  15.9 us (17%)
  local copies, waits for them, and re-layouts  1.48 us (2%)
    ppermute x15, waiting for transfers between devices, send(): lax.ppermute(block, DEVICE, [(i, i ^ offset) for i in range(clusters)])  28.1 us
    ppermute x15, starting transfers between devices, send(): lax.ppermute(block, DEVICE, [(i, i ^ offset) for i in range(clusters)])  23.4 us
    all_to_all x1, blocking collectives, per_device(): lax.all_to_all(best, DEVICE, split_axis=0, concat_axis=0, tiled=True)  15.9 us
    pallas_call x1, Pallas kernels, pack(): pl.pallas_call(functools.partial(pack_kernel, firsts=firsts, unit=unit, m...  9.43 us
    pallas_call x5, Pallas kernels, stage(): pl.pallas_call(functools.partial(stage_kernel, olds=olds, fresh=fresh, co...  8.98 us
    pallas_call x1, Pallas kernels, first_pack(): pl.pallas_call(functools.partial(first_pack_kernel, clusters=clusters, mo...  3.79 us
  transfers between devices with their start and end apart: 15, of which 5 were waited for; matrix products, arithmetic and copies ran while one was open for 0% of the time, Pallas kernels for 19%

profile of v5, /device:TPU:0, one launch (start us, length us, event | category | flops | bytes accessed | tf_op | source)
XLA Modules:
  0.0 92.1 jit_solution(14624901092944832751)
XLA Ops:
  0.0 3.8 %first_pack.1 = (bf16[776,128]{1,0:T(8,128)(2,1)}, bf16[776,128]{1,0:T(8,128)(2,1)}, s32[2,2048]{1,0:T(2,128)}, bf16[8,2048]{1,0:T(8,128)(2,1)}) custom-call(s32[1]{0:T(128)} %bitcast.me_ref, s32[1,2048]{1,0:T(1,128)} %bitcast.4, s32[1,2048]{1,0:T(1,128)} %bitcast.5, bf16[2048,512]{1,0:T(8,128)(2,1)} %emb_hbm.3), custom_call_target="tpu_custom_call" | custom-call | tf_op jit(solution)/shard_map/first_pack/pallas_call | solution.py:115
  3.8 4.1 %collective-permute-start = (bf16[776,128]{1,0:T(8,128)(2,1)}, bf16[776,128]{1,0:T(8,128)(2,1)S(1)}, u32[]{:S(2)}, u32[]{:S(2)}) collective-permute-start(bf16[776,128]{1,0:T(8,128)(2,1)} %get-tuple-element.32), channel_id=1, source_target_pairs={{0,8},{1,9},{2,10},{3,11},{4,12},{5,13},{6,14},{7,15},{8,0},{9,1},... | collective-permute-start | bytes 595976 | tf_op jit(solution)/shard_map/ppermute | solution.py:292
  7.9 0.7 copy-done.1
  8.6 0.8 copy-done.3
  9.4 9.4 %pack.1 = (bf16[776,128]{1,0:T(8,128)(2,1)S(1)}, bf16[776,128]{1,0:T(8,128)(2,1)S(1)}, bf16[776,128]{1,0:T(8,128)(2,1)S(1)}, bf16[776,128]{1,0:T(8,128)(2,1)S(1)...) custom-call(s32[2,2048]{1,0:T(2,128)S(1)} %copy-done.1, ...), custom_call_target="tpu_custom_call" | custom-call | tf_op jit(solution)/shard_map/pack/pallas_call | solution.py:148
  18.8 2.6 %collective-permute-start.2 = (bf16[776,128]{1,0:T(8,128)(2,1)S(1)}, bf16[776,128]{1,0:T(8,128)(2,1)S(1)}, u32[]{:S(2)}, u32[]{:S(2)}) collective-permute-start(bf16[776,128]{1,0:T(8,128)(2,1)S(1)} %get-tuple-element.36), channel_id=1, source_target_pairs={{0,6},{1,7},{2,4},{3,5},{4,2},{5,3},{6,0},{7,1},{8,14},{9,15},{10,... | collective-permute-start | bytes 595976 | tf_op jit(solution)/shard_map/ppermute | solution.py:292
  21.6 3.6 %collective-permute-start.4 = (bf16[776,128]{1,0:T(8,128)(2,1)S(1)}, bf16[776,128]{1,0:T(8,128)(2,1)S(1)}, u32[]{:S(2)}, u32[]{:S(2)}) collective-permute-start(bf16[776,128]{1,0:T(8,128)(2,1)S(1)} %get-tuple-element.40), channel_id=1, source_target_pairs={{0,10},{1,11},{2,8},{3,9},{4,14},{5,15},{6,12},{7,13},{8,2},{9,3},... | collective-permute-start | bytes 595976 | tf_op jit(solution)/shard_map/ppermute | solution.py:292
  25.1 1.7 %collective-permute-start.6 = (bf16[776,128]{1,0:T(8,128)(2,1)S(1)}, bf16[776,128]{1,0:T(8,128)(2,1)S(1)}, u32[]{:S(2)}, u32[]{:S(2)}) collective-permute-start(bf16[776,128]{1,0:T(8,128)(2,1)S(1)} %get-tuple-element.42), channel_id=1, source_target_pairs={{0,4},{1,5},{2,6},{3,7},{4,0},{5,1},{6,2},{7,3},{8,12},{9,13},{10,... | collective-permute-start | bytes 595976 | tf_op jit(solution)/shard_map/ppermute | solution.py:292
  26.8 10.9 %collective-permute-done.2.refs_2_ = bf16[776,128]{1,0:T(8,128)(2,1)S(1)} collective-permute-done((bf16[776,128]{1,0:T(8,128)(2,1)S(1)}, bf16[776,128]{1,0:T(8,128)(2,1)S(1)}, u32[]{:S(2)}, u32[]{:S(2)}) %collective-permute-start.2) | collective-permute-done | bytes 198688 | tf_op jit(solution)/shard_map/ppermute | solution.py:292
  37.7 4.1 %collective-permute-done.3.refs_3_ = bf16[776,128]{1,0:T(8,128)(2,1)S(1)} collective-permute-done((bf16[776,128]{1,0:T(8,128)(2,1)S(1)}, bf16[776,128]{1,0:T(8,128)(2,1)S(1)}, u32[]{:S(2)}, u32[]{:S(2)}) %collective-permute-start.3) | collective-permute-done | bytes 198688 | tf_op jit(solution)/shard_map/ppermute | solution.py:292
  41.9 2.6 %collective-permute-start.8 = (bf16[776,128]{1,0:T(8,128)(2,1)S(1)}, bf16[776,128]{1,0:T(8,128)(2,1)S(1)}, u32[]{:S(2)}, u32[]{:S(2)}) collective-permute-start(bf16[776,128]{1,0:T(8,128)(2,1)S(1)} %get-tuple-element.46), channel_id=1, source_target_pairs={{0,14},{1,15},{2,12},{3,13},{4,10},{5,11},{6,8},{7,9},{8,6},{9,7},... | collective-permute-start | bytes 595976 | tf_op jit(solution)/shard_map/ppermute | solution.py:292
  44.5 1.7 %collective-permute-start.9 = (bf16[776,128]{1,0:T(8,128)(2,1)S(1)}, bf16[776,128]{1,0:T(8,128)(2,1)S(1)}, u32[]{:S(2)}, u32[]{:S(2)}) collective-permute-start(bf16[776,128]{1,0:T(8,128)(2,1)S(1)} %get-tuple-element.47), channel_id=1, source_target_pairs={{0,15},{1,14},{2,13},{3,12},{4,11},{5,10},{6,9},{7,8},{8,7},{9,6},... | collective-permute-start | bytes 595976 | tf_op jit(solution)/shard_map/ppermute | solution.py:292
  47.2 1.6 %collective-permute-start.11 = (bf16[776,128]{1,0:T(8,128)(2,1)S(1)}, bf16[776,128]{1,0:T(8,128)(2,1)S(1)}, u32[]{:S(2)}, u32[]{:S(2)}) collective-permute-start(bf16[776,128]{1,0:T(8,128)(2,1)S(1)} %get-tuple-element.50), channel_id=1, source_target_pairs={{0,2},{1,3},{2,0},{3,1},{4,6},{5,7},{6,4},{7,5},{8,10},{9,11},{10,... | collective-permute-start | bytes 595976 | tf_op jit(solution)/shard_map/ppermute | solution.py:292
  48.7 11.1 %collective-permute-done.7.refs_5_ = bf16[776,128]{1,0:T(8,128)(2,1)S(1)} collective-permute-done((bf16[776,128]{1,0:T(8,128)(2,1)S(1)}, bf16[776,128]{1,0:T(8,128)(2,1)S(1)}, u32[]{:S(2)}, u32[]{:S(2)}) %collective-permute-start.7) | collective-permute-done | bytes 198688 | tf_op jit(solution)/shard_map/ppermute | solution.py:292
  59.8 1.3 %collective-permute-start.12 = (bf16[776,128]{1,0:T(8,128)(2,1)S(1)}, bf16[776,128]{1,0:T(8,128)(2,1)S(1)}, u32[]{:S(2)}, u32[]{:S(2)}) collective-permute-start(bf16[776,128]{1,0:T(8,128)(2,1)S(1)} %get-tuple-element.51), channel_id=1, source_target_pairs={{0,3},{1,2},{2,1},{3,0},{4,7},{5,6},{6,5},{7,4},{8,11},{9,10},{10,... | collective-permute-start | bytes 595976 | tf_op jit(solution)/shard_map/ppermute | solution.py:292
  61.2 3.5 %collective-permute-start.13 = (bf16[776,128]{1,0:T(8,128)(2,1)S(1)}, bf16[776,128]{1,0:T(8,128)(2,1)S(1)}, u32[]{:S(2)}, u32[]{:S(2)}) collective-permute-start(bf16[776,128]{1,0:T(8,128)(2,1)S(1)} %get-tuple-element.54), channel_id=1, source_target_pairs={{0,12},{1,13},{2,14},{3,15},{4,8},{5,9},{6,10},{7,11},{8,4},{9,5},... | collective-permute-start | bytes 595976 | tf_op jit(solution)/shard_map/ppermute | solution.py:292
  64.7 0.9 %stage_0.1 = (f32[2,768]{1,0:T(2,128)S(1)}, bf16[768,512]{1,0:T(8,128)(2,1)S(1)}) custom-call(s32[1]{0:T(128)} %bitcast.me_ref, bf16[776,128]{1,0:T(8,128)(2,1)S(1)} %collective-permute-done.refs_0_, bf16[776,128]{1,0:T(8,128)(2,1)S(1)} %collective-permute-done.1.refs_1_, bf16[776,128]{1,0:T(8,128)(2,1)S(1)} %collective-permute-done.2.refs_2_, ...), custom_call_target="tpu_custom_call" | custom-call | tf_op jit(solution)/shard_map/stage_0/pallas_call | solution.py:242
  65.7 1.6 %stage_1.1 = (f32[2,1536]{1,0:T(2,128)S(1)}, bf16[768,512]{1,0:T(8,128)(2,1)S(1)}) custom-call(s32[1]{0:T(128)} %bitcast.me_ref, f32[2,768]{1,0:T(2,128)S(1)} %get-tuple-element.38.refs_0_, bf16[768,512]{1,0:T(8,128)(2,1)S(1)} %get-tuple-element.39.refs_1_, bf16[776,128]{1,0:T(8,128)(2,1)S(1)} %collective-permute-done.4.refs_2_, ...), custom_call_target="tpu_custom_call" | custom-call | tf_op jit(solution)/shard_map/stage_1/pallas_call | solution.py:242
  67.3 4.0 %stage_2.1 = (f32[2,2688]{1,0:T(2,128)S(1)}, bf16[1152,512]{1,0:T(8,128)(2,1)S(1)}) custom-call(s32[1]{0:T(128)} %bitcast.me_ref, f32[2,1536]{1,0:T(2,128)S(1)} %get-tuple-element.44.refs_0_, bf16[768,512]{1,0:T(8,128)(2,1)S(1)} %get-tuple-element.39.refs_1_, bf16[768,512]{1,0:T(8,128)(2,1)S(1)} %get-tuple-element.45.refs_2_, ...), custom_call_target="tpu_custom_call" | custom-call | tf_op jit(solution)/shard_map/stage_2/pallas_call | solution.py:242
  71.3 1.2 %stage_3.1 = (f32[2,2944]{1,0:T(2,128)S(1)}, bf16[256,512]{1,0:T(8,128)(2,1)S(1)}) custom-call(s32[1]{0:T(128)} %bitcast.me_ref, f32[2,2688]{1,0:T(2,128)S(1)} %get-tuple-element.52.refs_0_, bf16[768,512]{1,0:T(8,128)(2,1)S(1)} %get-tuple-element.39.refs_1_, bf16[768,512]{1,0:T(8,128)(2,1)S(1)} %get-tuple-element.45.refs_2_, ...), custom_call_target="tpu_custom_call" | custom-call | tf_op jit(solution)/shard_map/stage_3/pallas_call | solution.py:242
  72.5 1.5 %collective-permute-done.14.refs_5_ = bf16[776,128]{1,0:T(8,128)(2,1)S(1)} collective-permute-done((bf16[776,128]{1,0:T(8,128)(2,1)S(1)}, bf16[776,128]{1,0:T(8,128)(2,1)S(1)}, u32[]{:S(2)}, u32[]{:S(2)}) %collective-permute-start.14) | collective-permute-done | bytes 198688 | tf_op jit(solution)/shard_map/ppermute | solution.py:292
  74.0 1.3 %stage_4.1 = f32[16,1,192]{2,1,0:T(1,128)S(1)} custom-call(s32[1]{0:T(128)} %bitcast.me_ref, f32[2,2944]{1,0:T(2,128)S(1)} %get-tuple-element.55.refs_0_, bf16[768,512]{1,0:T(8,128)(2,1)S(1)} %get-tuple-element.39.refs_1_, bf16[768,512]{1,0:T(8,128)(2,1)S(1)} %get-tuple-element.45.refs_2_, bf16[1152,512]{1,0:T(8,128)(2,1)S(1)} %get-tuple-element.53.refs_3_, ...), custom_call_target="tpu_custom_call" | custom-call | tf_op jit(solution)/shard_map/stage_4/pallas_call | solution.py:242
  75.3 15.9 %all_to_all.5.table_ref = f32[16,1,192]{2,1,0:T(1,128)S(1)} all-to-all(f32[16,1,192]{2,1,0:T(1,128)S(1)} %stage_4.1), channel_id=1, replica_groups=mesh['groups'=2,'dp'=8,'split'=2] {'dp','split'}, dimensions={0} | all-to-all | bytes 24576 | tf_op jit(solution)/shard_map/all_to_all | solution.py:330
  91.2 0.9 lookup.1
  (23 shorter events, 1.2 us)
Async XLA Ops:
  0.0 7.9 %copy-start = (bf16[2048,512]{1,0:T(8,128)(2,1)S(1)}, bf16[2048,512]{1,0:T(8,128)(2,1)}, u32[]{:S(2)}) copy-start(bf16[2048,512]{1,0:T(8,128)(2,1)} %emb_hbm.3) | copy-start | bytes 6291460
  3.8 21.3 %collective-permute-start = (bf16[776,128]{1,0:T(8,128)(2,1)}, bf16[776,128]{1,0:T(8,128)(2,1)S(1)}, u32[]{:S(2)}, u32[]{:S(2)}) collective-permute-start(bf16[776,128]{1,0:T(8,128)(2,1)} %get-tuple-element.32), channel_id=1, source_target_pairs={{0,8},{1,9},{2,10},{3,11},{4,12},{5,13},{6,14},{7,15},{8,0},{9,1},... | collective-permute-start | bytes 595976 | tf_op jit(solution)/shard_map/ppermute | solution.py:292
  7.9 17.2 %collective-permute-start.1 = (bf16[776,128]{1,0:T(8,128)(2,1)}, bf16[776,128]{1,0:T(8,128)(2,1)S(1)}, u32[]{:S(2)}, u32[]{:S(2)}) collective-permute-start(bf16[776,128]{1,0:T(8,128)(2,1)} %get-tuple-element.33), channel_id=1, source_target_pairs={{0,9},{1,8},{2,11},{3,10},{4,13},{5,12},{6,15},{7,14},{8,1},{9,0},... | collective-permute-start | bytes 595976 | tf_op jit(solution)/shard_map/ppermute | solution.py:292
  7.9 0.7 copy-start.1
  8.6 0.8 copy-start.3
  18.8 18.9 %collective-permute-start.2 = (bf16[776,128]{1,0:T(8,128)(2,1)S(1)}, bf16[776,128]{1,0:T(8,128)(2,1)S(1)}, u32[]{:S(2)}, u32[]{:S(2)}) collective-permute-start(bf16[776,128]{1,0:T(8,128)(2,1)S(1)} %get-tuple-element.36), channel_id=1, source_target_pairs={{0,6},{1,7},{2,4},{3,5},{4,2},{5,3},{6,0},{7,1},{8,14},{9,15},{10,... | collective-permute-start | bytes 595976 | tf_op jit(solution)/shard_map/ppermute | solution.py:292
  21.4 20.5 %collective-permute-start.3 = (bf16[776,128]{1,0:T(8,128)(2,1)S(1)}, bf16[776,128]{1,0:T(8,128)(2,1)S(1)}, u32[]{:S(2)}, u32[]{:S(2)}) collective-permute-start(bf16[776,128]{1,0:T(8,128)(2,1)S(1)} %get-tuple-element.37), channel_id=1, source_target_pairs={{0,7},{1,6},{2,5},{3,4},{4,3},{5,2},{6,1},{7,0},{8,15},{9,14},{10,... | collective-permute-start | bytes 595976 | tf_op jit(solution)/shard_map/ppermute | solution.py:292
  21.6 22.9 %collective-permute-start.4 = (bf16[776,128]{1,0:T(8,128)(2,1)S(1)}, bf16[776,128]{1,0:T(8,128)(2,1)S(1)}, u32[]{:S(2)}, u32[]{:S(2)}) collective-permute-start(bf16[776,128]{1,0:T(8,128)(2,1)S(1)} %get-tuple-element.40), channel_id=1, source_target_pairs={{0,10},{1,11},{2,8},{3,9},{4,14},{5,15},{6,12},{7,13},{8,2},{9,3},... | collective-permute-start | bytes 595976 | tf_op jit(solution)/shard_map/ppermute | solution.py:292
  25.1 21.1 %collective-permute-start.5 = (bf16[776,128]{1,0:T(8,128)(2,1)S(1)}, bf16[776,128]{1,0:T(8,128)(2,1)S(1)}, u32[]{:S(2)}, u32[]{:S(2)}) collective-permute-start(bf16[776,128]{1,0:T(8,128)(2,1)S(1)} %get-tuple-element.41), channel_id=1, source_target_pairs={{0,11},{1,10},{2,9},{3,8},{4,15},{5,14},{6,13},{7,12},{8,3},{9,2},... | collective-permute-start | bytes 595976 | tf_op jit(solution)/shard_map/ppermute | solution.py:292
  25.1 22.0 %collective-permute-start.6 = (bf16[776,128]{1,0:T(8,128)(2,1)S(1)}, bf16[776,128]{1,0:T(8,128)(2,1)S(1)}, u32[]{:S(2)}, u32[]{:S(2)}) collective-permute-start(bf16[776,128]{1,0:T(8,128)(2,1)S(1)} %get-tuple-element.42), channel_id=1, source_target_pairs={{0,4},{1,5},{2,6},{3,7},{4,0},{5,1},{6,2},{7,3},{8,12},{9,13},{10,... | collective-permute-start | bytes 595976 | tf_op jit(solution)/shard_map/ppermute | solution.py:292
  37.7 22.1 %collective-permute-start.7 = (bf16[776,128]{1,0:T(8,128)(2,1)S(1)}, bf16[776,128]{1,0:T(8,128)(2,1)S(1)}, u32[]{:S(2)}, u32[]{:S(2)}) collective-permute-start(bf16[776,128]{1,0:T(8,128)(2,1)S(1)} %get-tuple-element.43), channel_id=1, source_target_pairs={{0,5},{1,4},{2,7},{3,6},{4,1},{5,0},{6,3},{7,2},{8,13},{9,12},{10,... | collective-permute-start | bytes 595976 | tf_op jit(solution)/shard_map/ppermute | solution.py:292
  41.9 19.3 %collective-permute-start.8 = (bf16[776,128]{1,0:T(8,128)(2,1)S(1)}, bf16[776,128]{1,0:T(8,128)(2,1)S(1)}, u32[]{:S(2)}, u32[]{:S(2)}) collective-permute-start(bf16[776,128]{1,0:T(8,128)(2,1)S(1)} %get-tuple-element.46), channel_id=1, source_target_pairs={{0,14},{1,15},{2,12},{3,13},{4,10},{5,11},{6,8},{7,9},{8,6},{9,7},... | collective-permute-start | bytes 595976 | tf_op jit(solution)/shard_map/ppermute | solution.py:292
  44.5 20.2 %collective-permute-start.9 = (bf16[776,128]{1,0:T(8,128)(2,1)S(1)}, bf16[776,128]{1,0:T(8,128)(2,1)S(1)}, u32[]{:S(2)}, u32[]{:S(2)}) collective-permute-start(bf16[776,128]{1,0:T(8,128)(2,1)S(1)} %get-tuple-element.47), channel_id=1, source_target_pairs={{0,15},{1,14},{2,13},{3,12},{4,11},{5,10},{6,9},{7,8},{8,7},{9,6},... | collective-permute-start | bytes 595976 | tf_op jit(solution)/shard_map/ppermute | solution.py:292
  46.2 21.1 %collective-permute-start.10 = (bf16[776,128]{1,0:T(8,128)(2,1)S(1)}, bf16[776,128]{1,0:T(8,128)(2,1)S(1)}, u32[]{:S(2)}, u32[]{:S(2)}) collective-permute-start(bf16[776,128]{1,0:T(8,128)(2,1)S(1)} %get-tuple-element.49), channel_id=1, source_target_pairs={{0,1},{1,0},{2,3},{3,2},{4,5},{5,4},{6,7},{7,6},{8,9},{9,8},{10,11... | collective-permute-start | bytes 595976 | tf_op jit(solution)/shard_map/ppermute | solution.py:292
  47.2 20.1 %collective-permute-start.11 = (bf16[776,128]{1,0:T(8,128)(2,1)S(1)}, bf16[776,128]{1,0:T(8,128)(2,1)S(1)}, u32[]{:S(2)}, u32[]{:S(2)}) collective-permute-start(bf16[776,128]{1,0:T(8,128)(2,1)S(1)} %get-tuple-element.50), channel_id=1, source_target_pairs={{0,2},{1,3},{2,0},{3,1},{4,6},{5,7},{6,4},{7,5},{8,10},{9,11},{10,... | collective-permute-start | bytes 595976 | tf_op jit(solution)/shard_map/ppermute | solution.py:292
  59.8 7.4 %collective-permute-start.12 = (bf16[776,128]{1,0:T(8,128)(2,1)S(1)}, bf16[776,128]{1,0:T(8,128)(2,1)S(1)}, u32[]{:S(2)}, u32[]{:S(2)}) collective-permute-start(bf16[776,128]{1,0:T(8,128)(2,1)S(1)} %get-tuple-element.51), channel_id=1, source_target_pairs={{0,3},{1,2},{2,1},{3,0},{4,7},{5,6},{6,5},{7,4},{8,11},{9,10},{10,... | collective-permute-start | bytes 595976 | tf_op jit(solution)/shard_map/ppermute | solution.py:292
  61.2 10.1 %collective-permute-start.13 = (bf16[776,128]{1,0:T(8,128)(2,1)S(1)}, bf16[776,128]{1,0:T(8,128)(2,1)S(1)}, u32[]{:S(2)}, u32[]{:S(2)}) collective-permute-start(bf16[776,128]{1,0:T(8,128)(2,1)S(1)} %get-tuple-element.54), channel_id=1, source_target_pairs={{0,12},{1,13},{2,14},{3,15},{4,8},{5,9},{6,10},{7,11},{8,4},{9,5},... | collective-permute-start | bytes 595976 | tf_op jit(solution)/shard_map/ppermute | solution.py:292
  64.7 9.3 %collective-permute-start.14 = (bf16[776,128]{1,0:T(8,128)(2,1)S(1)}, bf16[776,128]{1,0:T(8,128)(2,1)S(1)}, u32[]{:S(2)}, u32[]{:S(2)}) collective-permute-start(bf16[776,128]{1,0:T(8,128)(2,1)S(1)} %get-tuple-element.57), channel_id=1, source_target_pairs={{0,13},{1,12},{2,15},{3,14},{4,9},{5,8},{6,11},{7,10},{8,5},{9,4},... | collective-permute-start | bytes 595976 | tf_op jit(solution)/shard_map/ppermute | solution.py:292
  72.5 18.8 %copy-start.2 = (s32[2,2048]{1,0:T(2,128)S(1)}, s32[2,2048]{1,0:T(2,128)}, u32[]{:S(2)}) copy-start(s32[2,2048]{1,0:T(2,128)} %get-tuple-element.34.slot_ref) | copy-start | bytes 49156

commit v6 on v5

--- a/solution.py
+++ b/solution.py
@@ -12,7 +12,7 @@
 DEVICE = ("dp", "split")
 LANES = 128
 GROUPS = 8
-ORDER = (8, 9, 6, 7, 10, 11, 4, 5, 14, 15, 0, 1, 2, 3, 12, 13)
+ORDER = (8, 9, 6, 7, 10, 11, 14, 15, 4, 5, 0, 1, 2, 3, 12, 13)
 STAGES = (2, 2, 3)
 LIMBS = 4
 KEY_ROWS = 2 * LIMBS

time: 92.4 us -> 90.7 us (0.982)
  waiting for transfers between devices: 28.1 us -> 21.4 us
  starting transfers between devices: 23.4 us -> 27.1 us
  blocking collectives: 15.9 us -> 17.2 us
    ppermute x15, waiting for transfers between devices: 28.1 us -> 21.4 us  [send(): lax.ppermute(block, DEVICE, [(i, i ^ offset) for i in range(clusters)])]
    ppermute x15, starting transfers between devices: 23.4 us -> 27.1 us  [send(): lax.ppermute(block, DEVICE, [(i, i ^ offset) for i in range(clusters)])]
    all_to_all x1, blocking collectives: 15.9 us -> 17.2 us  [per_device(): lax.all_to_all(best, DEVICE, split_axis=0, concat_axis=0, tiled=True)]
where the time goes in v6:
time: 90.7 us; the launch traced here: 90.4 us
  starting transfers between devices  27.1 us (30%)
  Pallas kernels  23.1 us (25%)
  waiting for transfers between devices  21.4 us (24%)
  blocking collectives  17.2 us (19%)
  local copies, waits for them, and re-layouts  1.48 us (2%)
    ppermute x15, starting transfers between devices, send(): lax.ppermute(block, DEVICE, [(i, i ^ offset) for i in range(clusters)])  27.1 us
    ppermute x15, waiting for transfers between devices, send(): lax.ppermute(block, DEVICE, [(i, i ^ offset) for i in range(clusters)])  21.4 us
    all_to_all x1, blocking collectives, per_device(): lax.all_to_all(best, DEVICE, split_axis=0, concat_axis=0, tiled=True)  17.2 us
    pallas_call x1, Pallas kernels, pack(): pl.pallas_call(functools.partial(pack_kernel, firsts=firsts, unit=unit, m...  9.43 us
    pallas_call x5, Pallas kernels, stage(): pl.pallas_call(functools.partial(stage_kernel, olds=olds, fresh=fresh, co...  8.98 us
    pallas_call x1, Pallas kernels, first_pack(): pl.pallas_call(functools.partial(first_pack_kernel, clusters=clusters, mo...  3.79 us
  transfers between devices with their start and end apart: 15, of which 5 were waited for; matrix products, arithmetic and copies ran while one was open for 0% of the time, Pallas kernels for 19%

profile of v6, /device:TPU:0, one launch (start us, length us, event | category | flops | bytes accessed | tf_op | source)
XLA Modules:
  0.0 90.4 jit_solution(5801791834426734030)
XLA Ops:
  0.0 3.8 %first_pack.1 = (bf16[776,128]{1,0:T(8,128)(2,1)}, bf16[776,128]{1,0:T(8,128)(2,1)}, s32[2,2048]{1,0:T(2,128)}, bf16[8,2048]{1,0:T(8,128)(2,1)}) custom-call(s32[1]{0:T(128)} %bitcast.me_ref, s32[1,2048]{1,0:T(1,128)} %bitcast.4, s32[1,2048]{1,0:T(1,128)} %bitcast.5, bf16[2048,512]{1,0:T(8,128)(2,1)} %emb_hbm.3), custom_call_target="tpu_custom_call" | custom-call | tf_op jit(solution)/shard_map/first_pack/pallas_call | solution.py:115
  3.8 4.1 %collective-permute-start = (bf16[776,128]{1,0:T(8,128)(2,1)}, bf16[776,128]{1,0:T(8,128)(2,1)S(1)}, u32[]{:S(2)}, u32[]{:S(2)}) collective-permute-start(bf16[776,128]{1,0:T(8,128)(2,1)} %get-tuple-element.32), channel_id=1, source_target_pairs={{0,8},{1,9},{2,10},{3,11},{4,12},{5,13},{6,14},{7,15},{8,0},{9,1},... | collective-permute-start | bytes 595976 | tf_op jit(solution)/shard_map/ppermute | solution.py:292
  8.6 0.8 copy-done.3
  9.4 9.4 %pack.1 = (bf16[776,128]{1,0:T(8,128)(2,1)S(1)}, bf16[776,128]{1,0:T(8,128)(2,1)S(1)}, bf16[776,128]{1,0:T(8,128)(2,1)S(1)}, bf16[776,128]{1,0:T(8,128)(2,1)S(1)...) custom-call(s32[2,2048]{1,0:T(2,128)S(1)} %copy-done.1, ...), custom_call_target="tpu_custom_call" | custom-call | tf_op jit(solution)/shard_map/pack/pallas_call | solution.py:148
  18.8 2.6 %collective-permute-start.2 = (bf16[776,128]{1,0:T(8,128)(2,1)S(1)}, bf16[776,128]{1,0:T(8,128)(2,1)S(1)}, u32[]{:S(2)}, u32[]{:S(2)}) collective-permute-start(bf16[776,128]{1,0:T(8,128)(2,1)S(1)} %get-tuple-element.36), channel_id=1, source_target_pairs={{0,6},{1,7},{2,4},{3,5},{4,2},{5,3},{6,0},{7,1},{8,14},{9,15},{10,... | collective-permute-start | bytes 595976 | tf_op jit(solution)/shard_map/ppermute | solution.py:292
  21.6 3.6 %collective-permute-start.4 = (bf16[776,128]{1,0:T(8,128)(2,1)S(1)}, bf16[776,128]{1,0:T(8,128)(2,1)S(1)}, u32[]{:S(2)}, u32[]{:S(2)}) collective-permute-start(bf16[776,128]{1,0:T(8,128)(2,1)S(1)} %get-tuple-element.40), channel_id=1, source_target_pairs={{0,10},{1,11},{2,8},{3,9},{4,14},{5,15},{6,12},{7,13},{8,2},{9,3},... | collective-permute-start | bytes 595976 | tf_op jit(solution)/shard_map/ppermute | solution.py:292
  25.1 5.2 %collective-permute-start.6 = (bf16[776,128]{1,0:T(8,128)(2,1)S(1)}, bf16[776,128]{1,0:T(8,128)(2,1)S(1)}, u32[]{:S(2)}, u32[]{:S(2)}) collective-permute-start(bf16[776,128]{1,0:T(8,128)(2,1)S(1)} %get-tuple-element.42), channel_id=1, source_target_pairs={{0,14},{1,15},{2,12},{3,13},{4,10},{5,11},{6,8},{7,9},{8,6},{9,7},... | collective-permute-start | bytes 595976 | tf_op jit(solution)/shard_map/ppermute | solution.py:292
  30.3 7.4 %collective-permute-done.2.refs_2_ = bf16[776,128]{1,0:T(8,128)(2,1)S(1)} collective-permute-done((bf16[776,128]{1,0:T(8,128)(2,1)S(1)}, bf16[776,128]{1,0:T(8,128)(2,1)S(1)}, u32[]{:S(2)}, u32[]{:S(2)}) %collective-permute-start.2) | collective-permute-done | bytes 198688 | tf_op jit(solution)/shard_map/ppermute | solution.py:292
  37.7 1.9 %collective-permute-start.7 = (bf16[776,128]{1,0:T(8,128)(2,1)S(1)}, bf16[776,128]{1,0:T(8,128)(2,1)S(1)}, u32[]{:S(2)}, u32[]{:S(2)}) collective-permute-start(bf16[776,128]{1,0:T(8,128)(2,1)S(1)} %get-tuple-element.43), channel_id=1, source_target_pairs={{0,15},{1,14},{2,13},{3,12},{4,11},{5,10},{6,9},{7,8},{8,7},{9,6},... | collective-permute-start | bytes 595976 | tf_op jit(solution)/shard_map/ppermute | solution.py:292
  39.7 2.2 %collective-permute-done.3.refs_3_ = bf16[776,128]{1,0:T(8,128)(2,1)S(1)} collective-permute-done((bf16[776,128]{1,0:T(8,128)(2,1)S(1)}, bf16[776,128]{1,0:T(8,128)(2,1)S(1)}, u32[]{:S(2)}, u32[]{:S(2)}) %collective-permute-start.3) | collective-permute-done | bytes 198688 | tf_op jit(solution)/shard_map/ppermute | solution.py:292
  41.9 1.5 %collective-permute-start.9 = (bf16[776,128]{1,0:T(8,128)(2,1)S(1)}, bf16[776,128]{1,0:T(8,128)(2,1)S(1)}, u32[]{:S(2)}, u32[]{:S(2)}) collective-permute-start(bf16[776,128]{1,0:T(8,128)(2,1)S(1)} %get-tuple-element.47), channel_id=1, source_target_pairs={{0,5},{1,4},{2,7},{3,6},{4,1},{5,0},{6,3},{7,2},{8,13},{9,12},{10,... | collective-permute-start | bytes 595976 | tf_op jit(solution)/shard_map/ppermute | solution.py:292
  43.4 8.6 %collective-permute-done.5.refs_3_ = bf16[776,128]{1,0:T(8,128)(2,1)S(1)} collective-permute-done((bf16[776,128]{1,0:T(8,128)(2,1)S(1)}, bf16[776,128]{1,0:T(8,128)(2,1)S(1)}, u32[]{:S(2)}, u32[]{:S(2)}) %collective-permute-start.5) | collective-permute-done | bytes 198688 | tf_op jit(solution)/shard_map/ppermute | solution.py:292
  52.8 1.0 %collective-permute-start.11 = (bf16[776,128]{1,0:T(8,128)(2,1)S(1)}, bf16[776,128]{1,0:T(8,128)(2,1)S(1)}, u32[]{:S(2)}, u32[]{:S(2)}) collective-permute-start(bf16[776,128]{1,0:T(8,128)(2,1)S(1)} %get-tuple-element.50), channel_id=1, source_target_pairs={{0,2},{1,3},{2,0},{3,1},{4,6},{5,7},{6,4},{7,5},{8,10},{9,11},{10,... | collective-permute-start | bytes 595976 | tf_op jit(solution)/shard_map/ppermute | solution.py:292
  54.1 2.1 %collective-permute-done.8.refs_3_ = bf16[776,128]{1,0:T(8,128)(2,1)S(1)} collective-permute-done((bf16[776,128]{1,0:T(8,128)(2,1)S(1)}, bf16[776,128]{1,0:T(8,128)(2,1)S(1)}, u32[]{:S(2)}, u32[]{:S(2)}) %collective-permute-start.8) | collective-permute-done | bytes 198688 | tf_op jit(solution)/shard_map/ppermute | solution.py:292
  56.2 3.1 %collective-permute-start.13 = (bf16[776,128]{1,0:T(8,128)(2,1)S(1)}, bf16[776,128]{1,0:T(8,128)(2,1)S(1)}, u32[]{:S(2)}, u32[]{:S(2)}) collective-permute-start(bf16[776,128]{1,0:T(8,128)(2,1)S(1)} %get-tuple-element.54), channel_id=1, source_target_pairs={{0,12},{1,13},{2,14},{3,15},{4,8},{5,9},{6,10},{7,11},{8,4},{9,5},... | collective-permute-start | bytes 595976 | tf_op jit(solution)/shard_map/ppermute | solution.py:292
  59.3 1.0 %collective-permute-done.9.refs_4_ = bf16[776,128]{1,0:T(8,128)(2,1)S(1)} collective-permute-done((bf16[776,128]{1,0:T(8,128)(2,1)S(1)}, bf16[776,128]{1,0:T(8,128)(2,1)S(1)}, u32[]{:S(2)}, u32[]{:S(2)}) %collective-permute-start.9) | collective-permute-done | bytes 198688 | tf_op jit(solution)/shard_map/ppermute | solution.py:292
  60.4 2.9 %collective-permute-start.14 = (bf16[776,128]{1,0:T(8,128)(2,1)S(1)}, bf16[776,128]{1,0:T(8,128)(2,1)S(1)}, u32[]{:S(2)}, u32[]{:S(2)}) collective-permute-start(bf16[776,128]{1,0:T(8,128)(2,1)S(1)} %get-tuple-element.57), channel_id=1, source_target_pairs={{0,13},{1,12},{2,15},{3,14},{4,9},{5,8},{6,11},{7,10},{8,5},{9,4},... | collective-permute-start | bytes 595976 | tf_op jit(solution)/shard_map/ppermute | solution.py:292
  63.2 0.9 %stage_0.1 = (f32[2,768]{1,0:T(2,128)S(1)}, bf16[768,512]{1,0:T(8,128)(2,1)S(1)}) custom-call(s32[1]{0:T(128)} %bitcast.me_ref, bf16[776,128]{1,0:T(8,128)(2,1)S(1)} %collective-permute-done.refs_0_, bf16[776,128]{1,0:T(8,128)(2,1)S(1)} %collective-permute-done.1.refs_1_, bf16[776,128]{1,0:T(8,128)(2,1)S(1)} %collective-permute-done.2.refs_2_, ...), custom_call_target="tpu_custom_call" | custom-call | tf_op jit(solution)/shard_map/stage_0/pallas_call | solution.py:242
  64.2 1.6 %stage_1.1 = (f32[2,1536]{1,0:T(2,128)S(1)}, bf16[768,512]{1,0:T(8,128)(2,1)S(1)}) custom-call(s32[1]{0:T(128)} %bitcast.me_ref, f32[2,768]{1,0:T(2,128)S(1)} %get-tuple-element.38.refs_0_, bf16[768,512]{1,0:T(8,128)(2,1)S(1)} %get-tuple-element.39.refs_1_, bf16[776,128]{1,0:T(8,128)(2,1)S(1)} %collective-permute-done.4.refs_2_, ...), custom_call_target="tpu_custom_call" | custom-call | tf_op jit(solution)/shard_map/stage_1/pallas_call | solution.py:242
  65.8 4.0 %stage_2.1 = (f32[2,2688]{1,0:T(2,128)S(1)}, bf16[1152,512]{1,0:T(8,128)(2,1)S(1)}) custom-call(s32[1]{0:T(128)} %bitcast.me_ref, f32[2,1536]{1,0:T(2,128)S(1)} %get-tuple-element.44.refs_0_, bf16[768,512]{1,0:T(8,128)(2,1)S(1)} %get-tuple-element.39.refs_1_, bf16[768,512]{1,0:T(8,128)(2,1)S(1)} %get-tuple-element.45.refs_2_, ...), custom_call_target="tpu_custom_call" | custom-call | tf_op jit(solution)/shard_map/stage_2/pallas_call | solution.py:242
  69.8 1.2 %stage_3.1 = (f32[2,2944]{1,0:T(2,128)S(1)}, bf16[256,512]{1,0:T(8,128)(2,1)S(1)}) custom-call(s32[1]{0:T(128)} %bitcast.me_ref, f32[2,2688]{1,0:T(2,128)S(1)} %get-tuple-element.52.refs_0_, bf16[768,512]{1,0:T(8,128)(2,1)S(1)} %get-tuple-element.39.refs_1_, bf16[768,512]{1,0:T(8,128)(2,1)S(1)} %get-tuple-element.45.refs_2_, ...), custom_call_target="tpu_custom_call" | custom-call | tf_op jit(solution)/shard_map/stage_3/pallas_call | solution.py:242
  71.0 1.3 %stage_4.1 = f32[16,1,192]{2,1,0:T(1,128)S(1)} custom-call(s32[1]{0:T(128)} %bitcast.me_ref, f32[2,2944]{1,0:T(2,128)S(1)} %get-tuple-element.55.refs_0_, bf16[768,512]{1,0:T(8,128)(2,1)S(1)} %get-tuple-element.39.refs_1_, bf16[768,512]{1,0:T(8,128)(2,1)S(1)} %get-tuple-element.45.refs_2_, bf16[1152,512]{1,0:T(8,128)(2,1)S(1)} %get-tuple-element.53.refs_3_, ...), custom_call_target="tpu_custom_call" | custom-call | tf_op jit(solution)/shard_map/stage_4/pallas_call | solution.py:242
  72.3 17.2 %all_to_all.5.table_ref = f32[16,1,192]{2,1,0:T(1,128)S(1)} all-to-all(f32[16,1,192]{2,1,0:T(1,128)S(1)} %stage_4.1), channel_id=1, replica_groups=mesh['groups'=2,'dp'=8,'split'=2] {'dp','split'}, dimensions={0} | all-to-all | bytes 24576 | tf_op jit(solution)/shard_map/all_to_all | solution.py:330
  89.5 0.9 %lookup.1 = f32[1,2048]{1,0:T(1,128)} custom-call(s32[1]{0:T(128)} %bitcast.me_ref, f32[16,1,192]{2,1,0:T(1,128)S(1)} %all_to_all.5.table_ref, s32[2,2048]{1,0:T(2,128)S(1)} %copy-done.2, bf16[192,2048]{1,0:T(8,128)(2,1)S(1)} %get-tuple-element.58.picks_ref), custom_call_target="tpu_custom_call" | custom-call | tf_op jit(solution)/shard_map/lookup/pallas_call | solution.py:273
  (23 shorter events, 2.0 us)
Async XLA Ops:
  0.0 7.9 %copy-start = (bf16[2048,512]{1,0:T(8,128)(2,1)S(1)}, bf16[2048,512]{1,0:T(8,128)(2,1)}, u32[]{:S(2)}) copy-start(bf16[2048,512]{1,0:T(8,128)(2,1)} %emb_hbm.3) | copy-start | bytes 6291460
  3.8 21.3 %collective-permute-start = (bf16[776,128]{1,0:T(8,128)(2,1)}, bf16[776,128]{1,0:T(8,128)(2,1)S(1)}, u32[]{:S(2)}, u32[]{:S(2)}) collective-permute-start(bf16[776,128]{1,0:T(8,128)(2,1)} %get-tuple-element.32), channel_id=1, source_target_pairs={{0,8},{1,9},{2,10},{3,11},{4,12},{5,13},{6,14},{7,15},{8,0},{9,1},... | collective-permute-start | bytes 595976 | tf_op jit(solution)/shard_map/ppermute | solution.py:292
  7.9 17.2 %collective-permute-start.1 = (bf16[776,128]{1,0:T(8,128)(2,1)}, bf16[776,128]{1,0:T(8,128)(2,1)S(1)}, u32[]{:S(2)}, u32[]{:S(2)}) collective-permute-start(bf16[776,128]{1,0:T(8,128)(2,1)} %get-tuple-element.33), channel_id=1, source_target_pairs={{0,9},{1,8},{2,11},{3,10},{4,13},{5,12},{6,15},{7,14},{8,1},{9,0},... | collective-permute-start | bytes 595976 | tf_op jit(solution)/shard_map/ppermute | solution.py:292
  7.9 0.7 copy-start.1
  8.6 0.8 copy-start.3
  18.8 18.9 %collective-permute-start.2 = (bf16[776,128]{1,0:T(8,128)(2,1)S(1)}, bf16[776,128]{1,0:T(8,128)(2,1)S(1)}, u32[]{:S(2)}, u32[]{:S(2)}) collective-permute-start(bf16[776,128]{1,0:T(8,128)(2,1)S(1)} %get-tuple-element.36), channel_id=1, source_target_pairs={{0,6},{1,7},{2,4},{3,5},{4,2},{5,3},{6,0},{7,1},{8,14},{9,15},{10,... | collective-permute-start | bytes 595976 | tf_op jit(solution)/shard_map/ppermute | solution.py:292
  21.4 20.5 %collective-permute-start.3 = (bf16[776,128]{1,0:T(8,128)(2,1)S(1)}, bf16[776,128]{1,0:T(8,128)(2,1)S(1)}, u32[]{:S(2)}, u32[]{:S(2)}) collective-permute-start(bf16[776,128]{1,0:T(8,128)(2,1)S(1)} %get-tuple-element.37), channel_id=1, source_target_pairs={{0,7},{1,6},{2,5},{3,4},{4,3},{5,2},{6,1},{7,0},{8,15},{9,14},{10,... | collective-permute-start | bytes 595976 | tf_op jit(solution)/shard_map/ppermute | solution.py:292
  21.6 20.3 %collective-permute-start.4 = (bf16[776,128]{1,0:T(8,128)(2,1)S(1)}, bf16[776,128]{1,0:T(8,128)(2,1)S(1)}, u32[]{:S(2)}, u32[]{:S(2)}) collective-permute-start(bf16[776,128]{1,0:T(8,128)(2,1)S(1)} %get-tuple-element.40), channel_id=1, source_target_pairs={{0,10},{1,11},{2,8},{3,9},{4,14},{5,15},{6,12},{7,13},{8,2},{9,3},... | collective-permute-start | bytes 595976 | tf_op jit(solution)/shard_map/ppermute | solution.py:292
  25.1 26.9 %collective-permute-start.5 = (bf16[776,128]{1,0:T(8,128)(2,1)S(1)}, bf16[776,128]{1,0:T(8,128)(2,1)S(1)}, u32[]{:S(2)}, u32[]{:S(2)}) collective-permute-start(bf16[776,128]{1,0:T(8,128)(2,1)S(1)} %get-tuple-element.41), channel_id=1, source_target_pairs={{0,11},{1,10},{2,9},{3,8},{4,15},{5,14},{6,13},{7,12},{8,3},{9,2},... | collective-permute-start | bytes 595976 | tf_op jit(solution)/shard_map/ppermute | solution.py:292
  25.1 27.6 %collective-permute-start.6 = (bf16[776,128]{1,0:T(8,128)(2,1)S(1)}, bf16[776,128]{1,0:T(8,128)(2,1)S(1)}, u32[]{:S(2)}, u32[]{:S(2)}) collective-permute-start(bf16[776,128]{1,0:T(8,128)(2,1)S(1)} %get-tuple-element.42), channel_id=1, source_target_pairs={{0,14},{1,15},{2,12},{3,13},{4,10},{5,11},{6,8},{7,9},{8,6},{9,7},... | collective-permute-start | bytes 595976 | tf_op jit(solution)/shard_map/ppermute | solution.py:292
  37.7 16.1 %collective-permute-start.7 = (bf16[776,128]{1,0:T(8,128)(2,1)S(1)}, bf16[776,128]{1,0:T(8,128)(2,1)S(1)}, u32[]{:S(2)}, u32[]{:S(2)}) collective-permute-start(bf16[776,128]{1,0:T(8,128)(2,1)S(1)} %get-tuple-element.43), channel_id=1, source_target_pairs={{0,15},{1,14},{2,13},{3,12},{4,11},{5,10},{6,9},{7,8},{8,7},{9,6},... | collective-permute-start | bytes 595976 | tf_op jit(solution)/shard_map/ppermute | solution.py:292
  41.9 14.4 %collective-permute-start.8 = (bf16[776,128]{1,0:T(8,128)(2,1)S(1)}, bf16[776,128]{1,0:T(8,128)(2,1)S(1)}, u32[]{:S(2)}, u32[]{:S(2)}) collective-permute-start(bf16[776,128]{1,0:T(8,128)(2,1)S(1)} %get-tuple-element.46), channel_id=1, source_target_pairs={{0,4},{1,5},{2,6},{3,7},{4,0},{5,1},{6,2},{7,3},{8,12},{9,13},{10,... | collective-permute-start | bytes 595976 | tf_op jit(solution)/shard_map/ppermute | solution.py:292
  41.9 18.5 %collective-permute-start.9 = (bf16[776,128]{1,0:T(8,128)(2,1)S(1)}, bf16[776,128]{1,0:T(8,128)(2,1)S(1)}, u32[]{:S(2)}, u32[]{:S(2)}) collective-permute-start(bf16[776,128]{1,0:T(8,128)(2,1)S(1)} %get-tuple-element.47), channel_id=1, source_target_pairs={{0,5},{1,4},{2,7},{3,6},{4,1},{5,0},{6,3},{7,2},{8,13},{9,12},{10,... | collective-permute-start | bytes 595976 | tf_op jit(solution)/shard_map/ppermute | solution.py:292
  52.0 13.7 %collective-permute-start.10 = (bf16[776,128]{1,0:T(8,128)(2,1)S(1)}, bf16[776,128]{1,0:T(8,128)(2,1)S(1)}, u32[]{:S(2)}, u32[]{:S(2)}) collective-permute-start(bf16[776,128]{1,0:T(8,128)(2,1)S(1)} %get-tuple-element.49), channel_id=1, source_target_pairs={{0,1},{1,0},{2,3},{3,2},{4,5},{5,4},{6,7},{7,6},{8,9},{9,8},{10,11... | collective-permute-start | bytes 595976 | tf_op jit(solution)/shard_map/ppermute | solution.py:292
  52.8 13.0 %collective-permute-start.11 = (bf16[776,128]{1,0:T(8,128)(2,1)S(1)}, bf16[776,128]{1,0:T(8,128)(2,1)S(1)}, u32[]{:S(2)}, u32[]{:S(2)}) collective-permute-start(bf16[776,128]{1,0:T(8,128)(2,1)S(1)} %get-tuple-element.50), channel_id=1, source_target_pairs={{0,2},{1,3},{2,0},{3,1},{4,6},{5,7},{6,4},{7,5},{8,10},{9,11},{10,... | collective-permute-start | bytes 595976 | tf_op jit(solution)/shard_map/ppermute | solution.py:292
  53.8 12.0 %collective-permute-start.12 = (bf16[776,128]{1,0:T(8,128)(2,1)S(1)}, bf16[776,128]{1,0:T(8,128)(2,1)S(1)}, u32[]{:S(2)}, u32[]{:S(2)}) collective-permute-start(bf16[776,128]{1,0:T(8,128)(2,1)S(1)} %get-tuple-element.51), channel_id=1, source_target_pairs={{0,3},{1,2},{2,1},{3,0},{4,7},{5,6},{6,5},{7,4},{8,11},{9,10},{10,... | collective-permute-start | bytes 595976 | tf_op jit(solution)/shard_map/ppermute | solution.py:292
  56.2 13.5 %collective-permute-start.13 = (bf16[776,128]{1,0:T(8,128)(2,1)S(1)}, bf16[776,128]{1,0:T(8,128)(2,1)S(1)}, u32[]{:S(2)}, u32[]{:S(2)}) collective-permute-start(bf16[776,128]{1,0:T(8,128)(2,1)S(1)} %get-tuple-element.54), channel_id=1, source_target_pairs={{0,12},{1,13},{2,14},{3,15},{4,8},{5,9},{6,10},{7,11},{8,4},{9,5},... | collective-permute-start | bytes 595976 | tf_op jit(solution)/shard_map/ppermute | solution.py:292
  60.4 10.6 %collective-permute-start.14 = (bf16[776,128]{1,0:T(8,128)(2,1)S(1)}, bf16[776,128]{1,0:T(8,128)(2,1)S(1)}, u32[]{:S(2)}, u32[]{:S(2)}) collective-permute-start(bf16[776,128]{1,0:T(8,128)(2,1)S(1)} %get-tuple-element.57), channel_id=1, source_target_pairs={{0,13},{1,12},{2,15},{3,14},{4,9},{5,8},{6,11},{7,10},{8,5},{9,4},... | collective-permute-start | bytes 595976 | tf_op jit(solution)/shard_map/ppermute | solution.py:292
  71.0 18.6 %copy-start.2 = (s32[2,2048]{1,0:T(2,128)S(1)}, s32[2,2048]{1,0:T(2,128)}, u32[]{:S(2)}) copy-start(s32[2,2048]{1,0:T(2,128)} %get-tuple-element.34.slot_ref) | copy-start | bytes 49156

commit v7 on v6

--- a/solution.py
+++ b/solution.py
@@ -12,7 +12,7 @@
 DEVICE = ("dp", "split")
 LANES = 128
 GROUPS = 8
-ORDER = (8, 9, 6, 7, 10, 11, 14, 15, 4, 5, 0, 1, 2, 3, 12, 13)
+ORDER = (8, 9, 6, 7, 10, 11, 14, 15, 0, 1, 4, 5, 2, 3, 12, 13)
 STAGES = (2, 2, 3)
 LIMBS = 4
 KEY_ROWS = 2 * LIMBS

time: 90.7 us -> 94.3 us (1.040)
  blocking collectives: 17.2 us -> 22.4 us
  starting transfers between devices: 27.1 us -> 23.9 us
  waiting for transfers between devices: 21.4 us -> 23 us
    all_to_all x1, blocking collectives: 17.2 us -> 22.4 us  [per_device(): lax.all_to_all(best, DEVICE, split_axis=0, concat_axis=0, tiled=True)]
    ppermute x15, starting transfers between devices: 27.1 us -> 23.9 us  [send(): lax.ppermute(block, DEVICE, [(i, i ^ offset) for i in range(clusters)])]
    ppermute x15, waiting for transfers between devices: 21.4 us -> 23 us  [send(): lax.ppermute(block, DEVICE, [(i, i ^ offset) for i in range(clusters)])]
  transfers between devices with their start and end apart: 15 -> 15, of which waited for: 5 -> 4; matrix products, arithmetic and copies ran while one was open for 0% -> 0% of each run, Pallas kernels for 19% -> 18%
where the time goes in v7:
time: 94.3 us; the launch traced here: 94 us
  starting transfers between devices  23.9 us (25%)
  Pallas kernels  23.1 us (24%)
  waiting for transfers between devices  23 us (24%)
  blocking collectives  22.4 us (24%)
  local copies, waits for them, and re-layouts  1.48 us (2%)
    ppermute x15, starting transfers between devices, send(): lax.ppermute(block, DEVICE, [(i, i ^ offset) for i in range(clusters)])  23.9 us
    ppermute x15, waiting for transfers between devices, send(): lax.ppermute(block, DEVICE, [(i, i ^ offset) for i in range(clusters)])  23 us
    all_to_all x1, blocking collectives, per_device(): lax.all_to_all(best, DEVICE, split_axis=0, concat_axis=0, tiled=True)  22.4 us
    pallas_call x1, Pallas kernels, pack(): pl.pallas_call(functools.partial(pack_kernel, firsts=firsts, unit=unit, m...  9.43 us
    pallas_call x5, Pallas kernels, stage(): pl.pallas_call(functools.partial(stage_kernel, olds=olds, fresh=fresh, co...  8.97 us
    pallas_call x1, Pallas kernels, first_pack(): pl.pallas_call(functools.partial(first_pack_kernel, clusters=clusters, mo...  3.79 us
  transfers between devices with their start and end apart: 15, of which 4 were waited for; matrix products, arithmetic and copies ran while one was open for 0% of the time, Pallas kernels for 18%

profile of v7, /device:TPU:0, one launch (start us, length us, event | category | flops | bytes accessed | tf_op | source)
XLA Modules:
  0.0 94.0 jit_solution(6479737915460827385)
XLA Ops:
  0.0 3.8 %first_pack.1 = (bf16[776,128]{1,0:T(8,128)(2,1)}, bf16[776,128]{1,0:T(8,128)(2,1)}, s32[2,2048]{1,0:T(2,128)}, bf16[8,2048]{1,0:T(8,128)(2,1)}) custom-call(s32[1]{0:T(128)} %bitcast.me_ref, s32[1,2048]{1,0:T(1,128)} %bitcast.4, s32[1,2048]{1,0:T(1,128)} %bitcast.5, bf16[2048,512]{1,0:T(8,128)(2,1)} %emb_hbm.3), custom_call_target="tpu_custom_call" | custom-call | tf_op jit(solution)/shard_map/first_pack/pallas_call | solution.py:115
  3.8 4.1 %collective-permute-start = (bf16[776,128]{1,0:T(8,128)(2,1)}, bf16[776,128]{1,0:T(8,128)(2,1)S(1)}, u32[]{:S(2)}, u32[]{:S(2)}) collective-permute-start(bf16[776,128]{1,0:T(8,128)(2,1)} %get-tuple-element.32), channel_id=1, source_target_pairs={{0,8},{1,9},{2,10},{3,11},{4,12},{5,13},{6,14},{7,15},{8,0},{9,1},... | collective-permute-start | bytes 595976 | tf_op jit(solution)/shard_map/ppermute | solution.py:292
  7.9 0.7 copy-done.1
  8.6 0.8 copy-done.3
  9.4 9.4 %pack.1 = (bf16[776,128]{1,0:T(8,128)(2,1)S(1)}, bf16[776,128]{1,0:T(8,128)(2,1)S(1)}, bf16[776,128]{1,0:T(8,128)(2,1)S(1)}, bf16[776,128]{1,0:T(8,128)(2,1)S(1)...) custom-call(s32[2,2048]{1,0:T(2,128)S(1)} %copy-done.1, ...), custom_call_target="tpu_custom_call" | custom-call | tf_op jit(solution)/shard_map/pack/pallas_call | solution.py:148
  18.8 2.6 %collective-permute-start.2 = (bf16[776,128]{1,0:T(8,128)(2,1)S(1)}, bf16[776,128]{1,0:T(8,128)(2,1)S(1)}, u32[]{:S(2)}, u32[]{:S(2)}) collective-permute-start(bf16[776,128]{1,0:T(8,128)(2,1)S(1)} %get-tuple-element.36), channel_id=1, source_target_pairs={{0,6},{1,7},{2,4},{3,5},{4,2},{5,3},{6,0},{7,1},{8,14},{9,15},{10,... | collective-permute-start | bytes 595976 | tf_op jit(solution)/shard_map/ppermute | solution.py:292
  21.6 3.6 %collective-permute-start.4 = (bf16[776,128]{1,0:T(8,128)(2,1)S(1)}, bf16[776,128]{1,0:T(8,128)(2,1)S(1)}, u32[]{:S(2)}, u32[]{:S(2)}) collective-permute-start(bf16[776,128]{1,0:T(8,128)(2,1)S(1)} %get-tuple-element.40), channel_id=1, source_target_pairs={{0,10},{1,11},{2,8},{3,9},{4,14},{5,15},{6,12},{7,13},{8,2},{9,3},... | collective-permute-start | bytes 595976 | tf_op jit(solution)/shard_map/ppermute | solution.py:292
  25.1 5.2 %collective-permute-start.6 = (bf16[776,128]{1,0:T(8,128)(2,1)S(1)}, bf16[776,128]{1,0:T(8,128)(2,1)S(1)}, u32[]{:S(2)}, u32[]{:S(2)}) collective-permute-start(bf16[776,128]{1,0:T(8,128)(2,1)S(1)} %get-tuple-element.42), channel_id=1, source_target_pairs={{0,14},{1,15},{2,12},{3,13},{4,10},{5,11},{6,8},{7,9},{8,6},{9,7},... | collective-permute-start | bytes 595976 | tf_op jit(solution)/shard_map/ppermute | solution.py:292
  30.3 7.4 %collective-permute-done.2.refs_2_ = bf16[776,128]{1,0:T(8,128)(2,1)S(1)} collective-permute-done((bf16[776,128]{1,0:T(8,128)(2,1)S(1)}, bf16[776,128]{1,0:T(8,128)(2,1)S(1)}, u32[]{:S(2)}, u32[]{:S(2)}) %collective-permute-start.2) | collective-permute-done | bytes 198688 | tf_op jit(solution)/shard_map/ppermute | solution.py:292
  37.7 1.9 %collective-permute-start.7 = (bf16[776,128]{1,0:T(8,128)(2,1)S(1)}, bf16[776,128]{1,0:T(8,128)(2,1)S(1)}, u32[]{:S(2)}, u32[]{:S(2)}) collective-permute-start(bf16[776,128]{1,0:T(8,128)(2,1)S(1)} %get-tuple-element.43), channel_id=1, source_target_pairs={{0,15},{1,14},{2,13},{3,12},{4,11},{5,10},{6,9},{7,8},{8,7},{9,6},... | collective-permute-start | bytes 595976 | tf_op jit(solution)/shard_map/ppermute | solution.py:292
  39.7 2.2 %collective-permute-done.3.refs_3_ = bf16[776,128]{1,0:T(8,128)(2,1)S(1)} collective-permute-done((bf16[776,128]{1,0:T(8,128)(2,1)S(1)}, bf16[776,128]{1,0:T(8,128)(2,1)S(1)}, u32[]{:S(2)}, u32[]{:S(2)}) %collective-permute-start.3) | collective-permute-done | bytes 198688 | tf_op jit(solution)/shard_map/ppermute | solution.py:292
  42.1 10.0 %collective-permute-done.5.refs_3_ = bf16[776,128]{1,0:T(8,128)(2,1)S(1)} collective-permute-done((bf16[776,128]{1,0:T(8,128)(2,1)S(1)}, bf16[776,128]{1,0:T(8,128)(2,1)S(1)}, u32[]{:S(2)}, u32[]{:S(2)}) %collective-permute-start.5) | collective-permute-done | bytes 198688 | tf_op jit(solution)/shard_map/ppermute | solution.py:292
  52.0 1.2 %collective-permute-start.11 = (bf16[776,128]{1,0:T(8,128)(2,1)S(1)}, bf16[776,128]{1,0:T(8,128)(2,1)S(1)}, u32[]{:S(2)}, u32[]{:S(2)}) collective-permute-start(bf16[776,128]{1,0:T(8,128)(2,1)S(1)} %get-tuple-element.50), channel_id=1, source_target_pairs={{0,2},{1,3},{2,0},{3,1},{4,6},{5,7},{6,4},{7,5},{8,10},{9,11},{10,... | collective-permute-start | bytes 595976 | tf_op jit(solution)/shard_map/ppermute | solution.py:292
  53.2 1.7 %collective-permute-start.12 = (bf16[776,128]{1,0:T(8,128)(2,1)S(1)}, bf16[776,128]{1,0:T(8,128)(2,1)S(1)}, u32[]{:S(2)}, u32[]{:S(2)}) collective-permute-start(bf16[776,128]{1,0:T(8,128)(2,1)S(1)} %get-tuple-element.51), channel_id=1, source_target_pairs={{0,3},{1,2},{2,1},{3,0},{4,7},{5,6},{6,5},{7,4},{8,11},{9,10},{10,... | collective-permute-start | bytes 595976 | tf_op jit(solution)/shard_map/ppermute | solution.py:292
  54.9 2.5 %collective-permute-start.13 = (bf16[776,128]{1,0:T(8,128)(2,1)S(1)}, bf16[776,128]{1,0:T(8,128)(2,1)S(1)}, u32[]{:S(2)}, u32[]{:S(2)}) collective-permute-start(bf16[776,128]{1,0:T(8,128)(2,1)S(1)} %get-tuple-element.54), channel_id=1, source_target_pairs={{0,12},{1,13},{2,14},{3,15},{4,8},{5,9},{6,10},{7,11},{8,4},{9,5},... | collective-permute-start | bytes 595976 | tf_op jit(solution)/shard_map/ppermute | solution.py:292
  57.4 0.8 collective-permute-start.14
  58.2 0.9 %stage_0.1 = (f32[2,768]{1,0:T(2,128)S(1)}, bf16[768,512]{1,0:T(8,128)(2,1)S(1)}) custom-call(s32[1]{0:T(128)} %bitcast.me_ref, bf16[776,128]{1,0:T(8,128)(2,1)S(1)} %collective-permute-done.refs_0_, bf16[776,128]{1,0:T(8,128)(2,1)S(1)} %collective-permute-done.1.refs_1_, bf16[776,128]{1,0:T(8,128)(2,1)S(1)} %collective-permute-done.2.refs_2_, ...), custom_call_target="tpu_custom_call" | custom-call | tf_op jit(solution)/shard_map/stage_0/pallas_call | solution.py:242
  59.2 1.6 %stage_1.1 = (f32[2,1536]{1,0:T(2,128)S(1)}, bf16[768,512]{1,0:T(8,128)(2,1)S(1)}) custom-call(s32[1]{0:T(128)} %bitcast.me_ref, f32[2,768]{1,0:T(2,128)S(1)} %get-tuple-element.38.refs_0_, bf16[768,512]{1,0:T(8,128)(2,1)S(1)} %get-tuple-element.39.refs_1_, bf16[776,128]{1,0:T(8,128)(2,1)S(1)} %collective-permute-done.4.refs_2_, ...), custom_call_target="tpu_custom_call" | custom-call | tf_op jit(solution)/shard_map/stage_1/pallas_call | solution.py:242
  60.7 3.4 %collective-permute-done.12.refs_8_ = bf16[776,128]{1,0:T(8,128)(2,1)S(1)} collective-permute-done((bf16[776,128]{1,0:T(8,128)(2,1)S(1)}, bf16[776,128]{1,0:T(8,128)(2,1)S(1)}, u32[]{:S(2)}, u32[]{:S(2)}) %collective-permute-start.12) | collective-permute-done | bytes 198688 | tf_op jit(solution)/shard_map/ppermute | solution.py:292
  64.1 4.0 %stage_2.1 = (f32[2,2688]{1,0:T(2,128)S(1)}, bf16[1152,512]{1,0:T(8,128)(2,1)S(1)}) custom-call(s32[1]{0:T(128)} %bitcast.me_ref, f32[2,1536]{1,0:T(2,128)S(1)} %get-tuple-element.44.refs_0_, bf16[768,512]{1,0:T(8,128)(2,1)S(1)} %get-tuple-element.39.refs_1_, bf16[768,512]{1,0:T(8,128)(2,1)S(1)} %get-tuple-element.45.refs_2_, ...), custom_call_target="tpu_custom_call" | custom-call | tf_op jit(solution)/shard_map/stage_2/pallas_call | solution.py:242
  68.1 1.2 %stage_3.1 = (f32[2,2944]{1,0:T(2,128)S(1)}, bf16[256,512]{1,0:T(8,128)(2,1)S(1)}) custom-call(s32[1]{0:T(128)} %bitcast.me_ref, f32[2,2688]{1,0:T(2,128)S(1)} %get-tuple-element.52.refs_0_, bf16[768,512]{1,0:T(8,128)(2,1)S(1)} %get-tuple-element.39.refs_1_, bf16[768,512]{1,0:T(8,128)(2,1)S(1)} %get-tuple-element.45.refs_2_, ...), custom_call_target="tpu_custom_call" | custom-call | tf_op jit(solution)/shard_map/stage_3/pallas_call | solution.py:242
  69.3 1.3 %stage_4.1 = f32[16,1,192]{2,1,0:T(1,128)S(1)} custom-call(s32[1]{0:T(128)} %bitcast.me_ref, f32[2,2944]{1,0:T(2,128)S(1)} %get-tuple-element.55.refs_0_, bf16[768,512]{1,0:T(8,128)(2,1)S(1)} %get-tuple-element.39.refs_1_, bf16[768,512]{1,0:T(8,128)(2,1)S(1)} %get-tuple-element.45.refs_2_, bf16[1152,512]{1,0:T(8,128)(2,1)S(1)} %get-tuple-element.53.refs_3_, ...), custom_call_target="tpu_custom_call" | custom-call | tf_op jit(solution)/shard_map/stage_4/pallas_call | solution.py:242
  70.6 22.4 %all_to_all.5.table_ref = f32[16,1,192]{2,1,0:T(1,128)S(1)} all-to-all(f32[16,1,192]{2,1,0:T(1,128)S(1)} %stage_4.1), channel_id=1, replica_groups=mesh['groups'=2,'dp'=8,'split'=2] {'dp','split'}, dimensions={0} | all-to-all | bytes 24576 | tf_op jit(solution)/shard_map/all_to_all | solution.py:330
  93.1 0.9 lookup.1
  (23 shorter events, 0.4 us)
Async XLA Ops:
  0.0 7.9 %copy-start = (bf16[2048,512]{1,0:T(8,128)(2,1)S(1)}, bf16[2048,512]{1,0:T(8,128)(2,1)}, u32[]{:S(2)}) copy-start(bf16[2048,512]{1,0:T(8,128)(2,1)} %emb_hbm.3) | copy-start | bytes 6291460
  3.8 21.3 %collective-permute-start = (bf16[776,128]{1,0:T(8,128)(2,1)}, bf16[776,128]{1,0:T(8,128)(2,1)S(1)}, u32[]{:S(2)}, u32[]{:S(2)}) collective-permute-start(bf16[776,128]{1,0:T(8,128)(2,1)} %get-tuple-element.32), channel_id=1, source_target_pairs={{0,8},{1,9},{2,10},{3,11},{4,12},{5,13},{6,14},{7,15},{8,0},{9,1},... | collective-permute-start | bytes 595976 | tf_op jit(solution)/shard_map/ppermute | solution.py:292
  7.9 17.2 %collective-permute-start.1 = (bf16[776,128]{1,0:T(8,128)(2,1)}, bf16[776,128]{1,0:T(8,128)(2,1)S(1)}, u32[]{:S(2)}, u32[]{:S(2)}) collective-permute-start(bf16[776,128]{1,0:T(8,128)(2,1)} %get-tuple-element.33), channel_id=1, source_target_pairs={{0,9},{1,8},{2,11},{3,10},{4,13},{5,12},{6,15},{7,14},{8,1},{9,0},... | collective-permute-start | bytes 595976 | tf_op jit(solution)/shard_map/ppermute | solution.py:292
  7.9 0.7 copy-start.1
  8.6 0.8 copy-start.3
  18.8 18.9 %collective-permute-start.2 = (bf16[776,128]{1,0:T(8,128)(2,1)S(1)}, bf16[776,128]{1,0:T(8,128)(2,1)S(1)}, u32[]{:S(2)}, u32[]{:S(2)}) collective-permute-start(bf16[776,128]{1,0:T(8,128)(2,1)S(1)} %get-tuple-element.36), channel_id=1, source_target_pairs={{0,6},{1,7},{2,4},{3,5},{4,2},{5,3},{6,0},{7,1},{8,14},{9,15},{10,... | collective-permute-start | bytes 595976 | tf_op jit(solution)/shard_map/ppermute | solution.py:292
  21.4 20.5 %collective-permute-start.3 = (bf16[776,128]{1,0:T(8,128)(2,1)S(1)}, bf16[776,128]{1,0:T(8,128)(2,1)S(1)}, u32[]{:S(2)}, u32[]{:S(2)}) collective-permute-start(bf16[776,128]{1,0:T(8,128)(2,1)S(1)} %get-tuple-element.37), channel_id=1, source_target_pairs={{0,7},{1,6},{2,5},{3,4},{4,3},{5,2},{6,1},{7,0},{8,15},{9,14},{10,... | collective-permute-start | bytes 595976 | tf_op jit(solution)/shard_map/ppermute | solution.py:292
  21.6 20.5 %collective-permute-start.4 = (bf16[776,128]{1,0:T(8,128)(2,1)S(1)}, bf16[776,128]{1,0:T(8,128)(2,1)S(1)}, u32[]{:S(2)}, u32[]{:S(2)}) collective-permute-start(bf16[776,128]{1,0:T(8,128)(2,1)S(1)} %get-tuple-element.40), channel_id=1, source_target_pairs={{0,10},{1,11},{2,8},{3,9},{4,14},{5,15},{6,12},{7,13},{8,2},{9,3},... | collective-permute-start | bytes 595976 | tf_op jit(solution)/shard_map/ppermute | solution.py:292
  25.1 26.9 %collective-permute-start.5 = (bf16[776,128]{1,0:T(8,128)(2,1)S(1)}, bf16[776,128]{1,0:T(8,128)(2,1)S(1)}, u32[]{:S(2)}, u32[]{:S(2)}) collective-permute-start(bf16[776,128]{1,0:T(8,128)(2,1)S(1)} %get-tuple-element.41), channel_id=1, source_target_pairs={{0,11},{1,10},{2,9},{3,8},{4,15},{5,14},{6,13},{7,12},{8,3},{9,2},... | collective-permute-start | bytes 595976 | tf_op jit(solution)/shard_map/ppermute | solution.py:292
  25.1 26.9 %collective-permute-start.6 = (bf16[776,128]{1,0:T(8,128)(2,1)S(1)}, bf16[776,128]{1,0:T(8,128)(2,1)S(1)}, u32[]{:S(2)}, u32[]{:S(2)}) collective-permute-start(bf16[776,128]{1,0:T(8,128)(2,1)S(1)} %get-tuple-element.42), channel_id=1, source_target_pairs={{0,14},{1,15},{2,12},{3,13},{4,10},{5,11},{6,8},{7,9},{8,6},{9,7},... | collective-permute-start | bytes 595976 | tf_op jit(solution)/shard_map/ppermute | solution.py:292
  37.7 15.5 %collective-permute-start.7 = (bf16[776,128]{1,0:T(8,128)(2,1)S(1)}, bf16[776,128]{1,0:T(8,128)(2,1)S(1)}, u32[]{:S(2)}, u32[]{:S(2)}) collective-permute-start(bf16[776,128]{1,0:T(8,128)(2,1)S(1)} %get-tuple-element.43), channel_id=1, source_target_pairs={{0,15},{1,14},{2,13},{3,12},{4,11},{5,10},{6,9},{7,8},{8,7},{9,6},... | collective-permute-start | bytes 595976 | tf_op jit(solution)/shard_map/ppermute | solution.py:292
  41.9 13.0 %collective-permute-start.8 = (bf16[776,128]{1,0:T(8,128)(2,1)S(1)}, bf16[776,128]{1,0:T(8,128)(2,1)S(1)}, u32[]{:S(2)}, u32[]{:S(2)}) collective-permute-start(bf16[776,128]{1,0:T(8,128)(2,1)S(1)} %get-tuple-element.47), channel_id=1, source_target_pairs={{0,1},{1,0},{2,3},{3,2},{4,5},{5,4},{6,7},{7,6},{8,9},{9,8},{10,11... | collective-permute-start | bytes 595976 | tf_op jit(solution)/shard_map/ppermute | solution.py:292
  42.1 15.3 %collective-permute-start.9 = (bf16[776,128]{1,0:T(8,128)(2,1)S(1)}, bf16[776,128]{1,0:T(8,128)(2,1)S(1)}, u32[]{:S(2)}, u32[]{:S(2)}) collective-permute-start(bf16[776,128]{1,0:T(8,128)(2,1)S(1)} %get-tuple-element.48), channel_id=1, source_target_pairs={{0,4},{1,5},{2,6},{3,7},{4,0},{5,1},{6,2},{7,3},{8,12},{9,13},{10,... | collective-permute-start | bytes 595976 | tf_op jit(solution)/shard_map/ppermute | solution.py:292
  52.0 8.7 %collective-permute-start.10 = (bf16[776,128]{1,0:T(8,128)(2,1)S(1)}, bf16[776,128]{1,0:T(8,128)(2,1)S(1)}, u32[]{:S(2)}, u32[]{:S(2)}) collective-permute-start(bf16[776,128]{1,0:T(8,128)(2,1)S(1)} %get-tuple-element.49), channel_id=1, source_target_pairs={{0,5},{1,4},{2,7},{3,6},{4,1},{5,0},{6,3},{7,2},{8,13},{9,12},{10,... | collective-permute-start | bytes 595976 | tf_op jit(solution)/shard_map/ppermute | solution.py:292
  52.0 8.7 %collective-permute-start.11 = (bf16[776,128]{1,0:T(8,128)(2,1)S(1)}, bf16[776,128]{1,0:T(8,128)(2,1)S(1)}, u32[]{:S(2)}, u32[]{:S(2)}) collective-permute-start(bf16[776,128]{1,0:T(8,128)(2,1)S(1)} %get-tuple-element.50), channel_id=1, source_target_pairs={{0,2},{1,3},{2,0},{3,1},{4,6},{5,7},{6,4},{7,5},{8,10},{9,11},{10,... | collective-permute-start | bytes 595976 | tf_op jit(solution)/shard_map/ppermute | solution.py:292
  53.2 10.9 %collective-permute-start.12 = (bf16[776,128]{1,0:T(8,128)(2,1)S(1)}, bf16[776,128]{1,0:T(8,128)(2,1)S(1)}, u32[]{:S(2)}, u32[]{:S(2)}) collective-permute-start(bf16[776,128]{1,0:T(8,128)(2,1)S(1)} %get-tuple-element.51), channel_id=1, source_target_pairs={{0,3},{1,2},{2,1},{3,0},{4,7},{5,6},{6,5},{7,4},{8,11},{9,10},{10,... | collective-permute-start | bytes 595976 | tf_op jit(solution)/shard_map/ppermute | solution.py:292
  54.9 13.2 %collective-permute-start.13 = (bf16[776,128]{1,0:T(8,128)(2,1)S(1)}, bf16[776,128]{1,0:T(8,128)(2,1)S(1)}, u32[]{:S(2)}, u32[]{:S(2)}) collective-permute-start(bf16[776,128]{1,0:T(8,128)(2,1)S(1)} %get-tuple-element.54), channel_id=1, source_target_pairs={{0,12},{1,13},{2,14},{3,15},{4,8},{5,9},{6,10},{7,11},{8,4},{9,5},... | collective-permute-start | bytes 595976 | tf_op jit(solution)/shard_map/ppermute | solution.py:292
  57.4 11.9 %collective-permute-start.14 = (bf16[776,128]{1,0:T(8,128)(2,1)S(1)}, bf16[776,128]{1,0:T(8,128)(2,1)S(1)}, u32[]{:S(2)}, u32[]{:S(2)}) collective-permute-start(bf16[776,128]{1,0:T(8,128)(2,1)S(1)} %get-tuple-element.57), channel_id=1, source_target_pairs={{0,13},{1,12},{2,15},{3,14},{4,9},{5,8},{6,11},{7,10},{8,5},{9,4},... | collective-permute-start | bytes 595976 | tf_op jit(solution)/shard_map/ppermute | solution.py:292
  69.3 23.8 %copy-start.2 = (s32[2,2048]{1,0:T(2,128)S(1)}, s32[2,2048]{1,0:T(2,128)}, u32[]{:S(2)}) copy-start(s32[2,2048]{1,0:T(2,128)} %get-tuple-element.34.slot_ref) | copy-start | bytes 49156
